TPU v7x, 32 devices: a whole 2x2x4 slice. The times are simulated.
32 devices in a mesh: sec: 8 (over z, x), op: 4 (over y, core).
Axes of the slice: x: 2, y: 2, z: 4, core: 2. Of those that a mesh axis runs over, the one named last changes fastest.
Arguments:
- state: float32 [8, 256, 256], P('sec'), may hold values from -6 to 6
- left_ops: float32 [32, 8, 256, 256], P('op', 'sec'), may hold values from -0.0625 to 0.0625
- right_ops: float32 [32, 8, 256, 256], P('op', 'sec'), may hold values from -0.375 to 0.375
- term_shift: int32 [32], P('op'), may hold values from -1 to 1
- sector_rows: int32 [8], P('sec'), may hold values from 128 to 256, as said below
- sector_cols: int32 [8], P('sec'), may hold values from 128 to 256, as said below
Outputs:
- correction: float32 [8, 256, 256], P('sec')
- image: float32 [8, 256, 256], P('sec')
Inputs may be any that keep to these rules, and one draw needn't show every extreme that they name: `sector_rows`: at least one sector has 256 live rows. `sector_cols`: at least one sector has 256 live columns.
All inputs are finite; a program needn't handle non-finite values.
Results may differ from a plain program's by a relative error of at most 0.0003.
Values sent between devices are 32-bit elements; how exact they have to be, the bound alone decides.
No kernel may reach another device: no remote copies, remote signals or barrier semaphores. Data moves between devices by JAX's collectives and lax.ppermute only.
A program may use at most 64 MiB of HBM per device.

v0:
```python
import jax
import jax.numpy as jnp
from jax import lax
from jax.sharding import PartitionSpec as P


def padded_2(block, sides, width):
    for axis, dim in sides:
        count = lax.axis_size(axis)
        forward = [(i, i + 1) for i in range(count - 1)]
        backward = [(target, source) for source, target in forward]
        low = lax.ppermute(
            lax.slice_in_dim(block, block.shape[dim] - width, None, axis=dim), axis, forward
        )
        high = lax.ppermute(lax.slice_in_dim(block, 0, width, axis=dim), axis, backward)
        block = jnp.concatenate([low, block, high], axis=dim)
    return block


def live_mask(sector_rows, sector_cols, block):
    place = jnp.arange(block, dtype=jnp.int32)
    rows_ok = place[None, :, None] < sector_rows[:, None, None]
    cols_ok = place[None, None, :] < sector_cols[:, None, None]
    return (rows_ok & cols_ok).astype(jnp.float32)


def apply_terms(field, left_ops, right_ops, term_shift):
    count = field.shape[0]
    padded = padded_2(field, (("sec", 0),), 1)
    total = jnp.zeros(field.shape, jnp.float32)
    for term in range(left_ops.shape[0]):
        start = 1 - term_shift[term]
        source = lax.dynamic_slice_in_dim(padded, start, count, 0)
        inner = jnp.einsum("tij,tjl->til", left_ops[term], source, precision=lax.Precision.HIGHEST)
        total = total + jnp.einsum(
            "til,tml->tim", inner, right_ops[term], precision=lax.Precision.HIGHEST
        )
    return total


def local(state, left_ops, right_ops, term_shift, sector_rows, sector_cols):
    block = state.shape[1]
    mask = live_mask(sector_rows, sector_cols, block)
    field = state * mask
    cells = state.shape[0] * lax.axis_size("sec") * block * block

    def whole_product(vector):
        partial_sum = apply_terms(vector, left_ops, right_ops, term_shift)
        return lax.psum(partial_sum, "op") * mask

    first = whole_product(field)
    cross, square = lax.psum((jnp.sum(field * first), jnp.sum(field * field)), "sec")
    theta = cross / square
    resid = first - theta * field
    energy = lax.psum(jnp.sum(resid * resid), "sec")
    correction = resid * lax.rsqrt(energy / cells + 1e-06)
    image = whole_product(correction)
    return (correction, image)


def solution(mesh):
    in_specs = (
        P("sec", None, None),
        P("op", "sec", None, None),
        P("op", "sec", None, None),
        P("op"),
        P("sec"),
        P("sec"),
    )
    out_specs = (P("sec", None, None), P("sec", None, None))
    return jax.shard_map(local, mesh=mesh, in_specs=in_specs, out_specs=out_specs, check_vma=False)
```

profile of v0, /device:TPU:0, one launch (start us, length us, event | category | flops | bytes accessed | tf_op | source)
XLA Modules:
  0.0 183.5 jit_solution(6636771230505370450)
XLA Ops:
  7.2 0.0 all-reduce.4.cloned.1.call-start
  8.5 1.1 and_select_fusion.2
  9.6 4.9 %collective-permute-start = (f32[1,256,256]{2,1,0:T(8,128)S(1)}, f32[1,256,256]{2,1,0:T(8,128)S(1)}, u32[]{:S(2)}, u32[]{:S(2)}) collective-permute-start(f32[1,256,256]{2,1,0:T(8,128)S(1)} %and_select_fusion.2), channel_id=1, source_target_pairs={{0,4},{4,8},{8,12},{12,16},{16,20},{20,24},{24,28},{1,5},{5,9},{9,... | collective-permute-start | bytes 786440 | tf_op jit(solution)/shard_map/ppermute | solution.py:12
  14.4 1.3 collective-permute-start.1
  15.7 1.6 fusion.132
  27.6 0.0 copy-start.1
  27.6 0.0 collective-permute-done
  27.7 0.0 collective-permute-done.1
  27.7 0.1 pad_maximum_fusion
  27.7 1.7 fusion.65
  29.4 1.6 fusion.57
  31.0 1.6 fusion.51
  32.6 0.0 copy-start
  32.6 1.7 fusion.45
  34.3 0.0 copy-done.1
  34.3 0.6 fusion.39
  34.9 0.6 fusion.33
  35.5 0.6 fusion.27
  36.1 0.6 fusion.21
  36.8 0.0 copy-done
  36.8 0.6 fusion.62
  37.4 0.6 convolution_add_fusion.13
  38.0 0.6 convolution_add_fusion.12
  38.6 0.6 convolution_add_fusion.11
  39.2 0.0 copy-start.3
  39.2 0.6 convolution_add_fusion.10
  39.8 0.6 convolution_add_fusion.9
  40.4 0.6 convolution_add_fusion.8
  41.0 1.3 fusion.1
  42.3 0.0 all-reduce.4.cloned.1.call-update
  42.4 0.0 all-reduce.6.cloned.1.call-start
  42.4 34.5 %all-reduce.4.cloned.1.call-done = f32[1,256,256]{2,1,0:T(8,128)} async-done(((f32[1,256,256]{2,1,0:T(8,128)}), f32[1,256,256]{2,1,0:T(8,128)}) %all-reduce.4.cloned.1.call-update) | async-done | bytes 262160 | tf_op jit(solution)/shard_map/psum | solution.py:49
  76.9 0.0 copy-done.3
  76.9 1.7 multiply_reduce_fusion.1
  78.6 22.0 %all-reduce = (f32[]{:T(128)}, f32[]{:T(128)}) all-reduce(f32[]{:T(128)} %get-tuple-element.3, f32[]{:T(128)} %get-tuple-element.2), channel_id=1, replica_groups=mesh['sec'=8,'op'=4] {'sec'}, use_global_device_ids=true, to_apply=%region_2.0 | all-reduce | flops 2 | bytes 16 | tf_op jit(solution)/shard_map/psum | solution.py:52
  101.9 1.7 multiply_reduce_fusion
  103.6 17.7 %psum.38 = f32[]{:T(128)} all-reduce(f32[]{:T(128)} %multiply_reduce_fusion), channel_id=1, replica_groups=mesh['sec'=8,'op'=4] {'sec'}, use_global_device_ids=true, to_apply=%region_6.0 | all-reduce | flops 1 | bytes 8 | tf_op jit(solution)/shard_map/psum | solution.py:55
  122.0 0.0 copy-start.2
  122.1 1.2 broadcast_multiply_fusion
  123.3 0.0 copy-start.4
  123.3 4.0 %collective-permute-start.2 = (f32[1,256,256]{2,1,0:T(8,128)S(1)}, f32[1,256,256]{2,1,0:T(8,128)S(1)}, u32[]{:S(2)}, u32[]{:S(2)}) collective-permute-start(f32[1,256,256]{2,1,0:T(8,128)S(1)} %broadcast_multiply_fusion), channel_id=1, source_target_pairs={{0,4},{4,8},{8,12},{12,16},{16,20},{20,24},{24,28},{1,5},{5,9},{9,... | collective-permute-start | bytes 786440 | tf_op jit(solution)/shard_map/ppermute | solution.py:12
  127.3 1.5 collective-permute-start.3
  128.8 2.4 %collective-permute-done.2 = f32[1,256,256]{2,1,0:T(8,128)S(1)} collective-permute-done((f32[1,256,256]{2,1,0:T(8,128)S(1)}, f32[1,256,256]{2,1,0:T(8,128)S(1)}, u32[]{:S(2)}, u32[]{:S(2)}) %collective-permute-start.2) | collective-permute-done | bytes 262176 | tf_op jit(solution)/shard_map/ppermute | solution.py:12
  131.2 4.4 %collective-permute-done.3 = f32[1,256,256]{2,1,0:T(8,128)S(1)} collective-permute-done((f32[1,256,256]{2,1,0:T(8,128)S(1)}, f32[1,256,256]{2,1,0:T(8,128)S(1)}, u32[]{:S(2)}, u32[]{:S(2)}) %collective-permute-start.3) | collective-permute-done | bytes 262176 | tf_op jit(solution)/shard_map/ppermute | solution.py:15
  135.6 0.1 pad_maximum_fusion.1
  135.7 0.6 fusion.16
  136.3 0.6 fusion.14
  136.9 0.6 fusion.12
  137.5 0.6 fusion.10
  138.1 0.6 fusion.8
  138.7 0.6 fusion.6
  139.3 0.6 fusion.4
  140.0 0.6 fusion.2
  140.6 0.6 fusion.60
  141.2 0.6 convolution_add_fusion.6
  141.8 0.6 convolution_add_fusion.5
  142.4 0.6 convolution_add_fusion.4
  143.0 0.6 convolution_add_fusion.3
  143.6 0.6 convolution_add_fusion.2
  144.2 0.6 convolution_add_fusion.1
  144.8 1.3 fusion
  146.1 0.0 all-reduce.6.cloned.1.call-update
  146.2 28.8 %all-reduce.6.cloned.1.call-done = f32[1,256,256]{2,1,0:T(8,128)} async-done(((f32[1,256,256]{2,1,0:T(8,128)}), f32[1,256,256]{2,1,0:T(8,128)}) %all-reduce.6.cloned.1.call-update) | async-done | bytes 262160 | tf_op jit(solution)/shard_map/psum | solution.py:49
  174.9 1.8 and_select_fusion
  (3 shorter events, 0.0 us)
Async XLA Ops:
  7.2 69.7 %all-reduce.4.cloned.1.call-start = ((), (), s32[]{:S(2)}) async-start(), calls=%async_computation | async-start | bytes 524288 | tf_op jit(solution)/shard_map/psum | solution.py:49
  9.6 18.1 %collective-permute-start = (f32[1,256,256]{2,1,0:T(8,128)S(1)}, f32[1,256,256]{2,1,0:T(8,128)S(1)}, u32[]{:S(2)}, u32[]{:S(2)}) collective-permute-start(f32[1,256,256]{2,1,0:T(8,128)S(1)} %and_select_fusion.2), channel_id=1, source_target_pairs={{0,4},{4,8},{8,12},{12,16},{16,20},{20,24},{24,28},{1,5},{5,9},{9,... | collective-permute-start | bytes 786440 | tf_op jit(solution)/shard_map/ppermute | solution.py:12
  14.4 13.2 %collective-permute-start.1 = (f32[1,256,256]{2,1,0:T(8,128)S(1)}, f32[1,256,256]{2,1,0:T(8,128)S(1)}, u32[]{:S(2)}, u32[]{:S(2)}) collective-permute-start(f32[1,256,256]{2,1,0:T(8,128)S(1)} %and_select_fusion.2), channel_id=1, source_target_pairs={{4,0},{8,4},{12,8},{16,12},{20,16},{24,20},{28,24},{5,1},{9,5},{13... | collective-permute-start | bytes 786440 | tf_op jit(solution)/shard_map/ppermute | solution.py:15
  27.6 6.7 %copy-start.1 = (f32[8,1,256,256]{3,2,1,0:T(8,128)S(1)}, f32[8,1,256,256]{3,2,1,0:T(8,128)}, u32[]{:S(2)}) copy-start(f32[8,1,256,256]{3,2,1,0:T(8,128)} %param.7) | copy-start | bytes 6291460
  32.6 4.2 %copy-start = (f32[8,1,256,256]{3,2,1,0:T(8,128)S(1)}, f32[8,1,256,256]{3,2,1,0:T(8,128)}, u32[]{:S(2)}) copy-start(f32[8,1,256,256]{3,2,1,0:T(8,128)} %param.8) | copy-start | bytes 6291460
  39.2 37.7 %copy-start.3 = (f32[1,256,256]{2,1,0:T(8,128)S(1)}, f32[1,256,256]{2,1,0:T(8,128)}, u32[]{:S(2)}) copy-start(f32[1,256,256]{2,1,0:T(8,128)} %param.6) | copy-start | bytes 786436
  42.4 132.6 %all-reduce.6.cloned.1.call-start = ((), (), s32[]{:S(2)}) async-start(), calls=%async_computation.1 | async-start | bytes 524288 | tf_op jit(solution)/shard_map/psum | solution.py:49
  122.0 13.6 %copy-start.2 = (f32[8,1,256,256]{3,2,1,0:T(8,128)S(1)}, f32[8,1,256,256]{3,2,1,0:T(8,128)}, u32[]{:S(2)}) copy-start(f32[8,1,256,256]{3,2,1,0:T(8,128)} %param.7) | copy-start | bytes 6291460
  123.3 14.8 %copy-start.4 = (f32[1,256,256]{2,1,0:T(8,128)}, f32[1,256,256]{2,1,0:T(8,128)S(1)}, u32[]{:S(2)}) copy-start(f32[1,256,256]{2,1,0:T(8,128)S(1)} %broadcast_multiply_fusion) | copy-start | bytes 786436
  123.3 7.9 %collective-permute-start.2 = (f32[1,256,256]{2,1,0:T(8,128)S(1)}, f32[1,256,256]{2,1,0:T(8,128)S(1)}, u32[]{:S(2)}, u32[]{:S(2)}) collective-permute-start(f32[1,256,256]{2,1,0:T(8,128)S(1)} %broadcast_multiply_fusion), channel_id=1, source_target_pairs={{0,4},{4,8},{8,12},{12,16},{16,20},{20,24},{24,28},{1,5},{5,9},{9,... | collective-permute-start | bytes 786440 | tf_op jit(solution)/shard_map/ppermute | solution.py:12
  127.3 8.3 %collective-permute-start.3 = (f32[1,256,256]{2,1,0:T(8,128)S(1)}, f32[1,256,256]{2,1,0:T(8,128)S(1)}, u32[]{:S(2)}, u32[]{:S(2)}) collective-permute-start(f32[1,256,256]{2,1,0:T(8,128)S(1)} %broadcast_multiply_fusion), channel_id=1, source_target_pairs={{4,0},{8,4},{12,8},{16,12},{20,16},{24,20},{28,24},{5,1},{9,5},{13... | collective-permute-start | bytes 786440 | tf_op jit(solution)/shard_map/ppermute | solution.py:15
Sparse Core Ops, SparseCore 0:
  42.5 34.3 all-reduce.3
  146.3 28.6 all-reduce.5
where the time goes:
time: 184 us
  waiting for transfers between devices  70.1 us (38%)
  blocking collectives  39.7 us (22%)
  between operations  28 us (15%)
  matrix products  24.8 us (13%)
  starting transfers between devices  11.7 us (6%)
  other arithmetic  7.55 us (4%)
    psum x2, waiting for transfers between devices, whole_product(): return lax.psum(partial_sum, 'op') * mask  63.3 us
    psum x1, blocking collectives, local(): lax.psum((jnp.sum(field * first), jnp.sum(field * field)), 'sec')  22 us
    psum x1, blocking collectives, local(): energy = lax.psum(jnp.sum(resid * resid), 'sec')  17.7 us
    dot_general x16, matrix products, apply_terms(): jnp.einsum('tij,tjl->til', left_ops[term], source, precision=lax.Precisio...  13.8 us
    dot_general x16, matrix products, apply_terms(): jnp.einsum('til,tml->tim', inner, right_ops[term], precision=lax.Precisio...  11 us
    ppermute x2, starting transfers between devices, padded_2(): lax.ppermute(lax.slice_in_dim(block, block.shape[dim] - width, None, axis...  8.87 us
    ppermute x2, waiting for transfers between devices, padded_2(): lax.ppermute(lax.slice_in_dim(block, 0, width, axis=dim), axis, backward)  4.41 us
  transfers between devices with their start and end apart: 6, of which 4 were waited for; matrix products, arithmetic and copies ran while one was open for 1% of the time, Pallas kernels for 0%

commit v1 on v0

v1 whole, which is shorter than its diff:
```python
import jax
import jax.numpy as jnp
from jax import lax
from jax.experimental import pallas as pl
from jax.experimental.pallas import tpu as pltpu
from jax.sharding import PartitionSpec as P

EXTRA = 8


def split(x):
    high = x.astype(jnp.bfloat16)
    low = (x - high.astype(jnp.float32)).astype(jnp.bfloat16)
    return high, low


def dot(a, b, contract):
    return lax.dot_general(
        a, b, (((1,), (contract,)), ((), ())), preferred_element_type=jnp.float32
    )


def product_kernel(place_ref, shift_ref, own_ref, near_ref, far_ref, left_ref, right_ref, *refs):
    core, slot = place_ref[0], place_ref[1]
    extra_ref = refs[0] if len(refs) == 6 else None
    send_ref, keep_ref, high, low, total = refs[-5:]
    for index, ref in ((1, own_ref), (slot, near_ref), (2 - slot, far_ref)):
        high[index], low[index] = split(ref[...])
    out = None
    for term in range(left_ref.shape[0]):
        source = 1 - shift_ref[term]
        left_high, left_low = split(left_ref[term, 0])
        right_high, right_low = split(right_ref[term, 0])
        v_high, v_low = high[source], low[source]
        inner = dot(left_high, v_high, 0) + (dot(left_low, v_high, 0) + dot(left_high, v_low, 0))
        inner_high, inner_low = split(inner)
        part = dot(inner_high, right_high, 1) + (
            dot(inner_low, right_high, 1) + dot(inner_high, right_low, 1)
        )
        out = part if out is None else out + part
    total[...] = out
    half = out.shape[0] // 2
    send_ref[pl.ds(0, half)] = total[pl.ds(pl.multiple_of((1 - core) * half, half), half)]
    keep_ref[pl.ds(0, half)] = total[pl.ds(pl.multiple_of(core * half, half), half)]
    if extra_ref is not None:
        send_ref[pl.ds(half, EXTRA)] = extra_ref[...]
        keep_ref[pl.ds(half, EXTRA)] = extra_ref[...]


def product(place, shift, own, near, far, left_ops, right_ops, extra=None):
    block = own.shape[0]
    rows = block // 2 + (0 if extra is None else EXTRA)
    vmem, smem = pl.BlockSpec(memory_space=pltpu.VMEM), pl.BlockSpec(memory_space=pltpu.SMEM)
    arrays = [own, near, far, left_ops, right_ops] + ([] if extra is None else [extra])
    return pl.pallas_call(
        product_kernel,
        out_shape=[jax.ShapeDtypeStruct((rows, own.shape[1]), jnp.float32)] * 2,
        in_specs=[smem, smem] + [vmem] * len(arrays),
        out_specs=[vmem, vmem],
        scratch_shapes=[
            pltpu.VMEM((3,) + own.shape, jnp.bfloat16),
            pltpu.VMEM((3,) + own.shape, jnp.bfloat16),
            pltpu.VMEM(own.shape, jnp.float32),
        ],
        compiler_params=pltpu.CompilerParams(vmem_limit_bytes=24 * 1024 * 1024),
        cost_estimate=pl.CostEstimate(
            flops=12 * left_ops.shape[0] * block**3, bytes_accessed=8 * left_ops.size, transcendentals=0
        ),
    )(place, shift, *arrays)


def live_mask(sector_rows, sector_cols, block):
    place = jnp.arange(block, dtype=jnp.int32)
    rows_ok = place[:, None] < sector_rows[0]
    cols_ok = place[None, :] < sector_cols[0]
    return (rows_ok & cols_ok).astype(jnp.float32)


def local(state, left_ops, right_ops, term_shift, sector_rows, sector_cols):
    sectors, ops = lax.axis_size("sec"), lax.axis_size("op")
    block = state.shape[1]
    half = block // 2
    cells = sectors * block * block
    sector, op = lax.axis_index("sec"), lax.axis_index("op")
    core = op % 2

    others = [(i, i ^ 1) for i in range(ops)]
    even = [(i, i + 1) for i in range(0, sectors - 1, 2)]
    odd = [(i, i + 1) for i in range(1, sectors - 1, 2)]
    neighbours = []
    for a in range(ops):
        for one, two in (even, odd)[a % 2]:
            neighbours += [(one * ops + a, two * ops + a), (two * ops + a, one * ops + a)]
    slot = jnp.where(sector % 2 == core, 2, 0)
    place = jnp.stack([core, slot]).astype(jnp.int32)

    mask = live_mask(sector_rows, sector_cols, block)
    field = state[0] * mask

    def exchange(v):
        near = lax.ppermute(v, ("sec", "op"), neighbours)
        return near, lax.ppermute(near, "op", others)

    def halves_summed(send, keep):
        total = keep + lax.ppermute(send, "op", others)
        step = 2
        while step < ops:
            total = total + lax.ppermute(total, "op", [(i, i ^ step) for i in range(ops)])
            step *= 2
        return total

    def joined(mine):
        other = lax.ppermute(mine, "op", others)
        return jnp.where(
            core == 0, jnp.concatenate([mine, other]), jnp.concatenate([other, mine])
        )

    def half_of(v):
        return jnp.where(core == 0, v[:half], v[half:])

    near, far = exchange(field)
    send, keep = product(place, term_shift, field, near, far, left_ops, right_ops)
    first = joined(halves_summed(send, keep) * half_of(mask))
    near, far = exchange(first)

    cross, square = jnp.sum(field * first), jnp.sum(field * field)
    own_theta = jnp.where(square > 0, cross / jnp.where(square > 0, square, 1.0), 0.0)
    own_resid = first - own_theta * field
    energy = jnp.sum(own_resid * own_resid)
    row = lax.broadcasted_iota(jnp.int32, (EXTRA, block), 0)
    lane = lax.broadcasted_iota(jnp.int32, (EXTRA, block), 1)
    values = jnp.where(row == 0, cross, jnp.where(row == 1, square, jnp.where(row == 2, energy, 0.0)))
    mine = jnp.where(lane == sector, values, 0.0)
    sums = jnp.where(op == 0, mine, 0.0)
    for base in range(1, sectors, ops):
        pairs = [
            (s * ops + a, (s + base + a) % sectors * ops + a)
            for s in range(sectors)
            for a in range(ops)
            if base + a < sectors
        ]
        sums = sums + lax.ppermute(mine, ("sec", "op"), pairs)

    send, keep = product(place, term_shift, first, near, far, left_ops, right_ops, sums)
    total = halves_summed(send, keep)
    crosses, squares, energies = (total[half + i, :] for i in range(3))
    theta = jnp.sum(crosses) / jnp.sum(squares)
    thetas = jnp.where(squares > 0, crosses / jnp.where(squares > 0, squares, 1.0), 0.0)
    energy = jnp.sum(energies + (thetas - theta) ** 2 * squares)
    scale = lax.rsqrt(energy / cells + 1e-06)
    image = joined(scale * (total[:half] - theta * half_of(first)) * half_of(mask))
    correction = scale * (first - theta * field)
    return correction[None], image[None]


def solution(mesh):
    in_specs = (
        P("sec", None, None),
        P("op", "sec", None, None),
        P("op", "sec", None, None),
        P("op"),
        P("sec"),
        P("sec"),
    )
    out_specs = (P("sec", None, None), P("sec", None, None))
    return jax.shard_map(local, mesh=mesh, in_specs=in_specs, out_specs=out_specs, check_vma=False)
```

time: 184 us -> 75.3 us (0.41)
  waiting for transfers between devices: 70.1 us -> 23.9 us
  blocking collectives: 39.7 us -> 0 us
  matrix products: 24.8 us -> 0 us
  between operations: 28 us -> 6.03 us
  starting transfers between devices: 11.7 us -> 20.6 us
  Pallas kernels: 0 us -> 5.66 us
  other arithmetic: 7.55 us -> 13.2 us
  local copies, waits for them, and re-layouts: 1.67 us -> 5.45 us
    psum x2 -> x0, waiting for transfers between devices: 63.3 us -> none  [whole_product(): return lax.psum(partial_sum, 'op') * mask]
    psum x2 -> x0, blocking collectives: 39.7 us -> none  [the longest x1 22 us: local(): lax.psum((jnp.sum(field * first), jnp.sum(field * field)), 'sec')]
    dot_general x32 -> x0, matrix products: 24.8 us -> none  [the longest x16 13.8 us: apply_terms(): jnp.einsum('tij,tjl->til', left_ops[term], source, precision=lax.Precisio...]
    ppermute x4 -> x12, waiting for transfers between devices: 6.79 us -> 23.9 us  [the longest x2 9.21 us: exchange(): near = lax.ppermute(v, ('sec', 'op'), neighbours)]
    ppermute x4 -> x12, starting transfers between devices: 11.6 us -> 20.6 us  [the longest x2 9.22 us: exchange(): near = lax.ppermute(v, ('sec', 'op'), neighbours)]
    pallas_call x0 -> x2, Pallas kernels: none -> 5.66 us  [product(): pl.pallas_call(product_kernel, out_shape=[jax.ShapeDtypeStruct((rows, own...]
    unnamed x10 -> x18, local copies, waits for them, and re-layouts: 0.03 us -> 5.45 us
    select_n x0 -> x3, other arithmetic: none -> 3.97 us  [the longest x1 2.6 us: local(): mine = jnp.where(lane == sector, values, 0.0)]
  transfers between devices with their start and end apart: 6 -> 12, of which waited for: 4 -> 9; matrix products, arithmetic and copies ran while one was open for 1% -> 12% of each run, Pallas kernels for 0% -> 0%
where the time goes in v1:
time: 75.3 us; the launch traced here: 74.8 us
  waiting for transfers between devices  23.9 us (32%)
  starting transfers between devices  20.6 us (27%)
  other arithmetic  13.2 us (18%)
  between operations  6.03 us (8%)
  Pallas kernels  5.66 us (8%)
  local copies, waits for them, and re-layouts  5.45 us (7%)
    ppermute x2, starting transfers between devices, exchange(): near = lax.ppermute(v, ('sec', 'op'), neighbours)  9.22 us
    ppermute x2, waiting for transfers between devices, exchange(): near = lax.ppermute(v, ('sec', 'op'), neighbours)  9.21 us
    ppermute x2, waiting for transfers between devices, halves_summed(): lax.ppermute(total, 'op', [(i, i ^ step) for i in range(ops)])  8.3 us
    ppermute x2, starting transfers between devices, local(): sums = sums + lax.ppermute(mine, ('sec', 'op'), pairs)  7.96 us
    pallas_call x2, Pallas kernels, product(): pl.pallas_call(product_kernel, out_shape=[jax.ShapeDtypeStruct((rows, own...  5.66 us
    unnamed x18, local copies, waits for them, and re-layouts  5.45 us
    ppermute x2, starting transfers between devices, halves_summed(): lax.ppermute(total, 'op', [(i, i ^ step) for i in range(ops)])  2.99 us
    select_n x1, other arithmetic, local(): mine = jnp.where(lane == sector, values, 0.0)  2.6 us
  transfers between devices with their start and end apart: 12, of which 9 were waited for; matrix products, arithmetic and copies ran while one was open for 12% of the time, Pallas kernels for 0%

profile of v1, /device:TPU:0, one launch (start us, length us, event | category | flops | bytes accessed | tf_op | source)
XLA Modules:
  0.0 74.8 jit_solution(4289832067582571984)
XLA Ops:
  1.9 1.1 %and_select_fusion.own_ref = f32[256,256]{1,0:T(8,128)S(1)} fusion(f32[1,256,256]{2,1,0:T(8,128)} %param.6, pred[256]{0:T(512)(128)(4,1)S(1)} %get-tuple-element.18, pred[256]{0:T(512)(128)(4,1)S(1)} %get-tuple-element.19), kind=kLoop, calls=%fused_computation.1 | loop fusion | flops 131072 | bytes 524800 | tf_op jit(solution)/shard_map/mul | solution.py:98
  3.0 4.8 %collective-permute-start = (f32[256,256]{1,0:T(8,128)S(1)}, f32[256,256]{1,0:T(8,128)S(1)}, u32[]{:S(2)}, u32[]{:S(2)}) collective-permute-start(f32[256,256]{1,0:T(8,128)S(1)} %and_select_fusion.own_ref), channel_id=1, source_target_pairs={{0,4},{4,0},{8,12},{12,8},{16,20},{20,16},{24,28},{28,24},{5,9},{9... | collective-permute-start | bytes 786440 | tf_op jit(solution)/shard_map/ppermute | solution.py:101
  7.8 6.4 %collective-permute-done.near_ref = f32[256,256]{1,0:T(8,128)S(1)} collective-permute-done((f32[256,256]{1,0:T(8,128)S(1)}, f32[256,256]{1,0:T(8,128)S(1)}, u32[]{:S(2)}, u32[]{:S(2)}) %collective-permute-start) | collective-permute-done | bytes 262176 | tf_op jit(solution)/shard_map/ppermute | solution.py:101
  14.3 0.0 collective-permute-start.1
  14.3 0.1 pad_add_fusion.place_ref
  14.4 1.5 %collective-permute-done.1.far_ref = f32[256,256]{1,0:T(8,128)S(1)} collective-permute-done((f32[256,256]{1,0:T(8,128)S(1)}, f32[256,256]{1,0:T(8,128)S(1)}, u32[]{:S(2)}, u32[]{:S(2)}) %collective-permute-start.1) | collective-permute-done | bytes 262176 | tf_op jit(solution)/shard_map/ppermute | solution.py:102
  15.8 0.0 copy-start
  15.8 1.6 %copy-done = f32[8,1,256,256]{3,2,1,0:T(8,128)S(1)} copy-done((f32[8,1,256,256]{3,2,1,0:T(8,128)S(1)}, f32[8,1,256,256]{3,2,1,0:T(8,128)}, u32[]{:S(2)}) %copy-start) | copy-done | bytes 2097176
  17.4 0.0 copy-start.2
  17.4 1.6 %copy-done.2 = f32[8,1,256,256]{3,2,1,0:T(8,128)S(1)} copy-done((f32[8,1,256,256]{3,2,1,0:T(8,128)S(1)}, f32[8,1,256,256]{3,2,1,0:T(8,128)}, u32[]{:S(2)}) %copy-start.2) | copy-done | bytes 2097176
  19.0 0.0 copy-start.4
  19.0 0.7 copy-done.4
  19.7 0.0 copy-start.6
  19.7 2.8 %shard_map.77 = (f32[128,256]{1,0:T(8,128)S(1)}, f32[128,256]{1,0:T(8,128)S(1)}) custom-call(s32[2]{0:T(128)S(1)} %pad_add_fusion.place_ref, s32[8]{0:T(128)S(1)} %copy-done.4, f32[256,256]{1,0:T(8,128)S(1)} %and_select_fusion.own_ref, f32[256,256]{1,0:T(8,128)S(1)} %collective-permute-done.near_ref, f32[256,256]{1,0:T(8,128)S(1)} %collective-permute-done.1.far_ref, ...), custom_call_target="tpu_custom_call" | custom-call | flops 1610612736 | bytes 4194304 | tf_op jit(solution)/shard_map/pallas_call | solution.py:55
  22.5 0.0 copy-start.1
  22.5 0.0 copy-start.5
  22.5 0.2 collective-permute-start.2
  22.7 1.2 %collective-permute-done.2 = f32[128,256]{1,0:T(8,128)S(1)} collective-permute-done((f32[128,256]{1,0:T(8,128)S(1)}, f32[128,256]{1,0:T(8,128)S(1)}, u32[]{:S(2)}, u32[]{:S(2)}) %collective-permute-start.2) | collective-permute-done | bytes 131104 | tf_op jit(solution)/shard_map/ppermute | solution.py:105
  23.9 1.6 %collective-permute-start.3 = (f32[128,256]{1,0:T(8,128)S(1)}, f32[128,256]{1,0:T(8,128)S(1)}, u32[]{:S(2)}, u32[]{:S(2)}) collective-permute-start(f32[128,256]{1,0:T(8,128)S(1)} %add.33), channel_id=1, source_target_pairs={{0,2},{1,3},{2,0},{3,1},{4,6},{5,7},{6,4},{7,5},{8,10},{9,11},{10,... | collective-permute-start | bytes 393224 | tf_op jit(solution)/shard_map/ppermute | solution.py:108
  25.5 0.1 and_convert_fusion
  25.6 3.9 %collective-permute-done.3 = f32[128,256]{1,0:T(8,128)S(1)} collective-permute-done((f32[128,256]{1,0:T(8,128)S(1)}, f32[128,256]{1,0:T(8,128)S(1)}, u32[]{:S(2)}, u32[]{:S(2)}) %collective-permute-start.3) | collective-permute-done | bytes 131104 | tf_op jit(solution)/shard_map/ppermute | solution.py:108
  29.6 0.1 collective-permute-start.4
  29.7 0.6 iota_compare_fusion.3
  30.2 0.8 %collective-permute-done.4 = f32[128,256]{1,0:T(8,128)S(1)} collective-permute-done((f32[128,256]{1,0:T(8,128)S(1)}, f32[128,256]{1,0:T(8,128)S(1)}, u32[]{:S(2)}, u32[]{:S(2)}) %collective-permute-start.4) | collective-permute-done | bytes 131104 | tf_op jit(solution)/shard_map/ppermute | solution.py:113
  31.0 0.0 copy-done.6
  31.0 0.0 copy-start.7
  31.0 0.8 %multiply_reduce_fusion.2 = (f32[]{:T(128)}, f32[]{:T(128)}, f32[256,256]{1,0:T(8,128)S(1)}) fusion(f32[128,256]{1,0:T(8,128)S(1)} %add_multiply_fusion, f32[128,256]{1,0:T(8,128)S(1)} %collective-permute-done.4, pred[]{:T(512)S(6)} %eq.45, f32[1,256,256]{2,1,0:T(8,128)S(1)} %copy-done.6, pred[256]{0:T(512)(128)(4,1)S(1)} %get-tuple-element.18, ...), kind=kLoop, calls=%fused_computation.9 | loop fusion | flops 589822 | bytes 786953 | tf_op jit(solution)/shard_map/reduce_sum | solution.py:126
  31.8 0.0 copy-done.7
  31.8 4.4 %collective-permute-start.5 = (f32[256,256]{1,0:T(8,128)S(1)}, f32[256,256]{1,0:T(8,128)S(1)}, u32[]{:S(2)}, u32[]{:S(2)}) collective-permute-start(f32[256,256]{1,0:T(8,128)S(1)} %get-tuple-element.14.own_ref), channel_id=1, source_target_pairs={{0,4},{4,0},{8,12},{12,8},{16,20},{20,16},{24,28},{28,24},{5,9},{9... | collective-permute-start | bytes 786440 | tf_op jit(solution)/shard_map/ppermute | solution.py:101
  36.2 0.6 iota_compare_fusion
  38.7 0.8 %multiply_reduce_fusion = f32[]{:T(128)} fusion(f32[256,256]{1,0:T(8,128)S(1)} %get-tuple-element.14.own_ref, f32[]{:T(128)S(6)} %select_n.99, f32[1,256,256]{2,1,0:T(8,128)S(1)} %copy-done.6, pred[256]{0:T(512)(128)(4,1)S(1)} %get-tuple-element.18, pred[256]{0:T(512)(128)(4,1)S(1)} %get-tuple-element.19), kind=kLoop, calls=%fused_computation.7 | loop fusion | flops 393215 | bytes 524808 | tf_op jit(solution)/shard_map/reduce_sum | solution.py:129
  39.5 0.6 compare_select_fusion.2
  40.1 0.0 copy-start.8
  40.1 2.8 %collective-permute-done.5.near_ref = f32[256,256]{1,0:T(8,128)S(1)} collective-permute-done((f32[256,256]{1,0:T(8,128)S(1)}, f32[256,256]{1,0:T(8,128)S(1)}, u32[]{:S(2)}, u32[]{:S(2)}) %collective-permute-start.5) | collective-permute-done | bytes 262176 | tf_op jit(solution)/shard_map/ppermute | solution.py:101
  42.9 0.0 collective-permute-start.6
  42.9 0.0 copy-done.8
  42.9 2.6 %select_select_fusion = f32[8,256]{1,0:T(8,128)} fusion(f32[8]{0:T(128)S(1)} %compare_select_fusion.2, f32[]{:T(128)} %get-tuple-element.11, f32[]{:T(128)} %get-tuple-element.10, pred[8]{0:T(512)(128)(4,1)} %get-tuple-element.20, pred[8]{0:T(512)(128)(4,1)} %get-tuple-element.21, pred[256]{0:T(512)(128)(4,1)} %iota_compare_fusion), kind=kLoop, calls=%fused_computation.18 | loop fusion | flops 6144 | bytes 8504 | tf_op jit(solution)/shard_map/jit(_where)/select_n | solution.py:133
  45.5 2.5 %collective-permute-start.7 = (f32[8,256]{1,0:T(8,128)}, f32[8,256]{1,0:T(8,128)}, u32[]{:S(2)}, u32[]{:S(2)}) collective-permute-start(f32[8,256]{1,0:T(8,128)} %select_select_fusion), channel_id=1, source_target_pairs={{0,4},{1,9},{2,14},{3,19},{4,8},{5,13},{6,18},{7,23},{8,12},{9,17}... | collective-permute-start | bytes 24584 | tf_op jit(solution)/shard_map/ppermute | solution.py:142
  48.0 5.5 %collective-permute-start.8 = (f32[8,256]{1,0:T(8,128)}, f32[8,256]{1,0:T(8,128)}, u32[]{:S(2)}, u32[]{:S(2)}) collective-permute-start(f32[8,256]{1,0:T(8,128)} %select_select_fusion), channel_id=1, source_target_pairs={{0,20},{1,25},{2,30},{4,24},{5,29},{6,2},{8,28},{9,1},{10,6},{12,0... | collective-permute-start | bytes 24584 | tf_op jit(solution)/shard_map/ppermute | solution.py:142
  53.5 0.0 collective-permute-done.7
  53.5 1.5 %collective-permute-done.8 = f32[8,256]{1,0:T(8,128)} collective-permute-done((f32[8,256]{1,0:T(8,128)}, f32[8,256]{1,0:T(8,128)}, u32[]{:S(2)}, u32[]{:S(2)}) %collective-permute-start.8) | collective-permute-done | bytes 8224 | tf_op jit(solution)/shard_map/ppermute | solution.py:142
  55.0 2.1 %add_add_fusion.refs_0_ = f32[8,256]{1,0:T(8,128)S(1)} fusion(f32[8,256]{1,0:T(8,128)} %collective-permute-done.8, f32[8,256]{1,0:T(8,128)} %collective-permute-done.7, pred[]{:T(512)S(6)} %eq.46, f32[8]{0:T(128)} %copy-done.8, f32[]{:T(128)} %get-tuple-element.11, pred[8]{0:T(512)(128)(4,1)} %get-tuple-element.20, f32[]{:T(128)} %get-tuple-element.10, ...), kind=kLoop, calls=%fused_computation.17 | loop fusion | flops 12288 | bytes 24889 | tf_op jit(solution)/shard_map/add | solution.py:142
  57.1 0.0 collective-permute-done.6.far_ref
  57.1 0.0 copy-done.1
  57.1 0.0 copy-done.5
  57.1 0.0 copy-start.3
  57.1 1.6 %copy-done.3 = f32[8,1,256,256]{3,2,1,0:T(8,128)S(1)} copy-done((f32[8,1,256,256]{3,2,1,0:T(8,128)S(1)}, f32[8,1,256,256]{3,2,1,0:T(8,128)}, u32[]{:S(2)}) %copy-start.3) | copy-done | bytes 2097176
  58.7 2.8 %shard_map.78 = (f32[136,256]{1,0:T(8,128)S(1)}, f32[136,256]{1,0:T(8,128)S(1)}) custom-call(s32[2]{0:T(128)S(1)} %pad_add_fusion.place_ref, s32[8]{0:T(128)S(1)} %copy-done.5, f32[256,256]{1,0:T(8,128)S(1)} %get-tuple-element.14.own_ref, f32[256,256]{1,0:T(8,128)S(1)} %collective-permute-done.5.near_ref, f32[256,256]{1,0:T(8,128)S(1)} %collective-permute-done.6.far_ref, ...), custom_call_target="tpu_custom_call" | custom-call | flops 1610612736 | bytes 4194304 | tf_op jit(solution)/shard_map/pallas_call | solution.py:55
  61.6 0.1 collective-permute-start.9
  61.6 1.3 %collective-permute-done.9 = f32[136,256]{1,0:T(8,128)S(1)} collective-permute-done((f32[136,256]{1,0:T(8,128)S(1)}, f32[136,256]{1,0:T(8,128)S(1)}, u32[]{:S(2)}, u32[]{:S(2)}) %collective-permute-start.9) | collective-permute-done | bytes 139296 | tf_op jit(solution)/shard_map/ppermute | solution.py:105
  63.0 1.4 %collective-permute-start.10 = (f32[136,256]{1,0:T(8,128)S(1)}, f32[136,256]{1,0:T(8,128)S(1)}, u32[]{:S(2)}, u32[]{:S(2)}) collective-permute-start(f32[136,256]{1,0:T(8,128)S(1)} %add.37), channel_id=1, source_target_pairs={{0,2},{1,3},{2,0},{3,1},{4,6},{5,7},{6,4},{7,5},{8,10},{9,11},{10,... | collective-permute-start | bytes 417800 | tf_op jit(solution)/shard_map/ppermute | solution.py:108
  64.4 4.4 %collective-permute-done.10 = f32[136,256]{1,0:T(8,128)S(1)} collective-permute-done((f32[136,256]{1,0:T(8,128)S(1)}, f32[136,256]{1,0:T(8,128)S(1)}, u32[]{:S(2)}, u32[]{:S(2)}) %collective-permute-start.10) | collective-permute-done | bytes 139296 | tf_op jit(solution)/shard_map/ppermute | solution.py:108
  68.8 0.7 slice_reduce_fusion.1
  70.8 0.6 add_reduce_fusion
  72.2 0.1 collective-permute-start.11
  72.2 1.8 %fusion.1 = f32[1,256,256]{2,1,0:T(8,128)} fusion(f32[1,128,256]{2,1,0:T(8,128)} %bitcast.21, f32[1,128,256]{2,1,0:T(8,128)S(1)} %bitcast.19, f32[1,256,256]{2,1,0:T(8,128)S(1)} %copy-done.6, f32[]{:T(128)S(6)} %div.14, f32[]{:T(128)S(6)} %rsqrt.3, pred[256]{0:T(512)(128)(4,1)S(1)} %get-tuple-element.18, pred[]{:T(512)S(6)} %eq.45, ...), kind=kLoop, calls=%fused_computation.5 | loop fusion | flops 524288 | bytes 786953 | tf_op jit(solution)/shard_map/mul | solution.py:152
  74.1 0.0 collective-permute-done.11
  74.1 0.7 maximum_select_fusion.2
  (6 shorter events, 0.1 us)
Async XLA Ops:
  3.0 11.3 %collective-permute-start = (f32[256,256]{1,0:T(8,128)S(1)}, f32[256,256]{1,0:T(8,128)S(1)}, u32[]{:S(2)}, u32[]{:S(2)}) collective-permute-start(f32[256,256]{1,0:T(8,128)S(1)} %and_select_fusion.own_ref), channel_id=1, source_target_pairs={{0,4},{4,0},{8,12},{12,8},{16,20},{20,16},{24,28},{28,24},{5,9},{9... | collective-permute-start | bytes 786440 | tf_op jit(solution)/shard_map/ppermute | solution.py:101
  14.3 1.5 %collective-permute-start.1 = (f32[256,256]{1,0:T(8,128)S(1)}, f32[256,256]{1,0:T(8,128)S(1)}, u32[]{:S(2)}, u32[]{:S(2)}) collective-permute-start(f32[256,256]{1,0:T(8,128)S(1)} %collective-permute-done.near_ref), channel_id=1, source_target_pairs={{0,1},{1,0},{2,3},{3,2},{4,5},{5,4},{6,7},{7,6},{8,9},{9,8},{10,11... | collective-permute-start | bytes 786440 | tf_op jit(solution)/shard_map/ppermute | solution.py:102
  15.8 1.6 %copy-start = (f32[8,1,256,256]{3,2,1,0:T(8,128)S(1)}, f32[8,1,256,256]{3,2,1,0:T(8,128)}, u32[]{:S(2)}) copy-start(f32[8,1,256,256]{3,2,1,0:T(8,128)} %left_ref.3) | copy-start | bytes 6291460
  17.4 1.6 %copy-start.2 = (f32[8,1,256,256]{3,2,1,0:T(8,128)S(1)}, f32[8,1,256,256]{3,2,1,0:T(8,128)}, u32[]{:S(2)}) copy-start(f32[8,1,256,256]{3,2,1,0:T(8,128)} %right_ref.3) | copy-start | bytes 6291460
  19.0 0.7 copy-start.4
  19.7 11.4 %copy-start.6 = (f32[1,256,256]{2,1,0:T(8,128)S(1)}, f32[1,256,256]{2,1,0:T(8,128)}, u32[]{:S(2)}) copy-start(f32[1,256,256]{2,1,0:T(8,128)} %param.6) | copy-start | bytes 786436
  22.5 34.6 %copy-start.1 = (f32[8,1,256,256]{3,2,1,0:T(8,128)S(1)}, f32[8,1,256,256]{3,2,1,0:T(8,128)}, u32[]{:S(2)}) copy-start(f32[8,1,256,256]{3,2,1,0:T(8,128)} %left_ref.3) | copy-start | bytes 6291460
  22.5 34.6 %copy-start.5 = (s32[8]{0:T(128)S(1)}, s32[8]{0:T(128)}, u32[]{:S(2)}) copy-start(s32[8]{0:T(128)} %shift_ref.3) | copy-start | bytes 100
  22.5 1.4 %collective-permute-start.2 = (f32[128,256]{1,0:T(8,128)S(1)}, f32[128,256]{1,0:T(8,128)S(1)}, u32[]{:S(2)}, u32[]{:S(2)}) collective-permute-start(f32[128,256]{1,0:T(8,128)S(1)} %get-tuple-element.7), channel_id=1, source_target_pairs={{0,1},{1,0},{2,3},{3,2},{4,5},{5,4},{6,7},{7,6},{8,9},{9,8},{10,11... | collective-permute-start | bytes 393224 | tf_op jit(solution)/shard_map/ppermute | solution.py:105
  23.9 5.6 %collective-permute-start.3 = (f32[128,256]{1,0:T(8,128)S(1)}, f32[128,256]{1,0:T(8,128)S(1)}, u32[]{:S(2)}, u32[]{:S(2)}) collective-permute-start(f32[128,256]{1,0:T(8,128)S(1)} %add.33), channel_id=1, source_target_pairs={{0,2},{1,3},{2,0},{3,1},{4,6},{5,7},{6,4},{7,5},{8,10},{9,11},{10,... | collective-permute-start | bytes 393224 | tf_op jit(solution)/shard_map/ppermute | solution.py:108
  29.6 1.4 %collective-permute-start.4 = (f32[128,256]{1,0:T(8,128)S(1)}, f32[128,256]{1,0:T(8,128)S(1)}, u32[]{:S(2)}, u32[]{:S(2)}) collective-permute-start(f32[128,256]{1,0:T(8,128)S(1)} %add_multiply_fusion), channel_id=1, source_target_pairs={{0,1},{1,0},{2,3},{3,2},{4,5},{5,4},{6,7},{7,6},{8,9},{9,8},{10,11... | collective-permute-start | bytes 393224 | tf_op jit(solution)/shard_map/ppermute | solution.py:113
  31.0 0.8 %copy-start.7 = (f32[128,256]{1,0:T(8,128)}, f32[128,256]{1,0:T(8,128)S(1)}, u32[]{:S(2)}) copy-start(f32[128,256]{1,0:T(8,128)S(1)} %collective-permute-done.4) | copy-start | bytes 393220
  31.8 11.1 %collective-permute-start.5 = (f32[256,256]{1,0:T(8,128)S(1)}, f32[256,256]{1,0:T(8,128)S(1)}, u32[]{:S(2)}, u32[]{:S(2)}) collective-permute-start(f32[256,256]{1,0:T(8,128)S(1)} %get-tuple-element.14.own_ref), channel_id=1, source_target_pairs={{0,4},{4,0},{8,12},{12,8},{16,20},{20,16},{24,28},{28,24},{5,9},{9... | collective-permute-start | bytes 786440 | tf_op jit(solution)/shard_map/ppermute | solution.py:101
  40.1 2.8 %copy-start.8 = (f32[8]{0:T(128)}, f32[8]{0:T(128)S(1)}, u32[]{:S(2)}) copy-start(f32[8]{0:T(128)S(1)} %compare_select_fusion.2) | copy-start | bytes 100
  42.9 14.2 %collective-permute-start.6 = (f32[256,256]{1,0:T(8,128)S(1)}, f32[256,256]{1,0:T(8,128)S(1)}, u32[]{:S(2)}, u32[]{:S(2)}) collective-permute-start(f32[256,256]{1,0:T(8,128)S(1)} %collective-permute-done.5.near_ref), channel_id=1, source_target_pairs={{0,1},{1,0},{2,3},{3,2},{4,5},{5,4},{6,7},{7,6},{8,9},{9,8},{10,11... | collective-permute-start | bytes 786440 | tf_op jit(solution)/shard_map/ppermute | solution.py:102
  45.5 8.0 %collective-permute-start.7 = (f32[8,256]{1,0:T(8,128)}, f32[8,256]{1,0:T(8,128)}, u32[]{:S(2)}, u32[]{:S(2)}) collective-permute-start(f32[8,256]{1,0:T(8,128)} %select_select_fusion), channel_id=1, source_target_pairs={{0,4},{1,9},{2,14},{3,19},{4,8},{5,13},{6,18},{7,23},{8,12},{9,17}... | collective-permute-start | bytes 24584 | tf_op jit(solution)/shard_map/ppermute | solution.py:142
  48.0 7.0 %collective-permute-start.8 = (f32[8,256]{1,0:T(8,128)}, f32[8,256]{1,0:T(8,128)}, u32[]{:S(2)}, u32[]{:S(2)}) collective-permute-start(f32[8,256]{1,0:T(8,128)} %select_select_fusion), channel_id=1, source_target_pairs={{0,20},{1,25},{2,30},{4,24},{5,29},{6,2},{8,28},{9,1},{10,6},{12,0... | collective-permute-start | bytes 24584 | tf_op jit(solution)/shard_map/ppermute | solution.py:142
  57.1 1.6 %copy-start.3 = (f32[8,1,256,256]{3,2,1,0:T(8,128)S(1)}, f32[8,1,256,256]{3,2,1,0:T(8,128)}, u32[]{:S(2)}) copy-start(f32[8,1,256,256]{3,2,1,0:T(8,128)} %right_ref.3) | copy-start | bytes 6291460
  61.6 1.4 %collective-permute-start.9 = (f32[136,256]{1,0:T(8,128)S(1)}, f32[136,256]{1,0:T(8,128)S(1)}, u32[]{:S(2)}, u32[]{:S(2)}) collective-permute-start(f32[136,256]{1,0:T(8,128)S(1)} %get-tuple-element.9), channel_id=1, source_target_pairs={{0,1},{1,0},{2,3},{3,2},{4,5},{5,4},{6,7},{7,6},{8,9},{9,8},{10,11... | collective-permute-start | bytes 417800 | tf_op jit(solution)/shard_map/ppermute | solution.py:105
  63.0 5.8 %collective-permute-start.10 = (f32[136,256]{1,0:T(8,128)S(1)}, f32[136,256]{1,0:T(8,128)S(1)}, u32[]{:S(2)}, u32[]{:S(2)}) collective-permute-start(f32[136,256]{1,0:T(8,128)S(1)} %add.37), channel_id=1, source_target_pairs={{0,2},{1,3},{2,0},{3,1},{4,6},{5,7},{6,4},{7,5},{8,10},{9,11},{10,... | collective-permute-start | bytes 417800 | tf_op jit(solution)/shard_map/ppermute | solution.py:108
  72.2 1.9 %collective-permute-start.11 = (f32[128,256]{1,0:T(8,128)S(1)}, f32[128,256]{1,0:T(8,128)S(1)}, u32[]{:S(2)}, u32[]{:S(2)}) collective-permute-start(f32[128,256]{1,0:T(8,128)S(1)} %fusion.5), channel_id=1, source_target_pairs={{0,1},{1,0},{2,3},{3,2},{4,5},{5,4},{6,7},{7,6},{8,9},{9,8},{10,11... | collective-permute-start | bytes 393224 | tf_op jit(solution)/shard_map/ppermute | solution.py:113

commit v2 on v0

v2 whole, which is shorter than its diff:
```python
import jax
import jax.numpy as jnp
from jax import lax
from jax.experimental import pallas as pl
from jax.experimental.pallas import tpu as pltpu
from jax.sharding import PartitionSpec as P

EXTRA = 8
VMEM = pl.BlockSpec(memory_space=pltpu.VMEM)
HBM = pl.BlockSpec(memory_space=pltpu.HBM)


def f32(*shape):
    return jax.ShapeDtypeStruct(shape, jnp.float32)


def in_hbm(x):
    return pltpu.with_memory_space_constraint(x, pltpu.HBM)


def call(kernel, out_shape, in_specs, *arrays, mib=4, **options):
    return pl.pallas_call(
        kernel,
        out_shape=out_shape,
        in_specs=in_specs,
        out_specs=jax.tree.map(lambda _: VMEM, out_shape),
        compiler_params=pltpu.CompilerParams(vmem_limit_bytes=mib * 1024 * 1024),
        **options,
    )(*arrays)


def core_index():
    return lax.rem(lax.axis_index("op"), 2)


def rows_of(core, half):
    return pl.ds(pl.multiple_of(core * half, half), half)


def split(x):
    high = x.astype(jnp.bfloat16)
    low = (x - high.astype(jnp.float32)).astype(jnp.bfloat16)
    return high, low


def dot(a, b, contract):
    return lax.dot_general(
        a, b, (((1,), (contract,)), ((), ())), preferred_element_type=jnp.float32
    )


def total_of(x):
    return jnp.sum(jnp.sum(x, axis=0, keepdims=True), axis=1, keepdims=True)


def field_kernel(state_ref, live_ref, mine_ref, other_ref, mask_ref, state, live, sems):
    copies = [
        pltpu.make_async_copy(ref, buffer, sems.at[i])
        for i, (ref, buffer) in enumerate(
            ((state_ref, state), (live_ref, live))
        )
    ]
    for copy in copies:
        copy.start()
    for copy in copies:
        copy.wait()
    half = mask_ref.shape[0]
    core = core_index()
    rows, cols = live[0], live[1]
    row = lax.broadcasted_iota(jnp.int32, mask_ref.shape, 0)
    lane = lax.broadcasted_iota(jnp.int32, mask_ref.shape, 1)
    for which, ref in ((core, mine_ref), (1 - core, other_ref)):
        inside = (row + which * half < rows) & (lane < cols)
        ref[...] = jnp.where(inside, state[0, rows_of(which, half)], 0.0)
    mask_ref[...] = jnp.where((row + core * half < rows) & (lane < cols), 1.0, 0.0)


def load_kernel(left_ref, right_ref, field_ref, left_out, right_out, sems):
    copies = [
        pltpu.make_async_copy(left_ref, left_out, sems.at[0]),
        pltpu.make_async_copy(right_ref, right_out, sems.at[1]),
    ]
    for copy in copies:
        copy.start()
    for copy in copies:
        copy.wait()


def load(left_ops, right_ops, field):
    return call(
        load_kernel,
        [f32(*left_ops.shape), f32(*right_ops.shape)],
        [HBM, HBM, VMEM],
        in_hbm(left_ops), in_hbm(right_ops), field,
        scratch_shapes=[pltpu.SemaphoreType.DMA((2,))],
        cost_estimate=pl.CostEstimate(flops=0, bytes_accessed=8 * left_ops.size, transcendentals=0),
    )


def product_kernel(shift_ref, *refs):
    halves, (left_ref, right_ref) = refs[:6], refs[6:8]
    tile_ref = refs[8] if len(refs) == 16 else None
    send_ref, keep_ref, high, low, total, shift, sem = refs[-7:]
    shifts = pltpu.make_async_copy(shift_ref, shift, sem)
    shifts.start()
    block = total.shape[0]
    half = block // 2
    core, sector = core_index(), lax.axis_index("sec")
    slot = jnp.where(lax.rem(sector, 2) == 0, 2, 0)
    for index, mine_ref, other_ref in zip((1, slot, 2 - slot), halves[::2], halves[1::2]):
        for which, ref in ((core, mine_ref), (1 - core, other_ref)):
            rows = rows_of(which, half)
            high[index, rows], low[index, rows] = split(ref[...])

    @pl.when(sector == 0)
    def _():
        high[0] = jnp.zeros(high.shape[1:], high.dtype)
        low[0] = jnp.zeros(low.shape[1:], low.dtype)

    @pl.when(sector == lax.axis_size("sec") - 1)
    def _():
        high[2] = jnp.zeros(high.shape[1:], high.dtype)
        low[2] = jnp.zeros(low.shape[1:], low.dtype)

    shifts.wait()
    out = None
    for term in range(left_ref.shape[0]):
        source = 1 - shift[term]
        left_high, left_low = split(left_ref[term, 0])
        right_high, right_low = split(right_ref[term, 0])
        v_high, v_low = high[source], low[source]
        inner = dot(left_high, v_high, 0) + (dot(left_low, v_high, 0) + dot(left_high, v_low, 0))
        inner_high, inner_low = split(inner)
        part = dot(inner_high, right_high, 1) + (
            dot(inner_low, right_high, 1) + dot(inner_high, right_low, 1)
        )
        out = part if out is None else out + part
    total[...] = out
    send_ref[pl.ds(0, half)] = total[rows_of(1 - core, half)]
    keep_ref[pl.ds(0, half)] = total[rows_of(core, half)]
    if tile_ref is not None:
        send_ref[pl.ds(half, EXTRA)] = tile_ref[...]
        keep_ref[pl.ds(half, EXTRA)] = tile_ref[...]


def product(shift, halves, left, right, tile=None):
    terms, _, block, _ = left.shape
    rows = block // 2 + (0 if tile is None else EXTRA)
    arrays = [*halves, left, right] + ([] if tile is None else [tile])
    return call(
        product_kernel,
        [f32(rows, block)] * 2,
        [HBM] + [VMEM] * len(arrays),
        in_hbm(shift), *arrays,
        mib=16,
        scratch_shapes=[
            pltpu.VMEM((3, block, block), jnp.bfloat16),
            pltpu.VMEM((3, block, block), jnp.bfloat16),
            pltpu.VMEM((block, block), jnp.float32),
            pltpu.SMEM(shift.shape, jnp.int32),
            pltpu.SemaphoreType.DMA(()),
        ],
        cost_estimate=pl.CostEstimate(
            flops=12 * terms * block**3, bytes_accessed=4 * left.size, transcendentals=0
        ),
    )


def tile_kernel(first_ref, first_other_ref, field_ref, field_other_ref, out_ref):
    first = jnp.concatenate([first_ref[...], first_other_ref[...]])
    field = jnp.concatenate([field_ref[...], field_other_ref[...]])
    cross, square = total_of(field * first), total_of(field * field)
    theta = jnp.where(square > 0, cross / jnp.where(square > 0, square, 1.0), 0.0)
    resid = first - theta * field
    energy = total_of(resid * resid)
    row = lax.broadcasted_iota(jnp.int32, out_ref.shape, 0)
    lane = lax.broadcasted_iota(jnp.int32, out_ref.shape, 1)
    values = jnp.where(row == 0, cross, jnp.where(row == 1, square, jnp.where(row == 2, energy, 0.0)))
    out_ref[...] = jnp.where(lane == lax.axis_index("sec"), values, 0.0)


def gathered_kernel(ops, sectors, tile_ref, *refs):
    *tile_refs, out_ref = refs
    op = lax.axis_index("op")
    total = jnp.where(op == 0, tile_ref[...], 0.0)
    for i, ref in enumerate(tile_refs):
        total = total + jnp.where(1 + i * ops + op < sectors, ref[...], 0.0)
    out_ref[...] = total


def merged(sums, cells):
    crosses, squares, energies = (sums[i : i + 1] for i in range(3))
    theta = jnp.sum(crosses, axis=1, keepdims=True) / jnp.sum(squares, axis=1, keepdims=True)
    thetas = jnp.where(squares > 0, crosses / jnp.where(squares > 0, squares, 1.0), 0.0)
    energy = jnp.sum(energies + (thetas - theta) ** 2 * squares, axis=1, keepdims=True)
    return theta, lax.rsqrt(energy / cells + 1e-06)


def image_kernel(cells, total_ref, peer_ref, mask_ref, first_ref, out_ref):
    half = out_ref.shape[0]
    theta, scale = merged(total_ref[pl.ds(half, EXTRA)] + peer_ref[pl.ds(half, EXTRA)], cells)
    total = (total_ref[pl.ds(0, half)] + peer_ref[pl.ds(0, half)]) * mask_ref[...]
    out_ref[...] = scale * (total - theta * first_ref[...])


def correction_kernel(cells, total_ref, peer_ref, first_ref, first_other_ref, field_ref, field_other_ref, out_ref):
    half = first_ref.shape[0]
    core = core_index()
    tile = pl.ds(half, EXTRA)
    theta, scale = merged(total_ref[tile] + peer_ref[tile], cells)
    out_ref[0, rows_of(core, half)] = scale * (first_ref[...] - theta * field_ref[...])
    out_ref[0, rows_of(1 - core, half)] = scale * (first_other_ref[...] - theta * field_other_ref[...])


def output_kernel(mine_ref, other_ref, out_ref):
    half = mine_ref.shape[0]
    core = core_index()
    out_ref[0, rows_of(core, half)] = mine_ref[...]
    out_ref[0, rows_of(1 - core, half)] = other_ref[...]


def local(state, left_ops, right_ops, term_shift, sector_rows, sector_cols):
    sectors, ops = lax.axis_size("sec"), lax.axis_size("op")
    block = state.shape[1]
    half = block // 2

    others = [(i, i ^ 1) for i in range(ops)]
    pairs = [(s, s ^ 1) for s in range(sectors)]
    between = []
    for a in range(ops):
        between += [(s * ops + a, s * ops + (a ^ 2)) for s in (0, sectors - 1)]
        for s in range(1, sectors - 1, 2):
            between += [(s * ops + a, (s + 1) * ops + a), ((s + 1) * ops + a, s * ops + a)]

    def swapped(v):
        return lax.ppermute(v, "op", others)

    def neighbours(mine):
        return lax.ppermute(mine, ("sec", "op"), between), lax.ppermute(mine, "sec", pairs)

    def over_chips(send, keep):
        total = keep + swapped(send)
        step = 2
        while step < ops // 2:
            total = total + lax.ppermute(total, "op", [(i, i ^ step) for i in range(ops)])
            step *= 2
        return total, lax.ppermute(total, "op", [(i, i ^ step) for i in range(ops)])

    field, field_other, mask = call(
        field_kernel,
        [f32(half, block)] * 3,
        [HBM] * 2,
        in_hbm(state), jnp.concatenate([sector_rows, sector_cols]),
        scratch_shapes=[
            pltpu.VMEM((1, block, block), jnp.float32),
            pltpu.SMEM((2,), jnp.int32),
            pltpu.SemaphoreType.DMA((2,)),
        ],
    )
    far, near = neighbours(field)
    left, right = load(left_ops, right_ops, field)
    near, left, right = lax.optimization_barrier((near, left, right))
    halves = [field, field_other, near, swapped(near), far, swapped(far)]
    total, peer = over_chips(*product(term_shift, halves, left, right))

    first = (total + peer) * mask
    far, near = neighbours(first)
    first_other = swapped(first)
    tile = call(tile_kernel, f32(EXTRA, block), [VMEM] * 4, first, first_other, field, field_other)
    tiles = []
    for base in range(1, sectors, ops):
        swaps = [
            (s * ops + a, (s ^ (base + a)) * ops + a if base + a < sectors else (s ^ 1) * ops + a)
            for s in range(sectors)
            for a in range(ops)
        ]
        tiles.append(lax.ppermute(tile, ("sec", "op"), swaps))
    tile = call(
        lambda *refs: gathered_kernel(ops, sectors, *refs),
        f32(EXTRA, block),
        [VMEM] * (1 + len(tiles)),
        tile, *tiles,
    )
    near, tile = lax.optimization_barrier((near, tile))
    halves = [first, first_other, near, swapped(near), far, swapped(far)]
    total, peer = over_chips(*product(term_shift, halves, left, right, tile))

    cells = sectors * block * block
    image = call(
        lambda *refs: image_kernel(cells, *refs),
        f32(half, block),
        [VMEM] * 4,
        total, peer, mask, first,
    )
    correction = call(
        lambda *refs: correction_kernel(cells, *refs),
        f32(1, block, block),
        [VMEM] * 6,
        total, peer, first, first_other, field, field_other,
    )
    image = call(output_kernel, f32(1, block, block), [VMEM] * 2, image, swapped(image))
    return correction, image


def solution(mesh):
    in_specs = (
        P("sec", None, None),
        P("op", "sec", None, None),
        P("op", "sec", None, None),
        P("op"),
        P("sec"),
        P("sec"),
    )
    out_specs = (P("sec", None, None), P("sec", None, None))
    return jax.shard_map(local, mesh=mesh, in_specs=in_specs, out_specs=out_specs, check_vma=False)
```

time: 184 us -> 49.5 us (0.27)
  waiting for transfers between devices: 70.1 us -> 16.9 us
  blocking collectives: 39.7 us -> 0 us
  between operations: 28 us -> 2.01 us
  matrix products: 24.8 us -> 0 us
  Pallas kernels: 0 us -> 11.2 us
  other arithmetic: 7.55 us -> 0.14 us
  starting transfers between devices: 11.7 us -> 19 us
    psum x2 -> x0, waiting for transfers between devices: 63.3 us -> none  [whole_product(): return lax.psum(partial_sum, 'op') * mask]
    psum x2 -> x0, blocking collectives: 39.7 us -> none  [the longest x1 22 us: local(): lax.psum((jnp.sum(field * first), jnp.sum(field * field)), 'sec')]
    dot_general x32 -> x0, matrix products: 24.8 us -> none  [the longest x16 13.8 us: apply_terms(): jnp.einsum('tij,tjl->til', left_ops[term], source, precision=lax.Precisio...]
    pallas_call x0 -> x9, Pallas kernels: none -> 11.2 us  [call(): pl.pallas_call(kernel, out_shape=out_shape, in_specs=in_specs, out_specs=...]
    ppermute x4 -> x16, waiting for transfers between devices: 6.79 us -> 16.9 us  [the longest x2 8.19 us: over_chips(): lax.ppermute(total, 'op', [(i, i ^ step) for i in range(ops)])]
    ppermute x4 -> x16, starting transfers between devices: 11.6 us -> 19 us  [the longest x2 5.51 us: neighbours(): lax.ppermute(mine, 'sec', pairs)]
    mul x3 -> x1, other arithmetic: 4.04 us -> 0.03 us  [local(): first = (total + peer) * mask]
    reduce_sum x2 -> x0, other arithmetic: 3.4 us -> none  [the longest x1 1.7 us: local(): energy = lax.psum(jnp.sum(resid * resid), 'sec')]
  transfers between devices with their start and end apart: 6 -> 16, of which waited for: 4 -> 11; matrix products, arithmetic and copies ran while one was open for 1% -> 0% of each run, Pallas kernels for 0% -> 7%
where the time goes in v2:
time: 49.5 us; the launch traced here: 49.3 us
  starting transfers between devices  19 us (38%)
  waiting for transfers between devices  16.9 us (34%)
  Pallas kernels  11.2 us (23%)
  between operations  2.01 us (4%)
    pallas_call x9, Pallas kernels, call(): pl.pallas_call(kernel, out_shape=out_shape, in_specs=in_specs, out_specs=...  11.2 us
    ppermute x2, waiting for transfers between devices, over_chips(): lax.ppermute(total, 'op', [(i, i ^ step) for i in range(ops)])  8.19 us
    ppermute x2, starting transfers between devices, neighbours(): lax.ppermute(mine, 'sec', pairs)  5.51 us
    ppermute x2, starting transfers between devices, over_chips(): lax.ppermute(total, 'op', [(i, i ^ step) for i in range(ops)])  5.08 us
    ppermute x8, waiting for transfers between devices, swapped(): return lax.ppermute(v, 'op', others)  4.95 us
    ppermute x2, starting transfers between devices, local(): tiles.append(lax.ppermute(tile, ('sec', 'op'), swaps))  4.06 us
    ppermute x2, starting transfers between devices, neighbours(): lax.ppermute(mine, ('sec', 'op'), between)  3.1 us
    ppermute x2, waiting for transfers between devices, local(): tiles.append(lax.ppermute(tile, ('sec', 'op'), swaps))  1.98 us
  transfers between devices with their start and end apart: 16, of which 11 were waited for; matrix products, arithmetic and copies ran while one was open for 0% of the time, Pallas kernels for 7%

profile of v2, /device:TPU:0, one launch (start us, length us, event | category | flops | bytes accessed | tf_op | source)
XLA Modules:
  0.0 49.3 jit_solution(1885312011698160690)
XLA Ops:
  1.9 0.1 pad_add_fusion.live_ref
  2.0 1.0 %shard_map.77 = (f32[128,256]{1,0:T(8,128)S(1)}, f32[128,256]{1,0:T(8,128)S(1)}, f32[128,256]{1,0:T(8,128)S(1)}) custom-call(f32[1,256,256]{2,1,0:T(8,128)} %state_ref.1, s32[2]{0:T(128)S(1)} %pad_add_fusion.live_ref), custom_call_target="tpu_custom_call" | custom-call | tf_op jit(solution)/shard_map/pallas_call | solution.py:22
  3.0 3.0 %collective-permute-start = (f32[128,256]{1,0:T(8,128)S(1)}, f32[128,256]{1,0:T(8,128)S(1)}, u32[]{:S(2)}, u32[]{:S(2)}) collective-permute-start(f32[128,256]{1,0:T(8,128)S(1)} %get-tuple-element.16.field_ref.refs_0_.refs_4_), channel_id=1, source_target_pairs={{0,4},{4,0},{8,12},{12,8},{16,20},{20,16},{24,28},{28,24},{1,5},{5... | collective-permute-start | bytes 393224 | tf_op jit(solution)/shard_map/ppermute | solution.py:239
  6.0 1.5 %collective-permute-start.2 = (f32[128,256]{1,0:T(8,128)S(1)}, f32[128,256]{1,0:T(8,128)S(1)}, u32[]{:S(2)}, u32[]{:S(2)}) collective-permute-start(f32[128,256]{1,0:T(8,128)S(1)} %get-tuple-element.16.field_ref.refs_0_.refs_4_), channel_id=1, source_target_pairs={{0,2},{28,30},{4,8},{8,4},{12,16},{16,12},{20,24},{24,20},{1,3},{2... | collective-permute-start | bytes 393224 | tf_op jit(solution)/shard_map/ppermute | solution.py:239
  7.6 2.2 %shard_map.78 = (f32[8,1,256,256]{3,2,1,0:T(8,128)S(1)}, f32[8,1,256,256]{3,2,1,0:T(8,128)S(1)}) custom-call(f32[8,1,256,256]{3,2,1,0:T(8,128)} %left_ref.1, f32[8,1,256,256]{3,2,1,0:T(8,128)} %right_ref.1, f32[128,256]{1,0:T(8,128)S(1)} %get-tuple-element.16.field_ref.refs_0_.refs_4_), custom_call_target="tpu_custom_call" | custom-call | bytes 4194304 | tf_op jit(solution)/shard_map/pallas_call | solution.py:22
  9.8 1.8 %collective-permute-done.refs_2_ = f32[128,256]{1,0:T(8,128)S(1)} collective-permute-done((f32[128,256]{1,0:T(8,128)S(1)}, f32[128,256]{1,0:T(8,128)S(1)}, u32[]{:S(2)}, u32[]{:S(2)}) %collective-permute-start) | collective-permute-done | bytes 131104 | tf_op jit(solution)/shard_map/ppermute | solution.py:239
  11.6 0.0 collective-permute-done.2.refs_4_
  11.6 0.0 collective-permute-start.3
  11.6 0.5 %collective-permute-start.1 = (f32[128,256]{1,0:T(8,128)S(1)}, f32[128,256]{1,0:T(8,128)S(1)}, u32[]{:S(2)}, u32[]{:S(2)}) collective-permute-start(f32[128,256]{1,0:T(8,128)S(1)} %collective-permute-done.refs_2_), channel_id=1, source_target_pairs={{0,1},{1,0},{2,3},{3,2},{4,5},{5,4},{6,7},{7,6},{8,9},{9,8},{10,11... | collective-permute-start | bytes 393224 | tf_op jit(solution)/shard_map/ppermute | solution.py:236
  12.1 0.8 %collective-permute-done.3.refs_5_ = f32[128,256]{1,0:T(8,128)S(1)} collective-permute-done((f32[128,256]{1,0:T(8,128)S(1)}, f32[128,256]{1,0:T(8,128)S(1)}, u32[]{:S(2)}, u32[]{:S(2)}) %collective-permute-start.3) | collective-permute-done | bytes 131104 | tf_op jit(solution)/shard_map/ppermute | solution.py:236
  12.9 0.2 collective-permute-done.1.refs_3_
  13.1 2.8 %shard_map.79 = (f32[128,256]{1,0:T(8,128)S(1)}, f32[128,256]{1,0:T(8,128)S(1)}) custom-call(s32[8]{0:T(128)} %shift_ref.3, f32[128,256]{1,0:T(8,128)S(1)} %get-tuple-element.16.field_ref.refs_0_.refs_4_, f32[128,256]{1,0:T(8,128)S(1)} %get-tuple-element.17.refs_1_.field_other_ref.refs_5_, f32[128,256]{1,0:T(8,128)S(1)} %collective-permute-done.refs_2_, ...), custom_call_target="tpu_custom_call" | custom-call | flops 1610612736 | bytes 2097152 | tf_op jit(solution)/shard_map/pallas_call | solution.py:22
  16.0 0.4 collective-permute-start.4
  16.4 1.0 %collective-permute-done.4 = f32[128,256]{1,0:T(8,128)S(1)} collective-permute-done((f32[128,256]{1,0:T(8,128)S(1)}, f32[128,256]{1,0:T(8,128)S(1)}, u32[]{:S(2)}, u32[]{:S(2)}) %collective-permute-start.4) | collective-permute-done | bytes 131104 | tf_op jit(solution)/shard_map/ppermute | solution.py:236
  17.4 1.6 %collective-permute-start.5 = (f32[128,256]{1,0:T(8,128)S(1)}, f32[128,256]{1,0:T(8,128)S(1)}, u32[]{:S(2)}, u32[]{:S(2)}) collective-permute-start(f32[128,256]{1,0:T(8,128)S(1)} %add.9), channel_id=1, source_target_pairs={{0,2},{1,3},{2,0},{3,1},{4,6},{5,7},{6,4},{7,5},{8,10},{9,11},{10,... | collective-permute-start | bytes 393224 | tf_op jit(solution)/shard_map/ppermute | solution.py:247
  19.0 4.2 %collective-permute-done.5 = f32[128,256]{1,0:T(8,128)S(1)} collective-permute-done((f32[128,256]{1,0:T(8,128)S(1)}, f32[128,256]{1,0:T(8,128)S(1)}, u32[]{:S(2)}, u32[]{:S(2)}) %collective-permute-start.5) | collective-permute-done | bytes 131104 | tf_op jit(solution)/shard_map/ppermute | solution.py:247
  23.2 0.1 collective-permute-start.6
  23.3 1.6 %collective-permute-start.11 = (f32[128,256]{1,0:T(8,128)S(1)}, f32[128,256]{1,0:T(8,128)S(1)}, u32[]{:S(2)}, u32[]{:S(2)}) collective-permute-start(f32[128,256]{1,0:T(8,128)S(1)} %add_multiply_fusion.first_ref.refs_0_.refs_2_.refs_3_), channel_id=1, source_target_pairs={{0,2},{28,30},{4,8},{8,4},{12,16},{16,12},{20,24},{24,20},{1,3},{2... | collective-permute-start | bytes 393224 | tf_op jit(solution)/shard_map/ppermute | solution.py:239
  24.9 2.5 %collective-permute-start.7 = (f32[128,256]{1,0:T(8,128)S(1)}, f32[128,256]{1,0:T(8,128)S(1)}, u32[]{:S(2)}, u32[]{:S(2)}) collective-permute-start(f32[128,256]{1,0:T(8,128)S(1)} %add_multiply_fusion.first_ref.refs_0_.refs_2_.refs_3_), channel_id=1, source_target_pairs={{0,4},{4,0},{8,12},{12,8},{16,20},{20,16},{24,28},{28,24},{1,5},{5... | collective-permute-start | bytes 393224 | tf_op jit(solution)/shard_map/ppermute | solution.py:239
  27.4 0.0 collective-permute-done.6.first_other_ref.refs_1_.refs_3_
  27.4 0.3 shard_map.80.refs_0_
  27.7 2.4 %collective-permute-start.9 = (f32[8,256]{1,0:T(8,128)S(1)}, f32[8,256]{1,0:T(8,128)S(1)}, u32[]{:S(2)}, u32[]{:S(2)}) collective-permute-start(f32[8,256]{1,0:T(8,128)S(1)} %shard_map.80.refs_0_), channel_id=1, source_target_pairs={{0,20},{1,25},{2,30},{3,7},{4,16},{5,29},{6,26},{7,3},{8,28},{9,17... | collective-permute-start | bytes 24584 | tf_op jit(solution)/shard_map/ppermute | solution.py:277
  30.1 1.7 %collective-permute-start.8 = (f32[8,256]{1,0:T(8,128)S(1)}, f32[8,256]{1,0:T(8,128)S(1)}, u32[]{:S(2)}, u32[]{:S(2)}) collective-permute-start(f32[8,256]{1,0:T(8,128)S(1)} %shard_map.80.refs_0_), channel_id=1, source_target_pairs={{0,4},{1,9},{2,14},{3,19},{4,0},{5,13},{6,10},{7,23},{8,12},{9,1},... | collective-permute-start | bytes 24584 | tf_op jit(solution)/shard_map/ppermute | solution.py:277
  31.7 0.0 collective-permute-done.11.refs_4_
  31.7 0.0 collective-permute-start.12
  31.7 1.4 %collective-permute-done.9.refs_2_ = f32[8,256]{1,0:T(8,128)S(1)} collective-permute-done((f32[8,256]{1,0:T(8,128)S(1)}, f32[8,256]{1,0:T(8,128)S(1)}, u32[]{:S(2)}, u32[]{:S(2)}) %collective-permute-start.9) | collective-permute-done | bytes 8224 | tf_op jit(solution)/shard_map/ppermute | solution.py:277
  33.1 0.6 %collective-permute-done.8.refs_1_ = f32[8,256]{1,0:T(8,128)S(1)} collective-permute-done((f32[8,256]{1,0:T(8,128)S(1)}, f32[8,256]{1,0:T(8,128)S(1)}, u32[]{:S(2)}, u32[]{:S(2)}) %collective-permute-start.8) | collective-permute-done | bytes 8224 | tf_op jit(solution)/shard_map/ppermute | solution.py:277
  33.7 0.0 collective-permute-done.7.refs_2_
  33.7 0.0 collective-permute-start.10
  33.7 0.0 collective-permute-done.12.refs_5_
  33.7 1.3 %collective-permute-done.10.refs_3_ = f32[128,256]{1,0:T(8,128)S(1)} collective-permute-done((f32[128,256]{1,0:T(8,128)S(1)}, f32[128,256]{1,0:T(8,128)S(1)}, u32[]{:S(2)}, u32[]{:S(2)}) %collective-permute-start.10) | collective-permute-done | bytes 131104 | tf_op jit(solution)/shard_map/ppermute | solution.py:236
  35.1 2.8 %shard_map.82 = (f32[136,256]{1,0:T(8,128)S(1)}, f32[136,256]{1,0:T(8,128)S(1)}) custom-call(s32[8]{0:T(128)} %shift_ref.3, f32[128,256]{1,0:T(8,128)S(1)} %add_multiply_fusion.first_ref.refs_0_.refs_2_.refs_3_, f32[128,256]{1,0:T(8,128)S(1)} %collective-permute-done.6.first_other_ref.refs_1_.refs_3_, f32[128,256]{1,0:T(8,128)S(1)} %collective-permute-done.7.refs_2_, ...), custom_call_target="tpu_custom_call" | custom-call | flops 1610612736 | bytes 2097152 | tf_op jit(solution)/shard_map/pallas_call | solution.py:22
  37.9 0.2 collective-permute-start.13
  38.1 1.2 %collective-permute-done.13 = f32[136,256]{1,0:T(8,128)S(1)} collective-permute-done((f32[136,256]{1,0:T(8,128)S(1)}, f32[136,256]{1,0:T(8,128)S(1)}, u32[]{:S(2)}, u32[]{:S(2)}) %collective-permute-start.13) | collective-permute-done | bytes 139296 | tf_op jit(solution)/shard_map/ppermute | solution.py:236
  39.4 3.5 %collective-permute-start.14 = (f32[136,256]{1,0:T(8,128)S(1)}, f32[136,256]{1,0:T(8,128)S(1)}, u32[]{:S(2)}, u32[]{:S(2)}) collective-permute-start(f32[136,256]{1,0:T(8,128)S(1)} %add.11.refs_0_), channel_id=1, source_target_pairs={{0,2},{1,3},{2,0},{3,1},{4,6},{5,7},{6,4},{7,5},{8,10},{9,11},{10,... | collective-permute-start | bytes 417800 | tf_op jit(solution)/shard_map/ppermute | solution.py:247
  42.9 4.0 %collective-permute-done.14.refs_1_ = f32[136,256]{1,0:T(8,128)S(1)} collective-permute-done((f32[136,256]{1,0:T(8,128)S(1)}, f32[136,256]{1,0:T(8,128)S(1)}, u32[]{:S(2)}, u32[]{:S(2)}) %collective-permute-start.14) | collective-permute-done | bytes 139296 | tf_op jit(solution)/shard_map/ppermute | solution.py:247
  46.8 0.3 shard_map.84.mine_ref
  47.1 0.1 collective-permute-start.15
  47.2 1.0 %shard_map.83 = f32[1,256,256]{2,1,0:T(8,128)} custom-call(f32[136,256]{1,0:T(8,128)S(1)} %add.11.refs_0_, f32[136,256]{1,0:T(8,128)S(1)} %collective-permute-done.14.refs_1_, f32[128,256]{1,0:T(8,128)S(1)} %add_multiply_fusion.first_ref.refs_0_.refs_2_.refs_3_, f32[128,256]{1,0:T(8,128)S(1)} %collective-permute-done.6.first_other_ref.refs_1_.refs_3_, ...), custom_call_target="tpu_custom_call" | custom-call | tf_op jit(solution)/shard_map/pallas_call | solution.py:22
  48.2 0.3 collective-permute-done.15.other_ref
  48.5 0.7 %shard_map.85 = f32[1,256,256]{2,1,0:T(8,128)} custom-call(f32[128,256]{1,0:T(8,128)S(1)} %shard_map.84.mine_ref, f32[128,256]{1,0:T(8,128)S(1)} %collective-permute-done.15.other_ref), custom_call_target="tpu_custom_call" | custom-call | tf_op jit(solution)/shard_map/pallas_call | solution.py:22
  (4 shorter events, 0.1 us)
Async XLA Ops:
  3.0 8.6 %collective-permute-start = (f32[128,256]{1,0:T(8,128)S(1)}, f32[128,256]{1,0:T(8,128)S(1)}, u32[]{:S(2)}, u32[]{:S(2)}) collective-permute-start(f32[128,256]{1,0:T(8,128)S(1)} %get-tuple-element.16.field_ref.refs_0_.refs_4_), channel_id=1, source_target_pairs={{0,4},{4,0},{8,12},{12,8},{16,20},{20,16},{24,28},{28,24},{1,5},{5... | collective-permute-start | bytes 393224 | tf_op jit(solution)/shard_map/ppermute | solution.py:239
  6.0 5.6 %collective-permute-start.2 = (f32[128,256]{1,0:T(8,128)S(1)}, f32[128,256]{1,0:T(8,128)S(1)}, u32[]{:S(2)}, u32[]{:S(2)}) collective-permute-start(f32[128,256]{1,0:T(8,128)S(1)} %get-tuple-element.16.field_ref.refs_0_.refs_4_), channel_id=1, source_target_pairs={{0,2},{28,30},{4,8},{8,4},{12,16},{16,12},{20,24},{24,20},{1,3},{2... | collective-permute-start | bytes 393224 | tf_op jit(solution)/shard_map/ppermute | solution.py:239
  11.6 1.3 %collective-permute-start.3 = (f32[128,256]{1,0:T(8,128)S(1)}, f32[128,256]{1,0:T(8,128)S(1)}, u32[]{:S(2)}, u32[]{:S(2)}) collective-permute-start(f32[128,256]{1,0:T(8,128)S(1)} %collective-permute-done.2.refs_4_), channel_id=1, source_target_pairs={{0,1},{1,0},{2,3},{3,2},{4,5},{5,4},{6,7},{7,6},{8,9},{9,8},{10,11... | collective-permute-start | bytes 393224 | tf_op jit(solution)/shard_map/ppermute | solution.py:236
  11.6 1.5 %collective-permute-start.1 = (f32[128,256]{1,0:T(8,128)S(1)}, f32[128,256]{1,0:T(8,128)S(1)}, u32[]{:S(2)}, u32[]{:S(2)}) collective-permute-start(f32[128,256]{1,0:T(8,128)S(1)} %collective-permute-done.refs_2_), channel_id=1, source_target_pairs={{0,1},{1,0},{2,3},{3,2},{4,5},{5,4},{6,7},{7,6},{8,9},{9,8},{10,11... | collective-permute-start | bytes 393224 | tf_op jit(solution)/shard_map/ppermute | solution.py:236
  16.0 1.4 %collective-permute-start.4 = (f32[128,256]{1,0:T(8,128)S(1)}, f32[128,256]{1,0:T(8,128)S(1)}, u32[]{:S(2)}, u32[]{:S(2)}) collective-permute-start(f32[128,256]{1,0:T(8,128)S(1)} %get-tuple-element.24), channel_id=1, source_target_pairs={{0,1},{1,0},{2,3},{3,2},{4,5},{5,4},{6,7},{7,6},{8,9},{9,8},{10,11... | collective-permute-start | bytes 393224 | tf_op jit(solution)/shard_map/ppermute | solution.py:236
  17.4 5.8 %collective-permute-start.5 = (f32[128,256]{1,0:T(8,128)S(1)}, f32[128,256]{1,0:T(8,128)S(1)}, u32[]{:S(2)}, u32[]{:S(2)}) collective-permute-start(f32[128,256]{1,0:T(8,128)S(1)} %add.9), channel_id=1, source_target_pairs={{0,2},{1,3},{2,0},{3,1},{4,6},{5,7},{6,4},{7,5},{8,10},{9,11},{10,... | collective-permute-start | bytes 393224 | tf_op jit(solution)/shard_map/ppermute | solution.py:247
  23.2 4.2 %collective-permute-start.6 = (f32[128,256]{1,0:T(8,128)S(1)}, f32[128,256]{1,0:T(8,128)S(1)}, u32[]{:S(2)}, u32[]{:S(2)}) collective-permute-start(f32[128,256]{1,0:T(8,128)S(1)} %add_multiply_fusion.first_ref.refs_0_.refs_2_.refs_3_), channel_id=1, source_target_pairs={{0,1},{1,0},{2,3},{3,2},{4,5},{5,4},{6,7},{7,6},{8,9},{9,8},{10,11... | collective-permute-start | bytes 393224 | tf_op jit(solution)/shard_map/ppermute | solution.py:236
  23.3 8.4 %collective-permute-start.11 = (f32[128,256]{1,0:T(8,128)S(1)}, f32[128,256]{1,0:T(8,128)S(1)}, u32[]{:S(2)}, u32[]{:S(2)}) collective-permute-start(f32[128,256]{1,0:T(8,128)S(1)} %add_multiply_fusion.first_ref.refs_0_.refs_2_.refs_3_), channel_id=1, source_target_pairs={{0,2},{28,30},{4,8},{8,4},{12,16},{16,12},{20,24},{24,20},{1,3},{2... | collective-permute-start | bytes 393224 | tf_op jit(solution)/shard_map/ppermute | solution.py:239
  24.9 8.8 %collective-permute-start.7 = (f32[128,256]{1,0:T(8,128)S(1)}, f32[128,256]{1,0:T(8,128)S(1)}, u32[]{:S(2)}, u32[]{:S(2)}) collective-permute-start(f32[128,256]{1,0:T(8,128)S(1)} %add_multiply_fusion.first_ref.refs_0_.refs_2_.refs_3_), channel_id=1, source_target_pairs={{0,4},{4,0},{8,12},{12,8},{16,20},{20,16},{24,28},{28,24},{1,5},{5... | collective-permute-start | bytes 393224 | tf_op jit(solution)/shard_map/ppermute | solution.py:239
  27.7 5.5 %collective-permute-start.9 = (f32[8,256]{1,0:T(8,128)S(1)}, f32[8,256]{1,0:T(8,128)S(1)}, u32[]{:S(2)}, u32[]{:S(2)}) collective-permute-start(f32[8,256]{1,0:T(8,128)S(1)} %shard_map.80.refs_0_), channel_id=1, source_target_pairs={{0,20},{1,25},{2,30},{3,7},{4,16},{5,29},{6,26},{7,3},{8,28},{9,17... | collective-permute-start | bytes 24584 | tf_op jit(solution)/shard_map/ppermute | solution.py:277
  30.1 3.7 %collective-permute-start.8 = (f32[8,256]{1,0:T(8,128)S(1)}, f32[8,256]{1,0:T(8,128)S(1)}, u32[]{:S(2)}, u32[]{:S(2)}) collective-permute-start(f32[8,256]{1,0:T(8,128)S(1)} %shard_map.80.refs_0_), channel_id=1, source_target_pairs={{0,4},{1,9},{2,14},{3,19},{4,0},{5,13},{6,10},{7,23},{8,12},{9,1},... | collective-permute-start | bytes 24584 | tf_op jit(solution)/shard_map/ppermute | solution.py:277
  31.7 2.0 %collective-permute-start.12 = (f32[128,256]{1,0:T(8,128)S(1)}, f32[128,256]{1,0:T(8,128)S(1)}, u32[]{:S(2)}, u32[]{:S(2)}) collective-permute-start(f32[128,256]{1,0:T(8,128)S(1)} %collective-permute-done.11.refs_4_), channel_id=1, source_target_pairs={{0,1},{1,0},{2,3},{3,2},{4,5},{5,4},{6,7},{7,6},{8,9},{9,8},{10,11... | collective-permute-start | bytes 393224 | tf_op jit(solution)/shard_map/ppermute | solution.py:236
  33.7 1.3 %collective-permute-start.10 = (f32[128,256]{1,0:T(8,128)S(1)}, f32[128,256]{1,0:T(8,128)S(1)}, u32[]{:S(2)}, u32[]{:S(2)}) collective-permute-start(f32[128,256]{1,0:T(8,128)S(1)} %collective-permute-done.7.refs_2_), channel_id=1, source_target_pairs={{0,1},{1,0},{2,3},{3,2},{4,5},{5,4},{6,7},{7,6},{8,9},{9,8},{10,11... | collective-permute-start | bytes 393224 | tf_op jit(solution)/shard_map/ppermute | solution.py:236
  37.9 1.4 %collective-permute-start.13 = (f32[136,256]{1,0:T(8,128)S(1)}, f32[136,256]{1,0:T(8,128)S(1)}, u32[]{:S(2)}, u32[]{:S(2)}) collective-permute-start(f32[136,256]{1,0:T(8,128)S(1)} %get-tuple-element.29), channel_id=1, source_target_pairs={{0,1},{1,0},{2,3},{3,2},{4,5},{5,4},{6,7},{7,6},{8,9},{9,8},{10,11... | collective-permute-start | bytes 417800 | tf_op jit(solution)/shard_map/ppermute | solution.py:236
  39.4 7.5 %collective-permute-start.14 = (f32[136,256]{1,0:T(8,128)S(1)}, f32[136,256]{1,0:T(8,128)S(1)}, u32[]{:S(2)}, u32[]{:S(2)}) collective-permute-start(f32[136,256]{1,0:T(8,128)S(1)} %add.11.refs_0_), channel_id=1, source_target_pairs={{0,2},{1,3},{2,0},{3,1},{4,6},{5,7},{6,4},{7,5},{8,10},{9,11},{10,... | collective-permute-start | bytes 417800 | tf_op jit(solution)/shard_map/ppermute | solution.py:247
  47.1 1.4 %collective-permute-start.15 = (f32[128,256]{1,0:T(8,128)S(1)}, f32[128,256]{1,0:T(8,128)S(1)}, u32[]{:S(2)}, u32[]{:S(2)}) collective-permute-start(f32[128,256]{1,0:T(8,128)S(1)} %shard_map.84.mine_ref), channel_id=1, source_target_pairs={{0,1},{1,0},{2,3},{3,2},{4,5},{5,4},{6,7},{7,6},{8,9},{9,8},{10,11... | collective-permute-start | bytes 393224 | tf_op jit(solution)/shard_map/ppermute | solution.py:236

commit v3 on v2

--- a/solution.py
+++ b/solution.py
@@ -75,34 +75,40 @@
     mask_ref[...] = jnp.where((row + core * half < rows) & (lane < cols), 1.0, 0.0)
 
 
-def load_kernel(left_ref, right_ref, field_ref, left_out, right_out, sems):
+def load_kernel(left_ref, right_ref, shift_ref, field_ref, left_out, right_out, shift_out, shift, sems):
+    terms = left_ref.shape[0]
+    shifts = pltpu.make_async_copy(shift_ref, shift, sems.at[2, 0])
     copies = [
-        pltpu.make_async_copy(left_ref, left_out, sems.at[0]),
-        pltpu.make_async_copy(right_ref, right_out, sems.at[1]),
+        pltpu.make_async_copy(ref.at[term], out.at[term], sems.at[side, term])
+        for term in range(terms)
+        for side, (ref, out) in enumerate(((left_ref, left_out), (right_ref, right_out)))
     ]
+    shifts.start()
     for copy in copies:
         copy.start()
+    shifts.wait()
+    for term in range(terms):
+        shift_out[term] = jnp.full(shift_out.shape[1:], shift[term], jnp.int32)
     for copy in copies:
         copy.wait()
 
 
-def load(left_ops, right_ops, field):
+def load(left_ops, right_ops, shift, field):
+    terms = shift.shape[0]
     return call(
         load_kernel,
-        [f32(*left_ops.shape), f32(*right_ops.shape)],
-        [HBM, HBM, VMEM],
-        in_hbm(left_ops), in_hbm(right_ops), field,
-        scratch_shapes=[pltpu.SemaphoreType.DMA((2,))],
+        [f32(*left_ops.shape), f32(*right_ops.shape), jax.ShapeDtypeStruct((terms, 8, 128), jnp.int32)],
+        [HBM, HBM, HBM, VMEM],
+        in_hbm(left_ops), in_hbm(right_ops), in_hbm(shift), field,
+        scratch_shapes=[pltpu.SMEM(shift.shape, jnp.int32), pltpu.SemaphoreType.DMA((3, terms))],
         cost_estimate=pl.CostEstimate(flops=0, bytes_accessed=8 * left_ops.size, transcendentals=0),
     )
 
 
 def product_kernel(shift_ref, *refs):
     halves, (left_ref, right_ref) = refs[:6], refs[6:8]
-    tile_ref = refs[8] if len(refs) == 16 else None
-    send_ref, keep_ref, high, low, total, shift, sem = refs[-7:]
-    shifts = pltpu.make_async_copy(shift_ref, shift, sem)
-    shifts.start()
+    tile_ref = refs[8] if len(refs) == 14 else None
+    send_ref, keep_ref, high, low, total = refs[-5:]
     block = total.shape[0]
     half = block // 2
     core, sector = core_index(), lax.axis_index("sec")
@@ -122,10 +128,9 @@
         high[2] = jnp.zeros(high.shape[1:], high.dtype)
         low[2] = jnp.zeros(low.shape[1:], low.dtype)
 
-    shifts.wait()
     out = None
     for term in range(left_ref.shape[0]):
-        source = 1 - shift[term]
+        source = 1 - shift_ref[term][0, 0]
         left_high, left_low = split(left_ref[term, 0])
         right_high, right_low = split(right_ref[term, 0])
         v_high, v_low = high[source], low[source]
@@ -150,15 +155,13 @@
     return call(
         product_kernel,
         [f32(rows, block)] * 2,
-        [HBM] + [VMEM] * len(arrays),
-        in_hbm(shift), *arrays,
+        [VMEM] * (1 + len(arrays)),
+        shift, *arrays,
         mib=16,
         scratch_shapes=[
             pltpu.VMEM((3, block, block), jnp.bfloat16),
             pltpu.VMEM((3, block, block), jnp.bfloat16),
             pltpu.VMEM((block, block), jnp.float32),
-            pltpu.SMEM(shift.shape, jnp.int32),
-            pltpu.SemaphoreType.DMA(()),
         ],
         cost_estimate=pl.CostEstimate(
             flops=12 * terms * block**3, bytes_accessed=4 * left.size, transcendentals=0
@@ -179,13 +182,19 @@
     out_ref[...] = jnp.where(lane == lax.axis_index("sec"), values, 0.0)
 
 
-def gathered_kernel(ops, sectors, tile_ref, *refs):
+def gathered_kernel(planes, tile_ref, *refs):
     *tile_refs, out_ref = refs
-    op = lax.axis_index("op")
-    total = jnp.where(op == 0, tile_ref[...], 0.0)
+    core = core_index()
+    total = jnp.where(core == 0, tile_ref[...], 0.0)
     for i, ref in enumerate(tile_refs):
-        total = total + jnp.where(1 + i * ops + op < sectors, ref[...], 0.0)
+        total = total + jnp.where(1 + 2 * i + core < planes, ref[...], 0.0)
     out_ref[...] = total
+
+
+def summed_kernel(keep_ref, got_ref, total_ref, sums_ref):
+    half = total_ref.shape[0]
+    total_ref[...] = keep_ref[pl.ds(0, half)] + got_ref[pl.ds(0, half)]
+    sums_ref[...] = keep_ref[pl.ds(half, EXTRA)] + got_ref[pl.ds(half, EXTRA)]
 
 
 def merged(sums, cells):
@@ -196,18 +205,16 @@
     return theta, lax.rsqrt(energy / cells + 1e-06)
 
 
-def image_kernel(cells, total_ref, peer_ref, mask_ref, first_ref, out_ref):
-    half = out_ref.shape[0]
-    theta, scale = merged(total_ref[pl.ds(half, EXTRA)] + peer_ref[pl.ds(half, EXTRA)], cells)
-    total = (total_ref[pl.ds(0, half)] + peer_ref[pl.ds(0, half)]) * mask_ref[...]
+def image_kernel(cells, sums_ref, total_ref, peer_ref, mask_ref, first_ref, out_ref):
+    theta, scale = merged(sums_ref[...], cells)
+    total = (total_ref[...] + peer_ref[...]) * mask_ref[...]
     out_ref[...] = scale * (total - theta * first_ref[...])
 
 
-def correction_kernel(cells, total_ref, peer_ref, first_ref, first_other_ref, field_ref, field_other_ref, out_ref):
+def correction_kernel(cells, sums_ref, first_ref, first_other_ref, field_ref, field_other_ref, out_ref):
     half = first_ref.shape[0]
     core = core_index()
-    tile = pl.ds(half, EXTRA)
-    theta, scale = merged(total_ref[tile] + peer_ref[tile], cells)
+    theta, scale = merged(sums_ref[...], cells)
     out_ref[0, rows_of(core, half)] = scale * (first_ref[...] - theta * field_ref[...])
     out_ref[0, rows_of(1 - core, half)] = scale * (first_other_ref[...] - theta * field_other_ref[...])
 
@@ -238,8 +245,7 @@
     def neighbours(mine):
         return lax.ppermute(mine, ("sec", "op"), between), lax.ppermute(mine, "sec", pairs)
 
-    def over_chips(send, keep):
-        total = keep + swapped(send)
+    def over_chips(total):
         step = 2
         while step < ops // 2:
             total = total + lax.ppermute(total, "op", [(i, i ^ step) for i in range(ops)])
@@ -258,45 +264,52 @@
         ],
     )
     far, near = neighbours(field)
-    left, right = load(left_ops, right_ops, field)
+    left, right, shift = load(left_ops, right_ops, term_shift, field)
     near, left, right = lax.optimization_barrier((near, left, right))
     halves = [field, field_other, near, swapped(near), far, swapped(far)]
-    total, peer = over_chips(*product(term_shift, halves, left, right))
+    send, keep = product(shift, halves, left, right)
+    total, peer = over_chips(keep + swapped(send))
 
     first = (total + peer) * mask
     far, near = neighbours(first)
     first_other = swapped(first)
     tile = call(tile_kernel, f32(EXTRA, block), [VMEM] * 4, first, first_other, field, field_other)
+    planes = sectors // 2
     tiles = []
-    for base in range(1, sectors, ops):
+    for base in range(1, planes, 2):
         swaps = [
-            (s * ops + a, (s ^ (base + a)) * ops + a if base + a < sectors else (s ^ 1) * ops + a)
+            (s * ops + a, (s ^ (2 * (base + a % 2) if base + a % 2 < planes else 2)) * ops + a)
             for s in range(sectors)
             for a in range(ops)
         ]
         tiles.append(lax.ppermute(tile, ("sec", "op"), swaps))
     tile = call(
-        lambda *refs: gathered_kernel(ops, sectors, *refs),
+        lambda *refs: gathered_kernel(planes, *refs),
         f32(EXTRA, block),
         [VMEM] * (1 + len(tiles)),
         tile, *tiles,
     )
     near, tile = lax.optimization_barrier((near, tile))
     halves = [first, first_other, near, swapped(near), far, swapped(far)]
-    total, peer = over_chips(*product(term_shift, halves, left, right, tile))
+    send, keep = product(shift, halves, left, right, tile)
+    total, sums = call(
+        summed_kernel, [f32(half, block), f32(EXTRA, block)], [VMEM] * 2, keep, swapped(send)
+    )
+    total, peer = over_chips(total)
+    sums = sums + lax.ppermute(sums, "sec", pairs)
 
     cells = sectors * block * block
     image = call(
         lambda *refs: image_kernel(cells, *refs),
         f32(half, block),
-        [VMEM] * 4,
-        total, peer, mask, first,
+        [VMEM] * 5,
+        sums, total, peer, mask, first,
     )
     correction = call(
         lambda *refs: correction_kernel(cells, *refs),
         f32(1, block, block),
-        [VMEM] * 6,
-        total, peer, first, first_other, field, field_other,
+        [VMEM] * 5,
+        sums, first, first_other, field, field_other,
     )
     image = call(output_kernel, f32(1, block, block), [VMEM] * 2, image, swapped(image))
     return correction, image

time: 49.5 us -> 46.4 us (0.937)
  waiting for transfers between devices: 16.9 us -> 15.7 us
  starting transfers between devices: 19 us -> 18.1 us
  Pallas kernels: 11.2 us -> 10.4 us
    ppermute x2, waiting for transfers between devices: 8.19 us -> 4.58 us  [over_chips(): lax.ppermute(total, 'op', [(i, i ^ step) for i in range(ops)])]
    ppermute x2, starting transfers between devices: 5.08 us -> 3.17 us  [over_chips(): lax.ppermute(total, 'op', [(i, i ^ step) for i in range(ops)])]
    ppermute x0 -> x1, starting transfers between devices: none -> 1.85 us  [local(): sums = sums + lax.ppermute(sums, 'sec', pairs)]
    ppermute x0 -> x1, waiting for transfers between devices: none -> 1.81 us  [local(): sums = sums + lax.ppermute(sums, 'sec', pairs)]
    ppermute x2, starting transfers between devices: 4.06 us -> 3.15 us  [local(): tiles.append(lax.ppermute(tile, ('sec', 'op'), swaps))]
    pallas_call x9 -> x10, Pallas kernels: 11.2 us -> 10.4 us  [call(): pl.pallas_call(kernel, out_shape=out_shape, in_specs=in_specs, out_specs=...]
    ppermute x2, waiting for transfers between devices: 1.98 us -> 2.64 us  [local(): tiles.append(lax.ppermute(tile, ('sec', 'op'), swaps))]
  transfers between devices with their start and end apart: 16 -> 17, of which waited for: 11 -> 11; matrix products, arithmetic and copies ran while one was open for 0% -> 0% of each run, Pallas kernels for 7% -> 8%
where the time goes in v3:
time: 46.4 us; the launch traced here: 46.3 us
  starting transfers between devices  18.1 us (39%)
  waiting for transfers between devices  15.7 us (34%)
  Pallas kernels  10.4 us (22%)
  between operations  2.01 us (4%)
    pallas_call x10, Pallas kernels, call(): pl.pallas_call(kernel, out_shape=out_shape, in_specs=in_specs, out_specs=...  10.4 us
    ppermute x2, starting transfers between devices, neighbours(): lax.ppermute(mine, 'sec', pairs)  5.5 us
    ppermute x8, waiting for transfers between devices, swapped(): return lax.ppermute(v, 'op', others)  4.94 us
    ppermute x2, waiting for transfers between devices, over_chips(): lax.ppermute(total, 'op', [(i, i ^ step) for i in range(ops)])  4.58 us
    ppermute x2, starting transfers between devices, over_chips(): lax.ppermute(total, 'op', [(i, i ^ step) for i in range(ops)])  3.17 us
    ppermute x2, starting transfers between devices, local(): tiles.append(lax.ppermute(tile, ('sec', 'op'), swaps))  3.15 us
    ppermute x2, starting transfers between devices, neighbours(): lax.ppermute(mine, ('sec', 'op'), between)  3.1 us
    ppermute x2, waiting for transfers between devices, local(): tiles.append(lax.ppermute(tile, ('sec', 'op'), swaps))  2.64 us
  transfers between devices with their start and end apart: 17, of which 11 were waited for; matrix products, arithmetic and copies ran while one was open for 0% of the time, Pallas kernels for 8%

profile of v3, /device:TPU:0, one launch (start us, length us, event | category | flops | bytes accessed | tf_op | source)
XLA Modules:
  0.0 46.3 jit_solution(17664386359157136278)
XLA Ops:
  1.9 0.1 pad_add_fusion.live_ref
  2.0 1.0 %shard_map.77 = (f32[128,256]{1,0:T(8,128)S(1)}, f32[128,256]{1,0:T(8,128)S(1)}, f32[128,256]{1,0:T(8,128)S(1)}) custom-call(f32[1,256,256]{2,1,0:T(8,128)} %state_ref.1, s32[2]{0:T(128)S(1)} %pad_add_fusion.live_ref), custom_call_target="tpu_custom_call" | custom-call | tf_op jit(solution)/shard_map/pallas_call | solution.py:22
  3.0 3.0 %collective-permute-start = (f32[128,256]{1,0:T(8,128)S(1)}, f32[128,256]{1,0:T(8,128)S(1)}, u32[]{:S(2)}, u32[]{:S(2)}) collective-permute-start(f32[128,256]{1,0:T(8,128)S(1)} %get-tuple-element.19.field_ref.refs_0_.refs_3_), channel_id=1, source_target_pairs={{0,4},{4,0},{8,12},{12,8},{16,20},{20,16},{24,28},{28,24},{1,5},{5... | collective-permute-start | bytes 393224 | tf_op jit(solution)/shard_map/ppermute | solution.py:246
  6.0 1.5 %collective-permute-start.2 = (f32[128,256]{1,0:T(8,128)S(1)}, f32[128,256]{1,0:T(8,128)S(1)}, u32[]{:S(2)}, u32[]{:S(2)}) collective-permute-start(f32[128,256]{1,0:T(8,128)S(1)} %get-tuple-element.19.field_ref.refs_0_.refs_3_), channel_id=1, source_target_pairs={{0,2},{28,30},{4,8},{8,4},{12,16},{16,12},{20,24},{24,20},{1,3},{2... | collective-permute-start | bytes 393224 | tf_op jit(solution)/shard_map/ppermute | solution.py:246
  7.6 2.3 %shard_map.78 = (f32[8,1,256,256]{3,2,1,0:T(8,128)S(1)}, f32[8,1,256,256]{3,2,1,0:T(8,128)S(1)}, s32[8,8,128]{2,1,0:T(8,128)S(1)}) custom-call(f32[8,1,256,256]{3,2,1,0:T(8,128)} %left_ref.1, f32[8,1,256,256]{3,2,1,0:T(8,128)} %right_ref.1, s32[8]{0:T(128)} %shift_ref.1, f32[128,256]{1,0:T(8,128)S(1)} %get-tuple-element.19.field_ref.refs_0_.refs_3_), custom_call_target="tpu_custom_call" | custom-call | bytes 4194304 | tf_op jit(solution)/shard_map/pallas_call | solution.py:22
  9.9 1.7 %collective-permute-done.refs_2_ = f32[128,256]{1,0:T(8,128)S(1)} collective-permute-done((f32[128,256]{1,0:T(8,128)S(1)}, f32[128,256]{1,0:T(8,128)S(1)}, u32[]{:S(2)}, u32[]{:S(2)}) %collective-permute-start) | collective-permute-done | bytes 131104 | tf_op jit(solution)/shard_map/ppermute | solution.py:246
  11.6 0.0 collective-permute-done.2.refs_4_
  11.6 0.0 collective-permute-start.3
  11.6 0.5 %collective-permute-start.1 = (f32[128,256]{1,0:T(8,128)S(1)}, f32[128,256]{1,0:T(8,128)S(1)}, u32[]{:S(2)}, u32[]{:S(2)}) collective-permute-start(f32[128,256]{1,0:T(8,128)S(1)} %collective-permute-done.refs_2_), channel_id=1, source_target_pairs={{0,1},{1,0},{2,3},{3,2},{4,5},{5,4},{6,7},{7,6},{8,9},{9,8},{10,11... | collective-permute-start | bytes 393224 | tf_op jit(solution)/shard_map/ppermute | solution.py:243
  12.1 0.8 %collective-permute-done.3.refs_5_ = f32[128,256]{1,0:T(8,128)S(1)} collective-permute-done((f32[128,256]{1,0:T(8,128)S(1)}, f32[128,256]{1,0:T(8,128)S(1)}, u32[]{:S(2)}, u32[]{:S(2)}) %collective-permute-start.3) | collective-permute-done | bytes 131104 | tf_op jit(solution)/shard_map/ppermute | solution.py:243
  12.9 0.2 collective-permute-done.1.refs_3_
  13.1 2.4 %shard_map.79 = (f32[128,256]{1,0:T(8,128)S(1)}, f32[128,256]{1,0:T(8,128)S(1)}) custom-call(s32[8,8,128]{2,1,0:T(8,128)S(1)} %get-tuple-element.20.shift_ref, f32[128,256]{1,0:T(8,128)S(1)} %get-tuple-element.19.field_ref.refs_0_.refs_3_, f32[128,256]{1,0:T(8,128)S(1)} %get-tuple-element.21.refs_1_.field_other_ref.refs_4_, ...), custom_call_target="tpu_custom_call" | custom-call | flops 1610612736 | bytes 2097152 | tf_op jit(solution)/shard_map/pallas_call | solution.py:22
  15.5 0.4 collective-permute-start.4
  15.9 1.0 %collective-permute-done.4 = f32[128,256]{1,0:T(8,128)S(1)} collective-permute-done((f32[128,256]{1,0:T(8,128)S(1)}, f32[128,256]{1,0:T(8,128)S(1)}, u32[]{:S(2)}, u32[]{:S(2)}) %collective-permute-start.4) | collective-permute-done | bytes 131104 | tf_op jit(solution)/shard_map/ppermute | solution.py:243
  16.9 1.6 %collective-permute-start.5 = (f32[128,256]{1,0:T(8,128)S(1)}, f32[128,256]{1,0:T(8,128)S(1)}, u32[]{:S(2)}, u32[]{:S(2)}) collective-permute-start(f32[128,256]{1,0:T(8,128)S(1)} %add.9), channel_id=1, source_target_pairs={{0,2},{1,3},{2,0},{3,1},{4,6},{5,7},{6,4},{7,5},{8,10},{9,11},{10,... | collective-permute-start | bytes 393224 | tf_op jit(solution)/shard_map/ppermute | solution.py:253
  18.5 4.2 %collective-permute-done.5 = f32[128,256]{1,0:T(8,128)S(1)} collective-permute-done((f32[128,256]{1,0:T(8,128)S(1)}, f32[128,256]{1,0:T(8,128)S(1)}, u32[]{:S(2)}, u32[]{:S(2)}) %collective-permute-start.5) | collective-permute-done | bytes 131104 | tf_op jit(solution)/shard_map/ppermute | solution.py:253
  22.8 0.1 collective-permute-start.6
  22.8 1.6 %collective-permute-start.11 = (f32[128,256]{1,0:T(8,128)S(1)}, f32[128,256]{1,0:T(8,128)S(1)}, u32[]{:S(2)}, u32[]{:S(2)}) collective-permute-start(f32[128,256]{1,0:T(8,128)S(1)} %add_multiply_fusion.first_ref.refs_0_.refs_1_.refs_4_), channel_id=1, source_target_pairs={{0,2},{28,30},{4,8},{8,4},{12,16},{16,12},{20,24},{24,20},{1,3},{2... | collective-permute-start | bytes 393224 | tf_op jit(solution)/shard_map/ppermute | solution.py:246
  24.4 2.5 %collective-permute-start.7 = (f32[128,256]{1,0:T(8,128)S(1)}, f32[128,256]{1,0:T(8,128)S(1)}, u32[]{:S(2)}, u32[]{:S(2)}) collective-permute-start(f32[128,256]{1,0:T(8,128)S(1)} %add_multiply_fusion.first_ref.refs_0_.refs_1_.refs_4_), channel_id=1, source_target_pairs={{0,4},{4,0},{8,12},{12,8},{16,20},{20,16},{24,28},{28,24},{1,5},{5... | collective-permute-start | bytes 393224 | tf_op jit(solution)/shard_map/ppermute | solution.py:246
  26.9 0.0 collective-permute-done.6.first_other_ref.refs_1_.refs_2_
  26.9 0.3 shard_map.80.refs_0_
  27.2 1.9 %collective-permute-start.9 = (f32[8,256]{1,0:T(8,128)S(1)}, f32[8,256]{1,0:T(8,128)S(1)}, u32[]{:S(2)}, u32[]{:S(2)}) collective-permute-start(f32[8,256]{1,0:T(8,128)S(1)} %shard_map.80.refs_0_), channel_id=1, source_target_pairs={{0,24},{1,9},{2,26},{3,11},{4,28},{5,13},{6,30},{7,15},{8,16},{9,1... | collective-permute-start | bytes 24584 | tf_op jit(solution)/shard_map/ppermute | solution.py:285
  29.1 1.2 %collective-permute-start.8 = (f32[8,256]{1,0:T(8,128)S(1)}, f32[8,256]{1,0:T(8,128)S(1)}, u32[]{:S(2)}, u32[]{:S(2)}) collective-permute-start(f32[8,256]{1,0:T(8,128)S(1)} %shard_map.80.refs_0_), channel_id=1, source_target_pairs={{0,8},{1,17},{2,10},{3,19},{4,12},{5,21},{6,14},{7,23},{8,0},{9,25... | collective-permute-start | bytes 24584 | tf_op jit(solution)/shard_map/ppermute | solution.py:285
  30.3 0.0 collective-permute-done.11.refs_4_
  30.3 0.0 collective-permute-start.12
  30.3 2.6 %collective-permute-done.9.refs_2_ = f32[8,256]{1,0:T(8,128)S(1)} collective-permute-done((f32[8,256]{1,0:T(8,128)S(1)}, f32[8,256]{1,0:T(8,128)S(1)}, u32[]{:S(2)}, u32[]{:S(2)}) %collective-permute-start.9) | collective-permute-done | bytes 8224 | tf_op jit(solution)/shard_map/ppermute | solution.py:285
  33.0 0.0 collective-permute-done.8.refs_1_
  33.0 0.0 collective-permute-done.7.refs_2_
  33.0 0.1 collective-permute-start.10
  33.1 0.0 collective-permute-done.12.refs_5_
  33.1 1.3 %collective-permute-done.10.refs_3_ = f32[128,256]{1,0:T(8,128)S(1)} collective-permute-done((f32[128,256]{1,0:T(8,128)S(1)}, f32[128,256]{1,0:T(8,128)S(1)}, u32[]{:S(2)}, u32[]{:S(2)}) %collective-permute-start.10) | collective-permute-done | bytes 131104 | tf_op jit(solution)/shard_map/ppermute | solution.py:243
  34.4 2.4 %shard_map.82 = (f32[136,256]{1,0:T(8,128)S(1)}, f32[136,256]{1,0:T(8,128)S(1)}) custom-call(s32[8,8,128]{2,1,0:T(8,128)S(1)} %get-tuple-element.20.shift_ref, f32[128,256]{1,0:T(8,128)S(1)} %add_multiply_fusion.first_ref.refs_0_.refs_1_.refs_4_, f32[128,256]{1,0:T(8,128)S(1)} %collective-permute-done.6.first_other_ref.refs_1_.refs_2_, ...), custom_call_target="tpu_custom_call" | custom-call | flops 1610612736 | bytes 2097152 | tf_op jit(solution)/shard_map/pallas_call | solution.py:22
  36.8 0.2 collective-permute-start.13
  37.0 1.2 %collective-permute-done.13.got_ref = f32[136,256]{1,0:T(8,128)S(1)} collective-permute-done((f32[136,256]{1,0:T(8,128)S(1)}, f32[136,256]{1,0:T(8,128)S(1)}, u32[]{:S(2)}, u32[]{:S(2)}) %collective-permute-start.13) | collective-permute-done | bytes 139296 | tf_op jit(solution)/shard_map/ppermute | solution.py:243
  38.2 1.6 %collective-permute-start.15 = (f32[128,256]{1,0:T(8,128)S(1)}, f32[128,256]{1,0:T(8,128)S(1)}, u32[]{:S(2)}, u32[]{:S(2)}) collective-permute-start(f32[128,256]{1,0:T(8,128)S(1)} %get-tuple-element.35.refs_1_), channel_id=1, source_target_pairs={{0,2},{1,3},{2,0},{3,1},{4,6},{5,7},{6,4},{7,5},{8,10},{9,11},{10,... | collective-permute-start | bytes 393224 | tf_op jit(solution)/shard_map/ppermute | solution.py:253
  39.8 1.8 %collective-permute-start.14 = (f32[8,256]{1,0:T(8,128)S(1)}, f32[8,256]{1,0:T(8,128)S(1)}, u32[]{:S(2)}, u32[]{:S(2)}) collective-permute-start(f32[8,256]{1,0:T(8,128)S(1)} %get-tuple-element.34), channel_id=1, source_target_pairs={{0,4},{4,0},{8,12},{12,8},{16,20},{20,16},{24,28},{28,24},{1,5},{5... | collective-permute-start | bytes 24584 | tf_op jit(solution)/shard_map/ppermute | solution.py:299
  41.7 1.8 %collective-permute-done.14 = f32[8,256]{1,0:T(8,128)S(1)} collective-permute-done((f32[8,256]{1,0:T(8,128)S(1)}, f32[8,256]{1,0:T(8,128)S(1)}, u32[]{:S(2)}, u32[]{:S(2)}) %collective-permute-start.14) | collective-permute-done | bytes 8224 | tf_op jit(solution)/shard_map/ppermute | solution.py:299
  43.5 0.4 collective-permute-done.15.refs_2_
  43.8 0.3 shard_map.85.mine_ref
  44.1 0.1 collective-permute-start.16
  44.2 1.0 %shard_map.84 = f32[1,256,256]{2,1,0:T(8,128)} custom-call(f32[8,256]{1,0:T(8,128)S(1)} %add.11.refs_0_, f32[128,256]{1,0:T(8,128)S(1)} %add_multiply_fusion.first_ref.refs_0_.refs_1_.refs_4_, f32[128,256]{1,0:T(8,128)S(1)} %collective-permute-done.6.first_other_ref.refs_1_.refs_2_, f32[128,256]{1,0:T(8,128)S(1)} %get-tuple-element.19.field_ref.refs_0_.refs_3_, ...), custom_call_target="tpu_custom_call" | custom-call | tf_op jit(solution)/shard_map/pallas_call | solution.py:22
  45.2 0.3 collective-permute-done.16.other_ref
  45.5 0.7 %shard_map.86 = f32[1,256,256]{2,1,0:T(8,128)} custom-call(f32[128,256]{1,0:T(8,128)S(1)} %shard_map.85.mine_ref, f32[128,256]{1,0:T(8,128)S(1)} %collective-permute-done.16.other_ref), custom_call_target="tpu_custom_call" | custom-call | tf_op jit(solution)/shard_map/pallas_call | solution.py:22
  (5 shorter events, 0.1 us)
Async XLA Ops:
  3.0 8.6 %collective-permute-start = (f32[128,256]{1,0:T(8,128)S(1)}, f32[128,256]{1,0:T(8,128)S(1)}, u32[]{:S(2)}, u32[]{:S(2)}) collective-permute-start(f32[128,256]{1,0:T(8,128)S(1)} %get-tuple-element.19.field_ref.refs_0_.refs_3_), channel_id=1, source_target_pairs={{0,4},{4,0},{8,12},{12,8},{16,20},{20,16},{24,28},{28,24},{1,5},{5... | collective-permute-start | bytes 393224 | tf_op jit(solution)/shard_map/ppermute | solution.py:246
  6.0 5.6 %collective-permute-start.2 = (f32[128,256]{1,0:T(8,128)S(1)}, f32[128,256]{1,0:T(8,128)S(1)}, u32[]{:S(2)}, u32[]{:S(2)}) collective-permute-start(f32[128,256]{1,0:T(8,128)S(1)} %get-tuple-element.19.field_ref.refs_0_.refs_3_), channel_id=1, source_target_pairs={{0,2},{28,30},{4,8},{8,4},{12,16},{16,12},{20,24},{24,20},{1,3},{2... | collective-permute-start | bytes 393224 | tf_op jit(solution)/shard_map/ppermute | solution.py:246
  11.6 1.3 %collective-permute-start.3 = (f32[128,256]{1,0:T(8,128)S(1)}, f32[128,256]{1,0:T(8,128)S(1)}, u32[]{:S(2)}, u32[]{:S(2)}) collective-permute-start(f32[128,256]{1,0:T(8,128)S(1)} %collective-permute-done.2.refs_4_), channel_id=1, source_target_pairs={{0,1},{1,0},{2,3},{3,2},{4,5},{5,4},{6,7},{7,6},{8,9},{9,8},{10,11... | collective-permute-start | bytes 393224 | tf_op jit(solution)/shard_map/ppermute | solution.py:243
  11.6 1.5 %collective-permute-start.1 = (f32[128,256]{1,0:T(8,128)S(1)}, f32[128,256]{1,0:T(8,128)S(1)}, u32[]{:S(2)}, u32[]{:S(2)}) collective-permute-start(f32[128,256]{1,0:T(8,128)S(1)} %collective-permute-done.refs_2_), channel_id=1, source_target_pairs={{0,1},{1,0},{2,3},{3,2},{4,5},{5,4},{6,7},{7,6},{8,9},{9,8},{10,11... | collective-permute-start | bytes 393224 | tf_op jit(solution)/shard_map/ppermute | solution.py:243
  15.5 1.4 %collective-permute-start.4 = (f32[128,256]{1,0:T(8,128)S(1)}, f32[128,256]{1,0:T(8,128)S(1)}, u32[]{:S(2)}, u32[]{:S(2)}) collective-permute-start(f32[128,256]{1,0:T(8,128)S(1)} %get-tuple-element.28), channel_id=1, source_target_pairs={{0,1},{1,0},{2,3},{3,2},{4,5},{5,4},{6,7},{7,6},{8,9},{9,8},{10,11... | collective-permute-start | bytes 393224 | tf_op jit(solution)/shard_map/ppermute | solution.py:243
  16.9 5.8 %collective-permute-start.5 = (f32[128,256]{1,0:T(8,128)S(1)}, f32[128,256]{1,0:T(8,128)S(1)}, u32[]{:S(2)}, u32[]{:S(2)}) collective-permute-start(f32[128,256]{1,0:T(8,128)S(1)} %add.9), channel_id=1, source_target_pairs={{0,2},{1,3},{2,0},{3,1},{4,6},{5,7},{6,4},{7,5},{8,10},{9,11},{10,... | collective-permute-start | bytes 393224 | tf_op jit(solution)/shard_map/ppermute | solution.py:253
  22.8 4.2 %collective-permute-start.6 = (f32[128,256]{1,0:T(8,128)S(1)}, f32[128,256]{1,0:T(8,128)S(1)}, u32[]{:S(2)}, u32[]{:S(2)}) collective-permute-start(f32[128,256]{1,0:T(8,128)S(1)} %add_multiply_fusion.first_ref.refs_0_.refs_1_.refs_4_), channel_id=1, source_target_pairs={{0,1},{1,0},{2,3},{3,2},{4,5},{5,4},{6,7},{7,6},{8,9},{9,8},{10,11... | collective-permute-start | bytes 393224 | tf_op jit(solution)/shard_map/ppermute | solution.py:243
  22.8 7.5 %collective-permute-start.11 = (f32[128,256]{1,0:T(8,128)S(1)}, f32[128,256]{1,0:T(8,128)S(1)}, u32[]{:S(2)}, u32[]{:S(2)}) collective-permute-start(f32[128,256]{1,0:T(8,128)S(1)} %add_multiply_fusion.first_ref.refs_0_.refs_1_.refs_4_), channel_id=1, source_target_pairs={{0,2},{28,30},{4,8},{8,4},{12,16},{16,12},{20,24},{24,20},{1,3},{2... | collective-permute-start | bytes 393224 | tf_op jit(solution)/shard_map/ppermute | solution.py:246
  24.4 8.6 %collective-permute-start.7 = (f32[128,256]{1,0:T(8,128)S(1)}, f32[128,256]{1,0:T(8,128)S(1)}, u32[]{:S(2)}, u32[]{:S(2)}) collective-permute-start(f32[128,256]{1,0:T(8,128)S(1)} %add_multiply_fusion.first_ref.refs_0_.refs_1_.refs_4_), channel_id=1, source_target_pairs={{0,4},{4,0},{8,12},{12,8},{16,20},{20,16},{24,28},{28,24},{1,5},{5... | collective-permute-start | bytes 393224 | tf_op jit(solution)/shard_map/ppermute | solution.py:246
  27.2 5.8 %collective-permute-start.9 = (f32[8,256]{1,0:T(8,128)S(1)}, f32[8,256]{1,0:T(8,128)S(1)}, u32[]{:S(2)}, u32[]{:S(2)}) collective-permute-start(f32[8,256]{1,0:T(8,128)S(1)} %shard_map.80.refs_0_), channel_id=1, source_target_pairs={{0,24},{1,9},{2,26},{3,11},{4,28},{5,13},{6,30},{7,15},{8,16},{9,1... | collective-permute-start | bytes 24584 | tf_op jit(solution)/shard_map/ppermute | solution.py:285
  29.1 3.9 %collective-permute-start.8 = (f32[8,256]{1,0:T(8,128)S(1)}, f32[8,256]{1,0:T(8,128)S(1)}, u32[]{:S(2)}, u32[]{:S(2)}) collective-permute-start(f32[8,256]{1,0:T(8,128)S(1)} %shard_map.80.refs_0_), channel_id=1, source_target_pairs={{0,8},{1,17},{2,10},{3,19},{4,12},{5,21},{6,14},{7,23},{8,0},{9,25... | collective-permute-start | bytes 24584 | tf_op jit(solution)/shard_map/ppermute | solution.py:285
  30.3 2.7 %collective-permute-start.12 = (f32[128,256]{1,0:T(8,128)S(1)}, f32[128,256]{1,0:T(8,128)S(1)}, u32[]{:S(2)}, u32[]{:S(2)}) collective-permute-start(f32[128,256]{1,0:T(8,128)S(1)} %collective-permute-done.11.refs_4_), channel_id=1, source_target_pairs={{0,1},{1,0},{2,3},{3,2},{4,5},{5,4},{6,7},{7,6},{8,9},{9,8},{10,11... | collective-permute-start | bytes 393224 | tf_op jit(solution)/shard_map/ppermute | solution.py:243
  33.0 1.4 %collective-permute-start.10 = (f32[128,256]{1,0:T(8,128)S(1)}, f32[128,256]{1,0:T(8,128)S(1)}, u32[]{:S(2)}, u32[]{:S(2)}) collective-permute-start(f32[128,256]{1,0:T(8,128)S(1)} %collective-permute-done.7.refs_2_), channel_id=1, source_target_pairs={{0,1},{1,0},{2,3},{3,2},{4,5},{5,4},{6,7},{7,6},{8,9},{9,8},{10,11... | collective-permute-start | bytes 393224 | tf_op jit(solution)/shard_map/ppermute | solution.py:243
  36.8 1.4 %collective-permute-start.13 = (f32[136,256]{1,0:T(8,128)S(1)}, f32[136,256]{1,0:T(8,128)S(1)}, u32[]{:S(2)}, u32[]{:S(2)}) collective-permute-start(f32[136,256]{1,0:T(8,128)S(1)} %get-tuple-element.33), channel_id=1, source_target_pairs={{0,1},{1,0},{2,3},{3,2},{4,5},{5,4},{6,7},{7,6},{8,9},{9,8},{10,11... | collective-permute-start | bytes 417800 | tf_op jit(solution)/shard_map/ppermute | solution.py:243
  38.2 5.6 %collective-permute-start.15 = (f32[128,256]{1,0:T(8,128)S(1)}, f32[128,256]{1,0:T(8,128)S(1)}, u32[]{:S(2)}, u32[]{:S(2)}) collective-permute-start(f32[128,256]{1,0:T(8,128)S(1)} %get-tuple-element.35.refs_1_), channel_id=1, source_target_pairs={{0,2},{1,3},{2,0},{3,1},{4,6},{5,7},{6,4},{7,5},{8,10},{9,11},{10,... | collective-permute-start | bytes 393224 | tf_op jit(solution)/shard_map/ppermute | solution.py:253
  39.8 3.7 %collective-permute-start.14 = (f32[8,256]{1,0:T(8,128)S(1)}, f32[8,256]{1,0:T(8,128)S(1)}, u32[]{:S(2)}, u32[]{:S(2)}) collective-permute-start(f32[8,256]{1,0:T(8,128)S(1)} %get-tuple-element.34), channel_id=1, source_target_pairs={{0,4},{4,0},{8,12},{12,8},{16,20},{20,16},{24,28},{28,24},{1,5},{5... | collective-permute-start | bytes 24584 | tf_op jit(solution)/shard_map/ppermute | solution.py:299
  44.1 1.4 %collective-permute-start.16 = (f32[128,256]{1,0:T(8,128)S(1)}, f32[128,256]{1,0:T(8,128)S(1)}, u32[]{:S(2)}, u32[]{:S(2)}) collective-permute-start(f32[128,256]{1,0:T(8,128)S(1)} %shard_map.85.mine_ref), channel_id=1, source_target_pairs={{0,1},{1,0},{2,3},{3,2},{4,5},{5,4},{6,7},{7,6},{8,9},{9,8},{10,11... | collective-permute-start | bytes 393224 | tf_op jit(solution)/shard_map/ppermute | solution.py:243

commit v4 on v3

--- a/solution.py
+++ b/solution.py
@@ -53,12 +53,15 @@
     return jnp.sum(jnp.sum(x, axis=0, keepdims=True), axis=1, keepdims=True)
 
 
-def field_kernel(state_ref, live_ref, mine_ref, other_ref, mask_ref, state, live, sems):
+def inside(shape, first_row, rows, cols):
+    row = lax.broadcasted_iota(jnp.int32, shape, 0) + first_row
+    return (row < rows) & (lax.broadcasted_iota(jnp.int32, shape, 1) < cols)
+
+
+def field_kernel(state_ref, live_ref, field_ref, other_ref, mask_ref, live_out, state, live, sems):
     copies = [
         pltpu.make_async_copy(ref, buffer, sems.at[i])
-        for i, (ref, buffer) in enumerate(
-            ((state_ref, state), (live_ref, live))
-        )
+        for i, (ref, buffer) in enumerate(((state_ref, state), (live_ref, live)))
     ]
     for copy in copies:
         copy.start()
@@ -67,12 +70,12 @@
     half = mask_ref.shape[0]
     core = core_index()
     rows, cols = live[0], live[1]
-    row = lax.broadcasted_iota(jnp.int32, mask_ref.shape, 0)
-    lane = lax.broadcasted_iota(jnp.int32, mask_ref.shape, 1)
-    for which, ref in ((core, mine_ref), (1 - core, other_ref)):
-        inside = (row + which * half < rows) & (lane < cols)
-        ref[...] = jnp.where(inside, state[0, rows_of(which, half)], 0.0)
-    mask_ref[...] = jnp.where((row + core * half < rows) & (lane < cols), 1.0, 0.0)
+    for which, ref in ((core, field_ref), (1 - core, other_ref)):
+        start = which * half
+        ref[...] = jnp.where(inside(ref.shape, start, rows, cols), state[0, rows_of(which, half)], 0.0)
+    mask_ref[...] = jnp.where(inside(mask_ref.shape, core * half, rows, cols), 1.0, 0.0)
+    row = lax.broadcasted_iota(jnp.int32, live_out.shape, 0)
+    live_out[...] = jnp.where(row == 0, rows, cols)
 
 
 def load_kernel(left_ref, right_ref, shift_ref, field_ref, left_out, right_out, shift_out, shift, sems):
@@ -105,18 +108,28 @@
     )
 
 
-def product_kernel(shift_ref, *refs):
-    halves, (left_ref, right_ref) = refs[:6], refs[6:8]
-    tile_ref = refs[8] if len(refs) == 14 else None
+def product_kernel(raw, tiled, shift_ref, *refs):
+    left_ref, right_ref, own_refs, refs = *refs[:2], refs[2:4], refs[4:]
     send_ref, keep_ref, high, low, total = refs[-5:]
     block = total.shape[0]
     half = block // 2
     core, sector = core_index(), lax.axis_index("sec")
     slot = jnp.where(lax.rem(sector, 2) == 0, 2, 0)
-    for index, mine_ref, other_ref in zip((1, slot, 2 - slot), halves[::2], halves[1::2]):
-        for which, ref in ((core, mine_ref), (1 - core, other_ref)):
+
+    def put(index, pair_of_refs):
+        for which, ref in zip((core, 1 - core), pair_of_refs):
             rows = rows_of(which, half)
             high[index, rows], low[index, rows] = split(ref[...])
+
+    put(1, own_refs)
+    if raw:
+        got = jnp.where(core == 0, slot, 2 - slot)
+        for index, ref, live_ref in zip((got, 2 - got), refs[:2], refs[2:4]):
+            live = inside((block, block), 0, live_ref[:1, :1], live_ref[1:2, :1])
+            high[index], low[index] = split(jnp.where(live, ref[...], 0.0))
+    else:
+        put(slot, refs[:2])
+        put(2 - slot, refs[2:4])
 
     @pl.when(sector == 0)
     def _():
@@ -143,20 +156,19 @@
     total[...] = out
     send_ref[pl.ds(0, half)] = total[rows_of(1 - core, half)]
     keep_ref[pl.ds(0, half)] = total[rows_of(core, half)]
-    if tile_ref is not None:
-        send_ref[pl.ds(half, EXTRA)] = tile_ref[...]
-        keep_ref[pl.ds(half, EXTRA)] = tile_ref[...]
-
-
-def product(shift, halves, left, right, tile=None):
+    if tiled:
+        send_ref[pl.ds(half, EXTRA)] = refs[4][...]
+        keep_ref[pl.ds(half, EXTRA)] = refs[4][...]
+
+
+def product(shift, left, right, *arrays, raw=False, tiled=False):
     terms, _, block, _ = left.shape
-    rows = block // 2 + (0 if tile is None else EXTRA)
-    arrays = [*halves, left, right] + ([] if tile is None else [tile])
+    arrays = [shift, left, right, *arrays]
     return call(
-        product_kernel,
-        [f32(rows, block)] * 2,
-        [VMEM] * (1 + len(arrays)),
-        shift, *arrays,
+        lambda *refs: product_kernel(raw, tiled, *refs),
+        [f32(block // 2 + (EXTRA if tiled else 0), block)] * 2,
+        [VMEM] * len(arrays),
+        *arrays,
         mib=16,
         scratch_shapes=[
             pltpu.VMEM((3, block, block), jnp.bfloat16),
@@ -197,24 +209,27 @@
     sums_ref[...] = keep_ref[pl.ds(half, EXTRA)] + got_ref[pl.ds(half, EXTRA)]
 
 
-def merged(sums, cells):
+def merged_kernel(cells, sums_ref, got_ref, out_ref):
+    sums = sums_ref[...] + got_ref[...]
     crosses, squares, energies = (sums[i : i + 1] for i in range(3))
     theta = jnp.sum(crosses, axis=1, keepdims=True) / jnp.sum(squares, axis=1, keepdims=True)
     thetas = jnp.where(squares > 0, crosses / jnp.where(squares > 0, squares, 1.0), 0.0)
     energy = jnp.sum(energies + (thetas - theta) ** 2 * squares, axis=1, keepdims=True)
-    return theta, lax.rsqrt(energy / cells + 1e-06)
-
-
-def image_kernel(cells, sums_ref, total_ref, peer_ref, mask_ref, first_ref, out_ref):
-    theta, scale = merged(sums_ref[...], cells)
+    scale = lax.rsqrt(energy / cells + 1e-06)
+    row = lax.broadcasted_iota(jnp.int32, out_ref.shape, 0)
+    out_ref[...] = jnp.where(row == 0, theta, scale)
+
+
+def image_kernel(merged_ref, total_ref, peer_ref, mask_ref, first_ref, out_ref):
+    theta, scale = merged_ref[0:1, :], merged_ref[1:2, :]
     total = (total_ref[...] + peer_ref[...]) * mask_ref[...]
     out_ref[...] = scale * (total - theta * first_ref[...])
 
 
-def correction_kernel(cells, sums_ref, first_ref, first_other_ref, field_ref, field_other_ref, out_ref):
+def correction_kernel(merged_ref, first_ref, first_other_ref, field_ref, field_other_ref, out_ref):
     half = first_ref.shape[0]
     core = core_index()
-    theta, scale = merged(sums_ref[...], cells)
+    theta, scale = merged_ref[0:1, :], merged_ref[1:2, :]
     out_ref[0, rows_of(core, half)] = scale * (first_ref[...] - theta * field_ref[...])
     out_ref[0, rows_of(1 - core, half)] = scale * (first_other_ref[...] - theta * field_other_ref[...])
 
@@ -252,9 +267,12 @@
             step *= 2
         return total, lax.ppermute(total, "op", [(i, i ^ step) for i in range(ops)])
 
-    field, field_other, mask = call(
+    crossing = [(s * ops + a, (s ^ 1) * ops + a) for s in range(sectors) for a in range(0, ops, 2)]
+    crossing += [(source, target) for source, target in between if source % 2]
+    got = lax.ppermute(state[0], ("sec", "op"), crossing)
+    field, field_other, mask, live = call(
         field_kernel,
-        [f32(half, block)] * 3,
+        [f32(half, block)] * 3 + [jax.ShapeDtypeStruct((8, 128), jnp.int32)],
         [HBM] * 2,
         in_hbm(state), jnp.concatenate([sector_rows, sector_cols]),
         scratch_shapes=[
@@ -263,11 +281,12 @@
             pltpu.SemaphoreType.DMA((2,)),
         ],
     )
-    far, near = neighbours(field)
+    live = lax.ppermute(live, ("sec", "op"), crossing)
     left, right, shift = load(left_ops, right_ops, term_shift, field)
-    near, left, right = lax.optimization_barrier((near, left, right))
-    halves = [field, field_other, near, swapped(near), far, swapped(far)]
-    send, keep = product(shift, halves, left, right)
+    got, left, right, live = lax.optimization_barrier((got, left, right, live))
+    send, keep = product(
+        shift, left, right, field, field_other, got, swapped(got), live, swapped(live), raw=True
+    )
     total, peer = over_chips(keep + swapped(send))
 
     first = (total + peer) * mask
@@ -290,26 +309,27 @@
         tile, *tiles,
     )
     near, tile = lax.optimization_barrier((near, tile))
-    halves = [first, first_other, near, swapped(near), far, swapped(far)]
-    send, keep = product(shift, halves, left, right, tile)
+    send, keep = product(
+        shift, left, right, first, first_other, near, swapped(near), far, swapped(far), tile, tiled=True
+    )
     total, sums = call(
         summed_kernel, [f32(half, block), f32(EXTRA, block)], [VMEM] * 2, keep, swapped(send)
     )
     total, peer = over_chips(total)
-    sums = sums + lax.ppermute(sums, "sec", pairs)
 
     cells = sectors * block * block
-    image = call(
-        lambda *refs: image_kernel(cells, *refs),
-        f32(half, block),
-        [VMEM] * 5,
-        sums, total, peer, mask, first,
-    )
+    merged = call(
+        lambda *refs: merged_kernel(cells, *refs),
+        f32(EXTRA, block),
+        [VMEM] * 2,
+        sums, lax.ppermute(sums, "sec", pairs),
+    )
+    image = call(image_kernel, f32(half, block), [VMEM] * 5, merged, total, peer, mask, first)
     correction = call(
-        lambda *refs: correction_kernel(cells, *refs),
+        correction_kernel,
         f32(1, block, block),
         [VMEM] * 5,
-        sums, first, first_other, field, field_other,
+        merged, first, first_other, field, field_other,
     )
     image = call(output_kernel, f32(1, block, block), [VMEM] * 2, image, swapped(image))
     return correction, image

time: 46.4 us -> 44.9 us (0.968)
  starting transfers between devices: 18.1 us -> 16.4 us
    ppermute x1 -> x3, starting transfers between devices: 1.85 us -> 4.92 us  [the longest x1 3 us: local(): got = lax.ppermute(state[0], ('sec', 'op'), crossing)]
    ppermute x2 -> x1, starting transfers between devices: 5.5 us -> 2.43 us  [neighbours(): lax.ppermute(mine, 'sec', pairs)]
    ppermute x1 -> x3, waiting for transfers between devices: 1.81 us -> 3.79 us  [the longest x1 1.98 us: local(): live = lax.ppermute(live, ('sec', 'op'), crossing)]
    ppermute x2 -> x1, waiting for transfers between devices: 1.7 us -> 0.01 us  [neighbours(): lax.ppermute(mine, 'sec', pairs)]
    ppermute x2 -> x1, starting transfers between devices: 3.1 us -> 1.58 us  [neighbours(): lax.ppermute(mine, ('sec', 'op'), between)]
    pallas_call x10 -> x11, Pallas kernels: 10.4 us -> 10.3 us  [call(): pl.pallas_call(kernel, out_shape=out_shape, in_specs=in_specs, out_specs=...]
  transfers between devices with their start and end apart: 17 -> 17, of which waited for: 11 -> 10; matrix products, arithmetic and copies ran while one was open for 0% -> 0% of each run, Pallas kernels for 8% -> 10%
where the time goes in v4:
time: 44.9 us; the launch traced here: 44.8 us
  starting transfers between devices  16.4 us (37%)
  waiting for transfers between devices  16 us (36%)
  Pallas kernels  10.3 us (23%)
  between operations  2.01 us (4%)
    pallas_call x11, Pallas kernels, call(): pl.pallas_call(kernel, out_shape=out_shape, in_specs=in_specs, out_specs=...  10.3 us
    ppermute x8, waiting for transfers between devices, swapped(): return lax.ppermute(v, 'op', others)  5.38 us
    ppermute x2, waiting for transfers between devices, over_chips(): lax.ppermute(total, 'op', [(i, i ^ step) for i in range(ops)])  4.15 us
    ppermute x2, starting transfers between devices, over_chips(): lax.ppermute(total, 'op', [(i, i ^ step) for i in range(ops)])  3.17 us
    ppermute x2, starting transfers between devices, local(): tiles.append(lax.ppermute(tile, ('sec', 'op'), swaps))  3.16 us
    ppermute x1, starting transfers between devices, local(): got = lax.ppermute(state[0], ('sec', 'op'), crossing)  3 us
    ppermute x2, waiting for transfers between devices, local(): tiles.append(lax.ppermute(tile, ('sec', 'op'), swaps))  2.64 us
    ppermute x1, starting transfers between devices, neighbours(): lax.ppermute(mine, 'sec', pairs)  2.43 us
  transfers between devices with their start and end apart: 17, of which 10 were waited for; matrix products, arithmetic and copies ran while one was open for 0% of the time, Pallas kernels for 10%

profile of v4, /device:TPU:0, one launch (start us, length us, event | category | flops | bytes accessed | tf_op | source)
XLA Modules:
  0.0 44.8 jit_solution(3459944244058228250)
XLA Ops:
  0.6 3.0 %collective-permute-start = (f32[256,256]{1,0:T(8,128)}, f32[256,256]{1,0:T(8,128)S(1)}, u32[]{:S(2)}, u32[]{:S(2)}) collective-permute-start(f32[256,256]{1,0:T(8,128)} %bitcast.1), channel_id=1, source_target_pairs={{0,4},{2,6},{4,0},{6,2},{8,12},{10,14},{12,8},{14,10},{16,20},{18,... | collective-permute-start | bytes 786440 | tf_op jit(solution)/shard_map/ppermute | solution.py:272
  4.9 0.1 pad_add_fusion.live_ref
  5.0 1.0 %shard_map.77 = (f32[128,256]{1,0:T(8,128)S(1)}, f32[128,256]{1,0:T(8,128)S(1)}, f32[128,256]{1,0:T(8,128)S(1)}, s32[8,128]{1,0:T(8,128)S(1)}) custom-call(f32[1,256,256]{2,1,0:T(8,128)} %state_ref.1, s32[2]{0:T(128)S(1)} %pad_add_fusion.live_ref), custom_call_target="tpu_custom_call" | custom-call | tf_op jit(solution)/shard_map/pallas_call | solution.py:22
  6.0 0.1 collective-permute-start.1
  6.1 2.4 %shard_map.78 = (f32[8,1,256,256]{3,2,1,0:T(8,128)S(1)}, f32[8,1,256,256]{3,2,1,0:T(8,128)S(1)}, s32[8,8,128]{2,1,0:T(8,128)S(1)}) custom-call(f32[8,1,256,256]{3,2,1,0:T(8,128)} %left_ref.1, f32[8,1,256,256]{3,2,1,0:T(8,128)} %right_ref.1, s32[8]{0:T(128)} %shift_ref.1, f32[128,256]{1,0:T(8,128)S(1)} %get-tuple-element.21.field_ref.refs_3_), custom_call_target="tpu_custom_call" | custom-call | bytes 4194304 | tf_op jit(solution)/shard_map/pallas_call | solution.py:22
  8.5 2.0 %collective-permute-done.1.refs_7_ = s32[8,128]{1,0:T(8,128)S(1)} collective-permute-done((s32[8,128]{1,0:T(8,128)S(1)}, s32[8,128]{1,0:T(8,128)S(1)}, u32[]{:S(2)}, u32[]{:S(2)}) %collective-permute-start.1) | collective-permute-done | bytes 4128 | tf_op jit(solution)/shard_map/ppermute | solution.py:284
  10.5 0.0 collective-permute-done.refs_5_
  10.5 0.0 collective-permute-start.2
  10.5 0.5 %collective-permute-start.3 = (s32[8,128]{1,0:T(8,128)S(1)}, s32[8,128]{1,0:T(8,128)S(1)}, u32[]{:S(2)}, u32[]{:S(2)}) collective-permute-start(s32[8,128]{1,0:T(8,128)S(1)} %collective-permute-done.1.refs_7_), channel_id=1, source_target_pairs={{0,1},{1,0},{2,3},{3,2},{4,5},{5,4},{6,7},{7,6},{8,9},{9,8},{10,11... | collective-permute-start | bytes 12296 | tf_op jit(solution)/shard_map/ppermute | solution.py:258
  11.0 1.0 %collective-permute-done.3.refs_8_ = s32[8,128]{1,0:T(8,128)S(1)} collective-permute-done((s32[8,128]{1,0:T(8,128)S(1)}, s32[8,128]{1,0:T(8,128)S(1)}, u32[]{:S(2)}, u32[]{:S(2)}) %collective-permute-start.3) | collective-permute-done | bytes 4128 | tf_op jit(solution)/shard_map/ppermute | solution.py:258
  12.0 0.0 collective-permute-done.2.refs_6_
  12.0 2.5 %shard_map.79 = (f32[128,256]{1,0:T(8,128)S(1)}, f32[128,256]{1,0:T(8,128)S(1)}) custom-call(s32[8,8,128]{2,1,0:T(8,128)S(1)} %get-tuple-element.22.refs_0_, f32[8,1,256,256]{3,2,1,0:T(8,128)S(1)} %get-tuple-element.26.refs_1_, f32[8,1,256,256]{3,2,1,0:T(8,128)S(1)} %get-tuple-element.27.refs_2_, f32[128,256]{1,0:T(8,128)S(1)} %get-tuple-element.21.field_ref.refs_3_, ...), custom_call_target="tpu_custom_call" | custom-call | flops 1610612736 | bytes 2097152 | tf_op jit(solution)/shard_map/pallas_call | solution.py:22
  14.5 0.2 collective-permute-start.4
  14.7 1.2 %collective-permute-done.4 = f32[128,256]{1,0:T(8,128)S(1)} collective-permute-done((f32[128,256]{1,0:T(8,128)S(1)}, f32[128,256]{1,0:T(8,128)S(1)}, u32[]{:S(2)}, u32[]{:S(2)}) %collective-permute-start.4) | collective-permute-done | bytes 131104 | tf_op jit(solution)/shard_map/ppermute | solution.py:258
  15.9 1.6 %collective-permute-start.5 = (f32[128,256]{1,0:T(8,128)S(1)}, f32[128,256]{1,0:T(8,128)S(1)}, u32[]{:S(2)}, u32[]{:S(2)}) collective-permute-start(f32[128,256]{1,0:T(8,128)S(1)} %add.6), channel_id=1, source_target_pairs={{0,2},{1,3},{2,0},{3,1},{4,6},{5,7},{6,4},{7,5},{8,10},{9,11},{10,... | collective-permute-start | bytes 393224 | tf_op jit(solution)/shard_map/ppermute | solution.py:268
  17.5 4.0 %collective-permute-done.5 = f32[128,256]{1,0:T(8,128)S(1)} collective-permute-done((f32[128,256]{1,0:T(8,128)S(1)}, f32[128,256]{1,0:T(8,128)S(1)}, u32[]{:S(2)}, u32[]{:S(2)}) %collective-permute-start.5) | collective-permute-done | bytes 131104 | tf_op jit(solution)/shard_map/ppermute | solution.py:268
  21.6 0.1 collective-permute-start.6
  21.6 1.6 %collective-permute-start.11 = (f32[128,256]{1,0:T(8,128)S(1)}, f32[128,256]{1,0:T(8,128)S(1)}, u32[]{:S(2)}, u32[]{:S(2)}) collective-permute-start(f32[128,256]{1,0:T(8,128)S(1)} %add_multiply_fusion.first_ref.refs_3_), channel_id=1, source_target_pairs={{0,2},{28,30},{4,8},{8,4},{12,16},{16,12},{20,24},{24,20},{1,3},{2... | collective-permute-start | bytes 393224 | tf_op jit(solution)/shard_map/ppermute | solution.py:261
  23.2 2.4 %collective-permute-start.7 = (f32[128,256]{1,0:T(8,128)S(1)}, f32[128,256]{1,0:T(8,128)S(1)}, u32[]{:S(2)}, u32[]{:S(2)}) collective-permute-start(f32[128,256]{1,0:T(8,128)S(1)} %add_multiply_fusion.first_ref.refs_3_), channel_id=1, source_target_pairs={{0,4},{4,0},{8,12},{12,8},{16,20},{20,16},{24,28},{28,24},{1,5},{5... | collective-permute-start | bytes 393224 | tf_op jit(solution)/shard_map/ppermute | solution.py:261
  25.6 0.0 collective-permute-done.6.first_other_ref.refs_4_
  25.7 0.3 shard_map.80.refs_0_
  25.9 1.9 %collective-permute-start.9 = (f32[8,256]{1,0:T(8,128)S(1)}, f32[8,256]{1,0:T(8,128)S(1)}, u32[]{:S(2)}, u32[]{:S(2)}) collective-permute-start(f32[8,256]{1,0:T(8,128)S(1)} %shard_map.80.refs_0_), channel_id=1, source_target_pairs={{0,24},{1,9},{2,26},{3,11},{4,28},{5,13},{6,30},{7,15},{8,16},{9,1... | collective-permute-start | bytes 24584 | tf_op jit(solution)/shard_map/ppermute | solution.py:304
  27.9 1.2 %collective-permute-start.8 = (f32[8,256]{1,0:T(8,128)S(1)}, f32[8,256]{1,0:T(8,128)S(1)}, u32[]{:S(2)}, u32[]{:S(2)}) collective-permute-start(f32[8,256]{1,0:T(8,128)S(1)} %shard_map.80.refs_0_), channel_id=1, source_target_pairs={{0,8},{1,17},{2,10},{3,19},{4,12},{5,21},{6,14},{7,23},{8,0},{9,25... | collective-permute-start | bytes 24584 | tf_op jit(solution)/shard_map/ppermute | solution.py:304
  29.1 0.0 collective-permute-done.11.refs_7_
  29.1 0.0 collective-permute-start.12
  29.1 2.6 %collective-permute-done.9.refs_2_ = f32[8,256]{1,0:T(8,128)S(1)} collective-permute-done((f32[8,256]{1,0:T(8,128)S(1)}, f32[8,256]{1,0:T(8,128)S(1)}, u32[]{:S(2)}, u32[]{:S(2)}) %collective-permute-start.9) | collective-permute-done | bytes 8224 | tf_op jit(solution)/shard_map/ppermute | solution.py:304
  31.7 0.0 collective-permute-done.8.refs_1_
  31.7 0.0 collective-permute-done.7.refs_5_
  31.7 0.1 collective-permute-start.10
  31.8 0.0 collective-permute-done.12.refs_8_
  31.8 1.3 %collective-permute-done.10.refs_6_ = f32[128,256]{1,0:T(8,128)S(1)} collective-permute-done((f32[128,256]{1,0:T(8,128)S(1)}, f32[128,256]{1,0:T(8,128)S(1)}, u32[]{:S(2)}, u32[]{:S(2)}) %collective-permute-start.10) | collective-permute-done | bytes 131104 | tf_op jit(solution)/shard_map/ppermute | solution.py:258
  33.1 2.4 %shard_map.82 = (f32[136,256]{1,0:T(8,128)S(1)}, f32[136,256]{1,0:T(8,128)S(1)}) custom-call(s32[8,8,128]{2,1,0:T(8,128)S(1)} %get-tuple-element.22.refs_0_, f32[8,1,256,256]{3,2,1,0:T(8,128)S(1)} %get-tuple-element.26.refs_1_, f32[8,1,256,256]{3,2,1,0:T(8,128)S(1)} %get-tuple-element.27.refs_2_, f32[128,256]{1,0:T(8,128)S(1)} %add_multiply_fusion.first_ref.refs_3_, ...), custom_call_target="tpu_custom_call" | custom-call | flops 1610612736 | bytes 2097152 | tf_op jit(solution)/shard_map/pallas_call | solution.py:22
  35.5 0.2 collective-permute-start.13
  35.7 1.2 %collective-permute-done.13.got_ref = f32[136,256]{1,0:T(8,128)S(1)} collective-permute-done((f32[136,256]{1,0:T(8,128)S(1)}, f32[136,256]{1,0:T(8,128)S(1)}, u32[]{:S(2)}, u32[]{:S(2)}) %collective-permute-start.13) | collective-permute-done | bytes 139296 | tf_op jit(solution)/shard_map/ppermute | solution.py:258
  37.0 1.6 %collective-permute-start.15 = (f32[128,256]{1,0:T(8,128)S(1)}, f32[128,256]{1,0:T(8,128)S(1)}, u32[]{:S(2)}, u32[]{:S(2)}) collective-permute-start(f32[128,256]{1,0:T(8,128)S(1)} %get-tuple-element.39.total_ref), channel_id=1, source_target_pairs={{0,2},{1,3},{2,0},{3,1},{4,6},{5,7},{6,4},{7,5},{8,10},{9,11},{10,... | collective-permute-start | bytes 393224 | tf_op jit(solution)/shard_map/ppermute | solution.py:268
  38.5 1.8 %collective-permute-start.14 = (f32[8,256]{1,0:T(8,128)S(1)}, f32[8,256]{1,0:T(8,128)S(1)}, u32[]{:S(2)}, u32[]{:S(2)}) collective-permute-start(f32[8,256]{1,0:T(8,128)S(1)} %get-tuple-element.38.refs_0_), channel_id=1, source_target_pairs={{0,4},{4,0},{8,12},{12,8},{16,20},{20,16},{24,28},{28,24},{1,5},{5... | collective-permute-start | bytes 24584 | tf_op jit(solution)/shard_map/ppermute | solution.py:325
  40.4 1.8 %collective-permute-done.14.refs_1_ = f32[8,256]{1,0:T(8,128)S(1)} collective-permute-done((f32[8,256]{1,0:T(8,128)S(1)}, f32[8,256]{1,0:T(8,128)S(1)}, u32[]{:S(2)}, u32[]{:S(2)}) %collective-permute-start.14) | collective-permute-done | bytes 8224 | tf_op jit(solution)/shard_map/ppermute | solution.py:325
  42.2 0.3 shard_map.84.merged_ref
  42.4 0.1 collective-permute-done.15.peer_ref
  42.6 0.1 collective-permute-start.16
  42.7 0.7 %shard_map.85 = f32[1,256,256]{2,1,0:T(8,128)} custom-call(f32[8,256]{1,0:T(8,128)S(1)} %shard_map.84.merged_ref, f32[128,256]{1,0:T(8,128)S(1)} %add_multiply_fusion.first_ref.refs_3_, f32[128,256]{1,0:T(8,128)S(1)} %collective-permute-done.6.first_other_ref.refs_4_, f32[128,256]{1,0:T(8,128)S(1)} %get-tuple-element.21.field_ref.refs_3_, ...), custom_call_target="tpu_custom_call" | custom-call | tf_op jit(solution)/shard_map/pallas_call | solution.py:22
  43.4 0.6 %collective-permute-done.16.other_ref = f32[128,256]{1,0:T(8,128)S(1)} collective-permute-done((f32[128,256]{1,0:T(8,128)S(1)}, f32[128,256]{1,0:T(8,128)S(1)}, u32[]{:S(2)}, u32[]{:S(2)}) %collective-permute-start.16) | collective-permute-done | bytes 131104 | tf_op jit(solution)/shard_map/ppermute | solution.py:258
  44.0 0.7 %shard_map.87 = f32[1,256,256]{2,1,0:T(8,128)} custom-call(f32[128,256]{1,0:T(8,128)S(1)} %shard_map.86.mine_ref, f32[128,256]{1,0:T(8,128)S(1)} %collective-permute-done.16.other_ref), custom_call_target="tpu_custom_call" | custom-call | tf_op jit(solution)/shard_map/pallas_call | solution.py:22
  (5 shorter events, 0.1 us)
Async XLA Ops:
  0.6 9.8 %collective-permute-start = (f32[256,256]{1,0:T(8,128)}, f32[256,256]{1,0:T(8,128)S(1)}, u32[]{:S(2)}, u32[]{:S(2)}) collective-permute-start(f32[256,256]{1,0:T(8,128)} %bitcast.1), channel_id=1, source_target_pairs={{0,4},{2,6},{4,0},{6,2},{8,12},{10,14},{12,8},{14,10},{16,20},{18,... | collective-permute-start | bytes 786440 | tf_op jit(solution)/shard_map/ppermute | solution.py:272
  6.0 4.4 %collective-permute-start.1 = (s32[8,128]{1,0:T(8,128)S(1)}, s32[8,128]{1,0:T(8,128)S(1)}, u32[]{:S(2)}, u32[]{:S(2)}) collective-permute-start(s32[8,128]{1,0:T(8,128)S(1)} %get-tuple-element.25), channel_id=1, source_target_pairs={{0,4},{2,6},{4,0},{6,2},{8,12},{10,14},{12,8},{14,10},{16,20},{18,... | collective-permute-start | bytes 12296 | tf_op jit(solution)/shard_map/ppermute | solution.py:284
  10.5 1.5 %collective-permute-start.2 = (f32[256,256]{1,0:T(8,128)S(1)}, f32[256,256]{1,0:T(8,128)S(1)}, u32[]{:S(2)}, u32[]{:S(2)}) collective-permute-start(f32[256,256]{1,0:T(8,128)S(1)} %collective-permute-done.refs_5_), channel_id=1, source_target_pairs={{0,1},{1,0},{2,3},{3,2},{4,5},{5,4},{6,7},{7,6},{8,9},{9,8},{10,11... | collective-permute-start | bytes 786440 | tf_op jit(solution)/shard_map/ppermute | solution.py:258
  10.5 1.5 %collective-permute-start.3 = (s32[8,128]{1,0:T(8,128)S(1)}, s32[8,128]{1,0:T(8,128)S(1)}, u32[]{:S(2)}, u32[]{:S(2)}) collective-permute-start(s32[8,128]{1,0:T(8,128)S(1)} %collective-permute-done.1.refs_7_), channel_id=1, source_target_pairs={{0,1},{1,0},{2,3},{3,2},{4,5},{5,4},{6,7},{7,6},{8,9},{9,8},{10,11... | collective-permute-start | bytes 12296 | tf_op jit(solution)/shard_map/ppermute | solution.py:258
  14.5 1.4 %collective-permute-start.4 = (f32[128,256]{1,0:T(8,128)S(1)}, f32[128,256]{1,0:T(8,128)S(1)}, u32[]{:S(2)}, u32[]{:S(2)}) collective-permute-start(f32[128,256]{1,0:T(8,128)S(1)} %get-tuple-element.32), channel_id=1, source_target_pairs={{0,1},{1,0},{2,3},{3,2},{4,5},{5,4},{6,7},{7,6},{8,9},{9,8},{10,11... | collective-permute-start | bytes 393224 | tf_op jit(solution)/shard_map/ppermute | solution.py:258
  15.9 5.6 %collective-permute-start.5 = (f32[128,256]{1,0:T(8,128)S(1)}, f32[128,256]{1,0:T(8,128)S(1)}, u32[]{:S(2)}, u32[]{:S(2)}) collective-permute-start(f32[128,256]{1,0:T(8,128)S(1)} %add.6), channel_id=1, source_target_pairs={{0,2},{1,3},{2,0},{3,1},{4,6},{5,7},{6,4},{7,5},{8,10},{9,11},{10,... | collective-permute-start | bytes 393224 | tf_op jit(solution)/shard_map/ppermute | solution.py:268
  21.6 4.1 %collective-permute-start.6 = (f32[128,256]{1,0:T(8,128)S(1)}, f32[128,256]{1,0:T(8,128)S(1)}, u32[]{:S(2)}, u32[]{:S(2)}) collective-permute-start(f32[128,256]{1,0:T(8,128)S(1)} %add_multiply_fusion.first_ref.refs_3_), channel_id=1, source_target_pairs={{0,1},{1,0},{2,3},{3,2},{4,5},{5,4},{6,7},{7,6},{8,9},{9,8},{10,11... | collective-permute-start | bytes 393224 | tf_op jit(solution)/shard_map/ppermute | solution.py:258
  21.6 7.4 %collective-permute-start.11 = (f32[128,256]{1,0:T(8,128)S(1)}, f32[128,256]{1,0:T(8,128)S(1)}, u32[]{:S(2)}, u32[]{:S(2)}) collective-permute-start(f32[128,256]{1,0:T(8,128)S(1)} %add_multiply_fusion.first_ref.refs_3_), channel_id=1, source_target_pairs={{0,2},{28,30},{4,8},{8,4},{12,16},{16,12},{20,24},{24,20},{1,3},{2... | collective-permute-start | bytes 393224 | tf_op jit(solution)/shard_map/ppermute | solution.py:261
  23.2 8.5 %collective-permute-start.7 = (f32[128,256]{1,0:T(8,128)S(1)}, f32[128,256]{1,0:T(8,128)S(1)}, u32[]{:S(2)}, u32[]{:S(2)}) collective-permute-start(f32[128,256]{1,0:T(8,128)S(1)} %add_multiply_fusion.first_ref.refs_3_), channel_id=1, source_target_pairs={{0,4},{4,0},{8,12},{12,8},{16,20},{20,16},{24,28},{28,24},{1,5},{5... | collective-permute-start | bytes 393224 | tf_op jit(solution)/shard_map/ppermute | solution.py:261
  25.9 5.8 %collective-permute-start.9 = (f32[8,256]{1,0:T(8,128)S(1)}, f32[8,256]{1,0:T(8,128)S(1)}, u32[]{:S(2)}, u32[]{:S(2)}) collective-permute-start(f32[8,256]{1,0:T(8,128)S(1)} %shard_map.80.refs_0_), channel_id=1, source_target_pairs={{0,24},{1,9},{2,26},{3,11},{4,28},{5,13},{6,30},{7,15},{8,16},{9,1... | collective-permute-start | bytes 24584 | tf_op jit(solution)/shard_map/ppermute | solution.py:304
  27.9 3.9 %collective-permute-start.8 = (f32[8,256]{1,0:T(8,128)S(1)}, f32[8,256]{1,0:T(8,128)S(1)}, u32[]{:S(2)}, u32[]{:S(2)}) collective-permute-start(f32[8,256]{1,0:T(8,128)S(1)} %shard_map.80.refs_0_), channel_id=1, source_target_pairs={{0,8},{1,17},{2,10},{3,19},{4,12},{5,21},{6,14},{7,23},{8,0},{9,25... | collective-permute-start | bytes 24584 | tf_op jit(solution)/shard_map/ppermute | solution.py:304
  29.1 2.7 %collective-permute-start.12 = (f32[128,256]{1,0:T(8,128)S(1)}, f32[128,256]{1,0:T(8,128)S(1)}, u32[]{:S(2)}, u32[]{:S(2)}) collective-permute-start(f32[128,256]{1,0:T(8,128)S(1)} %collective-permute-done.11.refs_7_), channel_id=1, source_target_pairs={{0,1},{1,0},{2,3},{3,2},{4,5},{5,4},{6,7},{7,6},{8,9},{9,8},{10,11... | collective-permute-start | bytes 393224 | tf_op jit(solution)/shard_map/ppermute | solution.py:258
  31.7 1.4 %collective-permute-start.10 = (f32[128,256]{1,0:T(8,128)S(1)}, f32[128,256]{1,0:T(8,128)S(1)}, u32[]{:S(2)}, u32[]{:S(2)}) collective-permute-start(f32[128,256]{1,0:T(8,128)S(1)} %collective-permute-done.7.refs_5_), channel_id=1, source_target_pairs={{0,1},{1,0},{2,3},{3,2},{4,5},{5,4},{6,7},{7,6},{8,9},{9,8},{10,11... | collective-permute-start | bytes 393224 | tf_op jit(solution)/shard_map/ppermute | solution.py:258
  35.5 1.4 %collective-permute-start.13 = (f32[136,256]{1,0:T(8,128)S(1)}, f32[136,256]{1,0:T(8,128)S(1)}, u32[]{:S(2)}, u32[]{:S(2)}) collective-permute-start(f32[136,256]{1,0:T(8,128)S(1)} %get-tuple-element.37), channel_id=1, source_target_pairs={{0,1},{1,0},{2,3},{3,2},{4,5},{5,4},{6,7},{7,6},{8,9},{9,8},{10,11... | collective-permute-start | bytes 417800 | tf_op jit(solution)/shard_map/ppermute | solution.py:258
  37.0 5.6 %collective-permute-start.15 = (f32[128,256]{1,0:T(8,128)S(1)}, f32[128,256]{1,0:T(8,128)S(1)}, u32[]{:S(2)}, u32[]{:S(2)}) collective-permute-start(f32[128,256]{1,0:T(8,128)S(1)} %get-tuple-element.39.total_ref), channel_id=1, source_target_pairs={{0,2},{1,3},{2,0},{3,1},{4,6},{5,7},{6,4},{7,5},{8,10},{9,11},{10,... | collective-permute-start | bytes 393224 | tf_op jit(solution)/shard_map/ppermute | solution.py:268
  38.5 3.7 %collective-permute-start.14 = (f32[8,256]{1,0:T(8,128)S(1)}, f32[8,256]{1,0:T(8,128)S(1)}, u32[]{:S(2)}, u32[]{:S(2)}) collective-permute-start(f32[8,256]{1,0:T(8,128)S(1)} %get-tuple-element.38.refs_0_), channel_id=1, source_target_pairs={{0,4},{4,0},{8,12},{12,8},{16,20},{20,16},{24,28},{28,24},{1,5},{5... | collective-permute-start | bytes 24584 | tf_op jit(solution)/shard_map/ppermute | solution.py:325
  42.6 1.4 %collective-permute-start.16 = (f32[128,256]{1,0:T(8,128)S(1)}, f32[128,256]{1,0:T(8,128)S(1)}, u32[]{:S(2)}, u32[]{:S(2)}) collective-permute-start(f32[128,256]{1,0:T(8,128)S(1)} %shard_map.86.mine_ref), channel_id=1, source_target_pairs={{0,1},{1,0},{2,3},{3,2},{4,5},{5,4},{6,7},{7,6},{8,9},{9,8},{10,11... | collective-permute-start | bytes 393224 | tf_op jit(solution)/shard_map/ppermute | solution.py:258

commit v5 on v4

--- a/solution.py
+++ b/solution.py
@@ -108,28 +108,47 @@
     )
 
 
-def product_kernel(raw, tiled, shift_ref, *refs):
-    left_ref, right_ref, own_refs, refs = *refs[:2], refs[2:4], refs[4:]
-    send_ref, keep_ref, high, low, total = refs[-5:]
-    block = total.shape[0]
-    half = block // 2
+def half_product(which, shift_ref, high, low, left_ref, right_ref):
+    half = left_ref.shape[2] // 2
+    rows = rows_of(which, half)
+
+    def thrice(a, b, contract):
+        (a_high, a_low), (b_high, b_low) = a, b
+        both = dot(jnp.concatenate([a_high, a_low]), b_high, contract)
+        return both[:half] + (both[half:] + dot(a_high, b_low, contract))
+
+    inner = []
+    for term in range(left_ref.shape[0]):
+        source = 1 - shift_ref[term][0, 0]
+        inner.append(thrice(split(left_ref[term, 0, rows]), (high[source], low[source]), 0))
+    out = None
+    for term in range(right_ref.shape[0]):
+        part = thrice(split(inner[term]), split(right_ref[term, 0]), 1)
+        out = part if out is None else out + part
+    return out
+
+
+def send_kernel(raw, shift_ref, left_ref, right_ref, own_ref, own_other_ref, *refs):
+    *refs, send_ref, high, low = refs
+    half, block = send_ref.shape
     core, sector = core_index(), lax.axis_index("sec")
     slot = jnp.where(lax.rem(sector, 2) == 0, 2, 0)
-
-    def put(index, pair_of_refs):
-        for which, ref in zip((core, 1 - core), pair_of_refs):
+    got = jnp.where(core == 1, slot, 2 - slot)
+
+    def put(index, mine_ref, other_ref):
+        for which, ref in ((core, mine_ref), (1 - core, other_ref)):
             rows = rows_of(which, half)
             high[index, rows], low[index, rows] = split(ref[...])
 
-    put(1, own_refs)
+    put(1, own_ref, own_other_ref)
     if raw:
-        got = jnp.where(core == 0, slot, 2 - slot)
-        for index, ref, live_ref in zip((got, 2 - got), refs[:2], refs[2:4]):
+        for index, ref, live_ref in zip((got, 2 - got), refs[:2], refs[2:]):
             live = inside((block, block), 0, live_ref[:1, :1], live_ref[1:2, :1])
             high[index], low[index] = split(jnp.where(live, ref[...], 0.0))
     else:
-        put(slot, refs[:2])
-        put(2 - slot, refs[2:4])
+        one_ref, one_other_ref, two_ref, two_other_ref = refs
+        put(got, one_ref, two_other_ref)
+        put(2 - got, two_ref, one_other_ref)
 
     @pl.when(sector == 0)
     def _():
@@ -141,43 +160,40 @@
         high[2] = jnp.zeros(high.shape[1:], high.dtype)
         low[2] = jnp.zeros(low.shape[1:], low.dtype)
 
-    out = None
-    for term in range(left_ref.shape[0]):
-        source = 1 - shift_ref[term][0, 0]
-        left_high, left_low = split(left_ref[term, 0])
-        right_high, right_low = split(right_ref[term, 0])
-        v_high, v_low = high[source], low[source]
-        inner = dot(left_high, v_high, 0) + (dot(left_low, v_high, 0) + dot(left_high, v_low, 0))
-        inner_high, inner_low = split(inner)
-        part = dot(inner_high, right_high, 1) + (
-            dot(inner_low, right_high, 1) + dot(inner_high, right_low, 1)
-        )
-        out = part if out is None else out + part
-    total[...] = out
-    send_ref[pl.ds(0, half)] = total[rows_of(1 - core, half)]
-    keep_ref[pl.ds(0, half)] = total[rows_of(core, half)]
-    if tiled:
-        send_ref[pl.ds(half, EXTRA)] = refs[4][...]
-        keep_ref[pl.ds(half, EXTRA)] = refs[4][...]
-
-
-def product(shift, left, right, *arrays, raw=False, tiled=False):
+    send_ref[...] = half_product(1 - core, shift_ref, high, low, left_ref, right_ref)
+
+
+def keep_kernel(shift_ref, left_ref, right_ref, high, low, *refs):
+    refs[-1][...] = half_product(core_index(), shift_ref, high, low, left_ref, right_ref)
+
+
+def product_options(left):
     terms, _, block, _ = left.shape
+    return dict(
+        mib=16,
+        cost_estimate=pl.CostEstimate(
+            flops=30 * terms * block**3, bytes_accessed=8 * left.size, transcendentals=0
+        ),
+    )
+
+
+def product_to_send(shift, left, right, *arrays, raw=False):
+    block = left.shape[-1]
     arrays = [shift, left, right, *arrays]
     return call(
-        lambda *refs: product_kernel(raw, tiled, *refs),
-        [f32(block // 2 + (EXTRA if tiled else 0), block)] * 2,
+        lambda *refs: send_kernel(raw, *refs),
+        [f32(block // 2, block)] + [jax.ShapeDtypeStruct((3, block, block), jnp.bfloat16)] * 2,
         [VMEM] * len(arrays),
         *arrays,
-        mib=16,
-        scratch_shapes=[
-            pltpu.VMEM((3, block, block), jnp.bfloat16),
-            pltpu.VMEM((3, block, block), jnp.bfloat16),
-            pltpu.VMEM((block, block), jnp.float32),
-        ],
-        cost_estimate=pl.CostEstimate(
-            flops=12 * terms * block**3, bytes_accessed=4 * left.size, transcendentals=0
-        ),
+        **product_options(left),
+    )
+
+
+def product_to_keep(shift, left, right, high, low, *after):
+    block = left.shape[-1]
+    arrays = [shift, left, right, high, low, *after]
+    return call(
+        keep_kernel, f32(block // 2, block), [VMEM] * len(arrays), *arrays, **product_options(left)
     )
 
 
@@ -194,19 +210,8 @@
     out_ref[...] = jnp.where(lane == lax.axis_index("sec"), values, 0.0)
 
 
-def gathered_kernel(planes, tile_ref, *refs):
-    *tile_refs, out_ref = refs
-    core = core_index()
-    total = jnp.where(core == 0, tile_ref[...], 0.0)
-    for i, ref in enumerate(tile_refs):
-        total = total + jnp.where(1 + 2 * i + core < planes, ref[...], 0.0)
-    out_ref[...] = total
-
-
-def summed_kernel(keep_ref, got_ref, total_ref, sums_ref):
-    half = total_ref.shape[0]
-    total_ref[...] = keep_ref[pl.ds(0, half)] + got_ref[pl.ds(0, half)]
-    sums_ref[...] = keep_ref[pl.ds(half, EXTRA)] + got_ref[pl.ds(half, EXTRA)]
+def added_kernel(a_ref, b_ref, after_ref, out_ref):
+    out_ref[...] = a_ref[...] + b_ref[...]
 
 
 def merged_kernel(cells, sums_ref, got_ref, out_ref):
@@ -257,9 +262,6 @@
     def swapped(v):
         return lax.ppermute(v, "op", others)
 
-    def neighbours(mine):
-        return lax.ppermute(mine, ("sec", "op"), between), lax.ppermute(mine, "sec", pairs)
-
     def over_chips(total):
         step = 2
         while step < ops // 2:
@@ -267,8 +269,10 @@
             step *= 2
         return total, lax.ppermute(total, "op", [(i, i ^ step) for i in range(ops)])
 
-    crossing = [(s * ops + a, (s ^ 1) * ops + a) for s in range(sectors) for a in range(0, ops, 2)]
-    crossing += [(source, target) for source, target in between if source % 2]
+    crossing = [(s * ops + a, (s ^ 1) * ops + a) for s in range(sectors) for a in range(1, ops, 2)]
+    crossing += [(source, target) for source, target in between if source % 2 == 0]
+    crossing_too = [(s * ops + a, (s ^ 1) * ops + a) for s in range(sectors) for a in range(0, ops, 2)]
+    crossing_too += [(source, target) for source, target in between if source % 2]
     got = lax.ppermute(state[0], ("sec", "op"), crossing)
     field, field_other, mask, live = call(
         field_kernel,
@@ -284,38 +288,36 @@
     live = lax.ppermute(live, ("sec", "op"), crossing)
     left, right, shift = load(left_ops, right_ops, term_shift, field)
     got, left, right, live = lax.optimization_barrier((got, left, right, live))
-    send, keep = product(
+    send, *parts = product_to_send(
         shift, left, right, field, field_other, got, swapped(got), live, swapped(live), raw=True
     )
+    total, peer = over_chips(product_to_keep(shift, left, right, *parts) + swapped(send))
+
+    first = (total + peer) * mask
+    one = lax.ppermute(first, ("sec", "op"), crossing)
+    two = lax.ppermute(first, ("sec", "op"), crossing_too)
+    first_other = swapped(first)
+    sums = call(tile_kernel, f32(EXTRA, block), [VMEM] * 4, first, first_other, field, field_other)
+
+    def with_distant(sums, step):
+        return sums + lax.ppermute(sums, "sec", [(s, s ^ step) for s in range(sectors)])
+
+    step = sectors // 2
+    while step > 2:
+        sums = with_distant(sums, step)
+        step //= 2
+    two, sums = lax.optimization_barrier((two, sums))
+    send, *parts = product_to_send(
+        shift, left, right, first, first_other, one, swapped(one), two, swapped(two)
+    )
+    sums = call(
+        added_kernel,
+        f32(EXTRA, block),
+        [VMEM] * 3,
+        sums, lax.ppermute(sums, "sec", [(s, s ^ 2) for s in range(sectors)]), send,
+    )
+    keep = product_to_keep(shift, left, right, *parts, sums)
     total, peer = over_chips(keep + swapped(send))
-
-    first = (total + peer) * mask
-    far, near = neighbours(first)
-    first_other = swapped(first)
-    tile = call(tile_kernel, f32(EXTRA, block), [VMEM] * 4, first, first_other, field, field_other)
-    planes = sectors // 2
-    tiles = []
-    for base in range(1, planes, 2):
-        swaps = [
-            (s * ops + a, (s ^ (2 * (base + a % 2) if base + a % 2 < planes else 2)) * ops + a)
-            for s in range(sectors)
-            for a in range(ops)
-        ]
-        tiles.append(lax.ppermute(tile, ("sec", "op"), swaps))
-    tile = call(
-        lambda *refs: gathered_kernel(planes, *refs),
-        f32(EXTRA, block),
-        [VMEM] * (1 + len(tiles)),
-        tile, *tiles,
-    )
-    near, tile = lax.optimization_barrier((near, tile))
-    send, keep = product(
-        shift, left, right, first, first_other, near, swapped(near), far, swapped(far), tile, tiled=True
-    )
-    total, sums = call(
-        summed_kernel, [f32(half, block), f32(EXTRA, block)], [VMEM] * 2, keep, swapped(send)
-    )
-    total, peer = over_chips(total)
 
     cells = sectors * block * block
     merged = call(

time: 44.9 us -> 42.9 us (0.955)
  waiting for transfers between devices: 16 us -> 11.1 us
  starting transfers between devices: 16.4 us -> 18.2 us
  Pallas kernels: 10.3 us -> 11.3 us
    ppermute x8, waiting for transfers between devices: 5.38 us -> 1.64 us  [swapped(): return lax.ppermute(v, 'op', others)]
    ppermute x4, starting transfers between devices: 7.17 us -> 8.38 us  [the longest x1 2.74 us: local(): two = lax.ppermute(first, ('sec', 'op'), crossing_too)]
    pallas_call x11 -> x12, Pallas kernels: 10.3 us -> 11.3 us  [call(): pl.pallas_call(kernel, out_shape=out_shape, in_specs=in_specs, out_specs=...]
    ppermute x4, waiting for transfers between devices: 2.65 us -> 1.69 us  [the longest x1 1.68 us: with_distant(): lax.ppermute(sums, 'sec', [(s, s ^ step) for s in range(sectors)])]
    ppermute x1, waiting for transfers between devices: 1.98 us -> 1.24 us  [local(): live = lax.ppermute(live, ('sec', 'op'), crossing)]
    ppermute x8, starting transfers between devices: 1.13 us -> 1.86 us  [swapped(): return lax.ppermute(v, 'op', others)]
    ppermute x2, waiting for transfers between devices: 4.15 us -> 4.76 us  [over_chips(): lax.ppermute(total, 'op', [(i, i ^ step) for i in range(ops)])]
  transfers between devices with their start and end apart: 17 -> 17, of which waited for: 10 -> 7; matrix products, arithmetic and copies ran while one was open for 0% -> 0% of each run, Pallas kernels for 10% -> 21%
where the time goes in v5:
time: 42.9 us; the launch traced here: 42.7 us
  starting transfers between devices  18.2 us (42%)
  Pallas kernels  11.3 us (26%)
  waiting for transfers between devices  11.1 us (26%)
  between operations  2.05 us (5%)
    pallas_call x12, Pallas kernels, call(): pl.pallas_call(kernel, out_shape=out_shape, in_specs=in_specs, out_specs=...  11.3 us
    ppermute x2, waiting for transfers between devices, over_chips(): lax.ppermute(total, 'op', [(i, i ^ step) for i in range(ops)])  4.76 us
    ppermute x1, starting transfers between devices, local(): got = lax.ppermute(state[0], ('sec', 'op'), crossing)  3.03 us
    ppermute x2, starting transfers between devices, over_chips(): lax.ppermute(total, 'op', [(i, i ^ step) for i in range(ops)])  2.92 us
    ppermute x1, starting transfers between devices, local(): two = lax.ppermute(first, ('sec', 'op'), crossing_too)  2.74 us
    ppermute x1, starting transfers between devices, with_distant(): lax.ppermute(sums, 'sec', [(s, s ^ step) for s in range(sectors)])  2.6 us
    ppermute x1, starting transfers between devices, local(): lax.ppermute(sums, 'sec', [(s, s ^ 2) for s in range(sectors)])  1.95 us
    ppermute x1, starting transfers between devices, local(): lax.ppermute(sums, 'sec', pairs)  1.91 us
  transfers between devices with their start and end apart: 17, of which 7 were waited for; matrix products, arithmetic and copies ran while one was open for 0% of the time, Pallas kernels for 21%

profile of v5, /device:TPU:0, one launch (start us, length us, event | category | flops | bytes accessed | tf_op | source)
XLA Modules:
  0.0 42.7 jit_solution(2154572138816242950)
XLA Ops:
  0.6 3.0 %collective-permute-start = (f32[256,256]{1,0:T(8,128)}, f32[256,256]{1,0:T(8,128)S(1)}, u32[]{:S(2)}, u32[]{:S(2)}) collective-permute-start(f32[256,256]{1,0:T(8,128)} %bitcast.1), channel_id=1, source_target_pairs={{1,5},{3,7},{5,1},{7,3},{9,13},{11,15},{13,9},{15,11},{17,21},{19,... | collective-permute-start | bytes 786440 | tf_op jit(solution)/shard_map/ppermute | solution.py:276
  5.0 0.1 pad_add_fusion.live_ref
  5.0 1.0 %shard_map.77 = (f32[128,256]{1,0:T(8,128)S(1)}, f32[128,256]{1,0:T(8,128)S(1)}, f32[128,256]{1,0:T(8,128)S(1)}, s32[8,128]{1,0:T(8,128)S(1)}) custom-call(f32[1,256,256]{2,1,0:T(8,128)} %state_ref.1, s32[2]{0:T(128)S(1)} %pad_add_fusion.live_ref), custom_call_target="tpu_custom_call" | custom-call | tf_op jit(solution)/shard_map/pallas_call | solution.py:22
  6.1 0.1 collective-permute-start.1
  6.1 2.4 %shard_map.78 = (f32[8,1,256,256]{3,2,1,0:T(8,128)S(1)}, f32[8,1,256,256]{3,2,1,0:T(8,128)S(1)}, s32[8,8,128]{2,1,0:T(8,128)S(1)}) custom-call(f32[8,1,256,256]{3,2,1,0:T(8,128)} %left_ref.1, f32[8,1,256,256]{3,2,1,0:T(8,128)} %right_ref.1, s32[8]{0:T(128)} %shift_ref.1, f32[128,256]{1,0:T(8,128)S(1)} %get-tuple-element.21.field_ref.refs_3_), custom_call_target="tpu_custom_call" | custom-call | bytes 4194304 | tf_op jit(solution)/shard_map/pallas_call | solution.py:22
  8.5 1.2 %collective-permute-done.1.refs_7_ = s32[8,128]{1,0:T(8,128)S(1)} collective-permute-done((s32[8,128]{1,0:T(8,128)S(1)}, s32[8,128]{1,0:T(8,128)S(1)}, u32[]{:S(2)}, u32[]{:S(2)}) %collective-permute-start.1) | collective-permute-done | bytes 4128 | tf_op jit(solution)/shard_map/ppermute | solution.py:288
  9.7 0.0 collective-permute-done.refs_5_
  9.7 0.0 collective-permute-start.2
  9.7 0.5 %collective-permute-start.3 = (s32[8,128]{1,0:T(8,128)S(1)}, s32[8,128]{1,0:T(8,128)S(1)}, u32[]{:S(2)}, u32[]{:S(2)}) collective-permute-start(s32[8,128]{1,0:T(8,128)S(1)} %collective-permute-done.1.refs_7_), channel_id=1, source_target_pairs={{0,1},{1,0},{2,3},{3,2},{4,5},{5,4},{6,7},{7,6},{8,9},{9,8},{10,11... | collective-permute-start | bytes 12296 | tf_op jit(solution)/shard_map/ppermute | solution.py:263
  10.3 1.0 %collective-permute-done.3.refs_8_ = s32[8,128]{1,0:T(8,128)S(1)} collective-permute-done((s32[8,128]{1,0:T(8,128)S(1)}, s32[8,128]{1,0:T(8,128)S(1)}, u32[]{:S(2)}, u32[]{:S(2)}) %collective-permute-start.3) | collective-permute-done | bytes 4128 | tf_op jit(solution)/shard_map/ppermute | solution.py:263
  11.3 0.0 collective-permute-done.2.refs_6_
  11.3 1.6 %shard_map.79 = (f32[128,256]{1,0:T(8,128)S(1)}, bf16[3,256,256]{2,1,0:T(8,128)(2,1)S(1)}, bf16[3,256,256]{2,1,0:T(8,128)(2,1)S(1)}) custom-call(s32[8,8,128]{2,1,0:T(8,128)S(1)} %get-tuple-element.22.refs_0_.shift_ref, f32[8,1,256,256]{3,2,1,0:T(8,128)S(1)} %get-tuple-element.26.refs_1_.left_ref, ...), custom_call_target="tpu_custom_call" | custom-call | flops 4026531840 | bytes 4194304 | tf_op jit(solution)/shard_map/pallas_call | solution.py:22
  12.9 0.2 collective-permute-start.4
  13.1 1.4 %shard_map.80 = f32[128,256]{1,0:T(8,128)S(1)} custom-call(s32[8,8,128]{2,1,0:T(8,128)S(1)} %get-tuple-element.22.refs_0_.shift_ref, f32[8,1,256,256]{3,2,1,0:T(8,128)S(1)} %get-tuple-element.26.refs_1_.left_ref, f32[8,1,256,256]{3,2,1,0:T(8,128)S(1)} %get-tuple-element.27.refs_2_.right_ref, bf16[3,256,256]{2,1,0:T(8,128)(2,1)S(1)} %get-tuple-element.31.high, ...), custom_call_target="tpu_custom_call" | custom-call | flops 4026531840 | bytes 4194304 | tf_op jit(solution)/shard_map/pallas_call | solution.py:22
  14.5 0.0 collective-permute-done.4
  14.6 1.3 %collective-permute-start.5 = (f32[128,256]{1,0:T(8,128)S(1)}, f32[128,256]{1,0:T(8,128)S(1)}, u32[]{:S(2)}, u32[]{:S(2)}) collective-permute-start(f32[128,256]{1,0:T(8,128)S(1)} %add.12), channel_id=1, source_target_pairs={{0,2},{1,3},{2,0},{3,1},{4,6},{5,7},{6,4},{7,5},{8,10},{9,11},{10,... | collective-permute-start | bytes 393224 | tf_op jit(solution)/shard_map/ppermute | solution.py:270
  15.9 4.5 %collective-permute-done.5 = f32[128,256]{1,0:T(8,128)S(1)} collective-permute-done((f32[128,256]{1,0:T(8,128)S(1)}, f32[128,256]{1,0:T(8,128)S(1)}, u32[]{:S(2)}, u32[]{:S(2)}) %collective-permute-start.5) | collective-permute-done | bytes 131104 | tf_op jit(solution)/shard_map/ppermute | solution.py:270
  20.4 0.1 collective-permute-start.7
  20.5 1.1 %collective-permute-start.10 = (f32[128,256]{1,0:T(8,128)S(1)}, f32[128,256]{1,0:T(8,128)S(1)}, u32[]{:S(2)}, u32[]{:S(2)}) collective-permute-start(f32[128,256]{1,0:T(8,128)S(1)} %add_multiply_fusion.first_ref.refs_3_), channel_id=1, source_target_pairs={{1,5},{3,7},{5,1},{7,3},{9,13},{11,15},{13,9},{15,11},{17,21},{19,... | collective-permute-start | bytes 393224 | tf_op jit(solution)/shard_map/ppermute | solution.py:297
  21.6 2.7 %collective-permute-start.6 = (f32[128,256]{1,0:T(8,128)S(1)}, f32[128,256]{1,0:T(8,128)S(1)}, u32[]{:S(2)}, u32[]{:S(2)}) collective-permute-start(f32[128,256]{1,0:T(8,128)S(1)} %add_multiply_fusion.first_ref.refs_3_), channel_id=1, source_target_pairs={{0,4},{2,6},{4,0},{6,2},{8,12},{10,14},{12,8},{14,10},{16,20},{18,... | collective-permute-start | bytes 393224 | tf_op jit(solution)/shard_map/ppermute | solution.py:298
  24.4 0.0 collective-permute-done.7.first_other_ref.refs_4_
  24.4 0.3 shard_map.81
  24.6 2.6 %collective-permute-start.8 = (f32[8,256]{1,0:T(8,128)S(1)}, f32[8,256]{1,0:T(8,128)S(1)}, u32[]{:S(2)}, u32[]{:S(2)}) collective-permute-start(f32[8,256]{1,0:T(8,128)S(1)} %shard_map.81), channel_id=1, source_target_pairs={{0,16},{4,20},{8,24},{12,28},{16,0},{20,4},{24,8},{28,12},{1,17},{... | collective-permute-start | bytes 24584 | tf_op jit(solution)/shard_map/ppermute | solution.py:303
  27.2 0.0 collective-permute-done.10.refs_5_
  27.2 0.7 %collective-permute-start.11 = (f32[128,256]{1,0:T(8,128)S(1)}, f32[128,256]{1,0:T(8,128)S(1)}, u32[]{:S(2)}, u32[]{:S(2)}) collective-permute-start(f32[128,256]{1,0:T(8,128)S(1)} %collective-permute-done.10.refs_5_), channel_id=1, source_target_pairs={{0,1},{1,0},{2,3},{3,2},{4,5},{5,4},{6,7},{7,6},{8,9},{9,8},{10,11... | collective-permute-start | bytes 393224 | tf_op jit(solution)/shard_map/ppermute | solution.py:263
  27.9 1.7 %collective-permute-done.8 = f32[8,256]{1,0:T(8,128)S(1)} collective-permute-done((f32[8,256]{1,0:T(8,128)S(1)}, f32[8,256]{1,0:T(8,128)S(1)}, u32[]{:S(2)}, u32[]{:S(2)}) %collective-permute-start.8) | collective-permute-done | bytes 8224 | tf_op jit(solution)/shard_map/ppermute | solution.py:303
  29.6 0.0 collective-permute-done.6.refs_7_
  29.6 0.0 collective-permute-start.12
  29.6 1.9 %collective-permute-start.9 = (f32[8,256]{1,0:T(8,128)S(1)}, f32[8,256]{1,0:T(8,128)S(1)}, u32[]{:S(2)}, u32[]{:S(2)}) collective-permute-start(f32[8,256]{1,0:T(8,128)S(1)} %add.14.a_ref), channel_id=1, source_target_pairs={{0,8},{4,12},{8,0},{12,4},{16,24},{20,28},{24,16},{28,20},{1,9},{5... | collective-permute-start | bytes 24584 | tf_op jit(solution)/shard_map/ppermute | solution.py:317
  31.6 0.0 collective-permute-done.11.refs_6_
  31.6 0.0 collective-permute-done.12.refs_8_
  31.6 1.5 %shard_map.82 = (f32[128,256]{1,0:T(8,128)S(1)}, bf16[3,256,256]{2,1,0:T(8,128)(2,1)S(1)}, bf16[3,256,256]{2,1,0:T(8,128)(2,1)S(1)}) custom-call(s32[8,8,128]{2,1,0:T(8,128)S(1)} %get-tuple-element.22.refs_0_.shift_ref, f32[8,1,256,256]{3,2,1,0:T(8,128)S(1)} %get-tuple-element.26.refs_1_.left_ref, ...), custom_call_target="tpu_custom_call" | custom-call | flops 4026531840 | bytes 4194304 | tf_op jit(solution)/shard_map/pallas_call | solution.py:22
  33.1 0.3 collective-permute-start.14
  33.4 0.0 collective-permute-done.9.b_ref
  33.4 1.4 %shard_map.86 = f32[128,256]{1,0:T(8,128)S(1)} custom-call(s32[8,8,128]{2,1,0:T(8,128)S(1)} %get-tuple-element.22.refs_0_.shift_ref, f32[8,1,256,256]{3,2,1,0:T(8,128)S(1)} %get-tuple-element.26.refs_1_.left_ref, f32[8,1,256,256]{3,2,1,0:T(8,128)S(1)} %get-tuple-element.27.refs_2_.right_ref, bf16[3,256,256]{2,1,0:T(8,128)(2,1)S(1)} %get-tuple-element.38.high, ...), custom_call_target="tpu_custom_call" | custom-call | flops 4026531840 | bytes 4194304 | tf_op jit(solution)/shard_map/pallas_call | solution.py:22
  34.8 0.0 collective-permute-done.14
  34.8 1.6 %collective-permute-start.15 = (f32[128,256]{1,0:T(8,128)S(1)}, f32[128,256]{1,0:T(8,128)S(1)}, u32[]{:S(2)}, u32[]{:S(2)}) collective-permute-start(f32[128,256]{1,0:T(8,128)S(1)} %add.15.total_ref), channel_id=1, source_target_pairs={{0,2},{1,3},{2,0},{3,1},{4,6},{5,7},{6,4},{7,5},{8,10},{9,11},{10,... | collective-permute-start | bytes 393224 | tf_op jit(solution)/shard_map/ppermute | solution.py:270
  36.4 1.9 %collective-permute-start.13 = (f32[8,256]{1,0:T(8,128)S(1)}, f32[8,256]{1,0:T(8,128)S(1)}, u32[]{:S(2)}, u32[]{:S(2)}) collective-permute-start(f32[8,256]{1,0:T(8,128)S(1)} %shard_map.83.refs_0_), channel_id=1, source_target_pairs={{0,4},{4,0},{8,12},{12,8},{16,20},{20,16},{24,28},{28,24},{1,5},{5... | collective-permute-start | bytes 24584 | tf_op jit(solution)/shard_map/ppermute | solution.py:327
  38.3 1.7 %collective-permute-done.13.refs_1_ = f32[8,256]{1,0:T(8,128)S(1)} collective-permute-done((f32[8,256]{1,0:T(8,128)S(1)}, f32[8,256]{1,0:T(8,128)S(1)}, u32[]{:S(2)}, u32[]{:S(2)}) %collective-permute-start.13) | collective-permute-done | bytes 8224 | tf_op jit(solution)/shard_map/ppermute | solution.py:327
  40.0 0.3 shard_map.84.merged_ref
  40.3 0.3 collective-permute-done.15.peer_ref
  40.6 0.1 collective-permute-start.16
  40.7 0.7 %shard_map.85 = f32[1,256,256]{2,1,0:T(8,128)} custom-call(f32[8,256]{1,0:T(8,128)S(1)} %shard_map.84.merged_ref, f32[128,256]{1,0:T(8,128)S(1)} %add_multiply_fusion.first_ref.refs_3_, f32[128,256]{1,0:T(8,128)S(1)} %collective-permute-done.7.first_other_ref.refs_4_, f32[128,256]{1,0:T(8,128)S(1)} %get-tuple-element.21.field_ref.refs_3_, ...), custom_call_target="tpu_custom_call" | custom-call | tf_op jit(solution)/shard_map/pallas_call | solution.py:22
  41.4 0.6 %collective-permute-done.16.other_ref = f32[128,256]{1,0:T(8,128)S(1)} collective-permute-done((f32[128,256]{1,0:T(8,128)S(1)}, f32[128,256]{1,0:T(8,128)S(1)}, u32[]{:S(2)}, u32[]{:S(2)}) %collective-permute-start.16) | collective-permute-done | bytes 131104 | tf_op jit(solution)/shard_map/ppermute | solution.py:263
  42.0 0.7 %shard_map.88 = f32[1,256,256]{2,1,0:T(8,128)} custom-call(f32[128,256]{1,0:T(8,128)S(1)} %shard_map.87.mine_ref, f32[128,256]{1,0:T(8,128)S(1)} %collective-permute-done.16.other_ref), custom_call_target="tpu_custom_call" | custom-call | tf_op jit(solution)/shard_map/pallas_call | solution.py:22
  (6 shorter events, 0.1 us)
Async XLA Ops:
  0.6 9.1 %collective-permute-start = (f32[256,256]{1,0:T(8,128)}, f32[256,256]{1,0:T(8,128)S(1)}, u32[]{:S(2)}, u32[]{:S(2)}) collective-permute-start(f32[256,256]{1,0:T(8,128)} %bitcast.1), channel_id=1, source_target_pairs={{1,5},{3,7},{5,1},{7,3},{9,13},{11,15},{13,9},{15,11},{17,21},{19,... | collective-permute-start | bytes 786440 | tf_op jit(solution)/shard_map/ppermute | solution.py:276
  6.1 3.7 %collective-permute-start.1 = (s32[8,128]{1,0:T(8,128)S(1)}, s32[8,128]{1,0:T(8,128)S(1)}, u32[]{:S(2)}, u32[]{:S(2)}) collective-permute-start(s32[8,128]{1,0:T(8,128)S(1)} %get-tuple-element.25), channel_id=1, source_target_pairs={{1,5},{3,7},{5,1},{7,3},{9,13},{11,15},{13,9},{15,11},{17,21},{19,... | collective-permute-start | bytes 12296 | tf_op jit(solution)/shard_map/ppermute | solution.py:288
  9.7 1.5 %collective-permute-start.2 = (f32[256,256]{1,0:T(8,128)S(1)}, f32[256,256]{1,0:T(8,128)S(1)}, u32[]{:S(2)}, u32[]{:S(2)}) collective-permute-start(f32[256,256]{1,0:T(8,128)S(1)} %collective-permute-done.refs_5_), channel_id=1, source_target_pairs={{0,1},{1,0},{2,3},{3,2},{4,5},{5,4},{6,7},{7,6},{8,9},{9,8},{10,11... | collective-permute-start | bytes 786440 | tf_op jit(solution)/shard_map/ppermute | solution.py:263
  9.7 1.5 %collective-permute-start.3 = (s32[8,128]{1,0:T(8,128)S(1)}, s32[8,128]{1,0:T(8,128)S(1)}, u32[]{:S(2)}, u32[]{:S(2)}) collective-permute-start(s32[8,128]{1,0:T(8,128)S(1)} %collective-permute-done.1.refs_7_), channel_id=1, source_target_pairs={{0,1},{1,0},{2,3},{3,2},{4,5},{5,4},{6,7},{7,6},{8,9},{9,8},{10,11... | collective-permute-start | bytes 12296 | tf_op jit(solution)/shard_map/ppermute | solution.py:263
  12.9 1.6 %collective-permute-start.4 = (f32[128,256]{1,0:T(8,128)S(1)}, f32[128,256]{1,0:T(8,128)S(1)}, u32[]{:S(2)}, u32[]{:S(2)}) collective-permute-start(f32[128,256]{1,0:T(8,128)S(1)} %get-tuple-element.33), channel_id=1, source_target_pairs={{0,1},{1,0},{2,3},{3,2},{4,5},{5,4},{6,7},{7,6},{8,9},{9,8},{10,11... | collective-permute-start | bytes 393224 | tf_op jit(solution)/shard_map/ppermute | solution.py:263
  14.6 5.8 %collective-permute-start.5 = (f32[128,256]{1,0:T(8,128)S(1)}, f32[128,256]{1,0:T(8,128)S(1)}, u32[]{:S(2)}, u32[]{:S(2)}) collective-permute-start(f32[128,256]{1,0:T(8,128)S(1)} %add.12), channel_id=1, source_target_pairs={{0,2},{1,3},{2,0},{3,1},{4,6},{5,7},{6,4},{7,5},{8,10},{9,11},{10,... | collective-permute-start | bytes 393224 | tf_op jit(solution)/shard_map/ppermute | solution.py:270
  20.4 3.9 %collective-permute-start.7 = (f32[128,256]{1,0:T(8,128)S(1)}, f32[128,256]{1,0:T(8,128)S(1)}, u32[]{:S(2)}, u32[]{:S(2)}) collective-permute-start(f32[128,256]{1,0:T(8,128)S(1)} %add_multiply_fusion.first_ref.refs_3_), channel_id=1, source_target_pairs={{0,1},{1,0},{2,3},{3,2},{4,5},{5,4},{6,7},{7,6},{8,9},{9,8},{10,11... | collective-permute-start | bytes 393224 | tf_op jit(solution)/shard_map/ppermute | solution.py:263
  20.5 6.7 %collective-permute-start.10 = (f32[128,256]{1,0:T(8,128)S(1)}, f32[128,256]{1,0:T(8,128)S(1)}, u32[]{:S(2)}, u32[]{:S(2)}) collective-permute-start(f32[128,256]{1,0:T(8,128)S(1)} %add_multiply_fusion.first_ref.refs_3_), channel_id=1, source_target_pairs={{1,5},{3,7},{5,1},{7,3},{9,13},{11,15},{13,9},{15,11},{17,21},{19,... | collective-permute-start | bytes 393224 | tf_op jit(solution)/shard_map/ppermute | solution.py:297
  21.6 8.0 %collective-permute-start.6 = (f32[128,256]{1,0:T(8,128)S(1)}, f32[128,256]{1,0:T(8,128)S(1)}, u32[]{:S(2)}, u32[]{:S(2)}) collective-permute-start(f32[128,256]{1,0:T(8,128)S(1)} %add_multiply_fusion.first_ref.refs_3_), channel_id=1, source_target_pairs={{0,4},{2,6},{4,0},{6,2},{8,12},{10,14},{12,8},{14,10},{16,20},{18,... | collective-permute-start | bytes 393224 | tf_op jit(solution)/shard_map/ppermute | solution.py:298
  24.6 5.0 %collective-permute-start.8 = (f32[8,256]{1,0:T(8,128)S(1)}, f32[8,256]{1,0:T(8,128)S(1)}, u32[]{:S(2)}, u32[]{:S(2)}) collective-permute-start(f32[8,256]{1,0:T(8,128)S(1)} %shard_map.81), channel_id=1, source_target_pairs={{0,16},{4,20},{8,24},{12,28},{16,0},{20,4},{24,8},{28,12},{1,17},{... | collective-permute-start | bytes 24584 | tf_op jit(solution)/shard_map/ppermute | solution.py:303
  27.2 4.4 %collective-permute-start.11 = (f32[128,256]{1,0:T(8,128)S(1)}, f32[128,256]{1,0:T(8,128)S(1)}, u32[]{:S(2)}, u32[]{:S(2)}) collective-permute-start(f32[128,256]{1,0:T(8,128)S(1)} %collective-permute-done.10.refs_5_), channel_id=1, source_target_pairs={{0,1},{1,0},{2,3},{3,2},{4,5},{5,4},{6,7},{7,6},{8,9},{9,8},{10,11... | collective-permute-start | bytes 393224 | tf_op jit(solution)/shard_map/ppermute | solution.py:263
  29.6 2.0 %collective-permute-start.12 = (f32[128,256]{1,0:T(8,128)S(1)}, f32[128,256]{1,0:T(8,128)S(1)}, u32[]{:S(2)}, u32[]{:S(2)}) collective-permute-start(f32[128,256]{1,0:T(8,128)S(1)} %collective-permute-done.6.refs_7_), channel_id=1, source_target_pairs={{0,1},{1,0},{2,3},{3,2},{4,5},{5,4},{6,7},{7,6},{8,9},{9,8},{10,11... | collective-permute-start | bytes 393224 | tf_op jit(solution)/shard_map/ppermute | solution.py:263
  29.6 3.7 %collective-permute-start.9 = (f32[8,256]{1,0:T(8,128)S(1)}, f32[8,256]{1,0:T(8,128)S(1)}, u32[]{:S(2)}, u32[]{:S(2)}) collective-permute-start(f32[8,256]{1,0:T(8,128)S(1)} %add.14.a_ref), channel_id=1, source_target_pairs={{0,8},{4,12},{8,0},{12,4},{16,24},{20,28},{24,16},{28,20},{1,9},{5... | collective-permute-start | bytes 24584 | tf_op jit(solution)/shard_map/ppermute | solution.py:317
  33.1 1.7 %collective-permute-start.14 = (f32[128,256]{1,0:T(8,128)S(1)}, f32[128,256]{1,0:T(8,128)S(1)}, u32[]{:S(2)}, u32[]{:S(2)}) collective-permute-start(f32[128,256]{1,0:T(8,128)S(1)} %get-tuple-element.37.after_ref), channel_id=1, source_target_pairs={{0,1},{1,0},{2,3},{3,2},{4,5},{5,4},{6,7},{7,6},{8,9},{9,8},{10,11... | collective-permute-start | bytes 393224 | tf_op jit(solution)/shard_map/ppermute | solution.py:263
  34.8 5.7 %collective-permute-start.15 = (f32[128,256]{1,0:T(8,128)S(1)}, f32[128,256]{1,0:T(8,128)S(1)}, u32[]{:S(2)}, u32[]{:S(2)}) collective-permute-start(f32[128,256]{1,0:T(8,128)S(1)} %add.15.total_ref), channel_id=1, source_target_pairs={{0,2},{1,3},{2,0},{3,1},{4,6},{5,7},{6,4},{7,5},{8,10},{9,11},{10,... | collective-permute-start | bytes 393224 | tf_op jit(solution)/shard_map/ppermute | solution.py:270
  36.4 3.7 %collective-permute-start.13 = (f32[8,256]{1,0:T(8,128)S(1)}, f32[8,256]{1,0:T(8,128)S(1)}, u32[]{:S(2)}, u32[]{:S(2)}) collective-permute-start(f32[8,256]{1,0:T(8,128)S(1)} %shard_map.83.refs_0_), channel_id=1, source_target_pairs={{0,4},{4,0},{8,12},{12,8},{16,20},{20,16},{24,28},{28,24},{1,5},{5... | collective-permute-start | bytes 24584 | tf_op jit(solution)/shard_map/ppermute | solution.py:327
  40.6 1.4 %collective-permute-start.16 = (f32[128,256]{1,0:T(8,128)S(1)}, f32[128,256]{1,0:T(8,128)S(1)}, u32[]{:S(2)}, u32[]{:S(2)}) collective-permute-start(f32[128,256]{1,0:T(8,128)S(1)} %shard_map.87.mine_ref), channel_id=1, source_target_pairs={{0,1},{1,0},{2,3},{3,2},{4,5},{5,4},{6,7},{7,6},{8,9},{9,8},{10,11... | collective-permute-start | bytes 393224 | tf_op jit(solution)/shard_map/ppermute | solution.py:263

commit v6 on v5

--- a/solution.py
+++ b/solution.py
@@ -43,10 +43,8 @@
     return high, low
 
 
-def dot(a, b, contract):
-    return lax.dot_general(
-        a, b, (((1,), (contract,)), ((), ())), preferred_element_type=jnp.float32
-    )
+def dot(a, b):
+    return jnp.dot(a, b, preferred_element_type=jnp.float32)
 
 
 def total_of(x):
@@ -78,21 +76,26 @@
     live_out[...] = jnp.where(row == 0, rows, cols)
 
 
-def load_kernel(left_ref, right_ref, shift_ref, field_ref, left_out, right_out, shift_out, shift, sems):
+def load_kernel(left_ref, right_ref, shift_ref, field_ref, left_out, right_out, shift_out, right, shift, sems):
     terms = left_ref.shape[0]
     shifts = pltpu.make_async_copy(shift_ref, shift, sems.at[2, 0])
-    copies = [
-        pltpu.make_async_copy(ref.at[term], out.at[term], sems.at[side, term])
+    rights = [
+        pltpu.make_async_copy(right_ref.at[term], right.at[term], sems.at[0, term])
         for term in range(terms)
-        for side, (ref, out) in enumerate(((left_ref, left_out), (right_ref, right_out)))
     ]
-    shifts.start()
-    for copy in copies:
+    lefts = [
+        pltpu.make_async_copy(left_ref.at[term], left_out.at[term], sems.at[1, term])
+        for term in range(terms)
+    ]
+    for copy in (shifts, *rights, *lefts):
         copy.start()
     shifts.wait()
     for term in range(terms):
         shift_out[term] = jnp.full(shift_out.shape[1:], shift[term], jnp.int32)
-    for copy in copies:
+    for term in range(terms):
+        rights[term].wait()
+        right_out[term, 0] = right[term, 0].T
+    for copy in lefts:
         copy.wait()
 
 
@@ -103,7 +106,12 @@
         [f32(*left_ops.shape), f32(*right_ops.shape), jax.ShapeDtypeStruct((terms, 8, 128), jnp.int32)],
         [HBM, HBM, HBM, VMEM],
         in_hbm(left_ops), in_hbm(right_ops), in_hbm(shift), field,
-        scratch_shapes=[pltpu.SMEM(shift.shape, jnp.int32), pltpu.SemaphoreType.DMA((3, terms))],
+        mib=8,
+        scratch_shapes=[
+            pltpu.VMEM(right_ops.shape, jnp.float32),
+            pltpu.SMEM(shift.shape, jnp.int32),
+            pltpu.SemaphoreType.DMA((3, terms)),
+        ],
         cost_estimate=pl.CostEstimate(flops=0, bytes_accessed=8 * left_ops.size, transcendentals=0),
     )
 
@@ -112,18 +120,18 @@
     half = left_ref.shape[2] // 2
     rows = rows_of(which, half)
 
-    def thrice(a, b, contract):
+    def thrice(a, b):
         (a_high, a_low), (b_high, b_low) = a, b
-        both = dot(jnp.concatenate([a_high, a_low]), b_high, contract)
-        return both[:half] + (both[half:] + dot(a_high, b_low, contract))
+        both = dot(jnp.concatenate([a_high, a_low]), b_high)
+        return both[:half] + (both[half:] + dot(a_high, b_low))
 
     inner = []
     for term in range(left_ref.shape[0]):
         source = 1 - shift_ref[term][0, 0]
-        inner.append(thrice(split(left_ref[term, 0, rows]), (high[source], low[source]), 0))
+        inner.append(thrice(split(left_ref[term, 0, rows]), (high[source], low[source])))
     out = None
     for term in range(right_ref.shape[0]):
-        part = thrice(split(inner[term]), split(right_ref[term, 0]), 1)
+        part = thrice(split(inner[term]), split(right_ref[term, 0]))
         out = part if out is None else out + part
     return out
 

time: 42.9 us -> 42.1 us (0.981)
  Pallas kernels: 11.3 us -> 10.5 us
    pallas_call x12, Pallas kernels: 11.3 us -> 10.5 us  [call(): pl.pallas_call(kernel, out_shape=out_shape, in_specs=in_specs, out_specs=...]
  transfers between devices with their start and end apart: 17 -> 17, of which waited for: 7 -> 8; matrix products, arithmetic and copies ran while one was open for 0% -> 0% of each run, Pallas kernels for 21% -> 20%
where the time goes in v6:
time: 42.1 us; the launch traced here: 41.9 us
  starting transfers between devices  18.2 us (43%)
  waiting for transfers between devices  11 us (26%)
  Pallas kernels  10.5 us (25%)
  between operations  2.05 us (5%)
    pallas_call x12, Pallas kernels, call(): pl.pallas_call(kernel, out_shape=out_shape, in_specs=in_specs, out_specs=...  10.5 us
    ppermute x2, waiting for transfers between devices, over_chips(): lax.ppermute(total, 'op', [(i, i ^ step) for i in range(ops)])  4.58 us
    ppermute x1, starting transfers between devices, local(): got = lax.ppermute(state[0], ('sec', 'op'), crossing)  3.03 us
    ppermute x2, starting transfers between devices, over_chips(): lax.ppermute(total, 'op', [(i, i ^ step) for i in range(ops)])  2.93 us
    ppermute x1, starting transfers between devices, local(): two = lax.ppermute(first, ('sec', 'op'), crossing_too)  2.74 us
    ppermute x1, starting transfers between devices, with_distant(): lax.ppermute(sums, 'sec', [(s, s ^ step) for s in range(sectors)])  2.59 us
    ppermute x1, starting transfers between devices, local(): lax.ppermute(sums, 'sec', [(s, s ^ 2) for s in range(sectors)])  1.96 us
    ppermute x1, starting transfers between devices, local(): lax.ppermute(sums, 'sec', pairs)  1.94 us
  transfers between devices with their start and end apart: 17, of which 8 were waited for; matrix products, arithmetic and copies ran while one was open for 0% of the time, Pallas kernels for 20%

profile of v6, /device:TPU:0, one launch (start us, length us, event | category | flops | bytes accessed | tf_op | source)
XLA Modules:
  0.0 41.9 jit_solution(5319274430675262461)
XLA Ops:
  0.6 3.0 %collective-permute-start = (f32[256,256]{1,0:T(8,128)}, f32[256,256]{1,0:T(8,128)S(1)}, u32[]{:S(2)}, u32[]{:S(2)}) collective-permute-start(f32[256,256]{1,0:T(8,128)} %bitcast.1), channel_id=1, source_target_pairs={{1,5},{3,7},{5,1},{7,3},{9,13},{11,15},{13,9},{15,11},{17,21},{19,... | collective-permute-start | bytes 786440 | tf_op jit(solution)/shard_map/ppermute | solution.py:284
  5.0 0.1 pad_add_fusion.live_ref
  5.0 1.0 %shard_map.77 = (f32[128,256]{1,0:T(8,128)S(1)}, f32[128,256]{1,0:T(8,128)S(1)}, f32[128,256]{1,0:T(8,128)S(1)}, s32[8,128]{1,0:T(8,128)S(1)}) custom-call(f32[1,256,256]{2,1,0:T(8,128)} %state_ref.1, s32[2]{0:T(128)S(1)} %pad_add_fusion.live_ref), custom_call_target="tpu_custom_call" | custom-call | tf_op jit(solution)/shard_map/pallas_call | solution.py:22
  6.1 0.1 collective-permute-start.1
  6.1 2.4 %shard_map.78 = (f32[8,1,256,256]{3,2,1,0:T(8,128)S(1)}, f32[8,1,256,256]{3,2,1,0:T(8,128)S(1)}, s32[8,8,128]{2,1,0:T(8,128)S(1)}) custom-call(f32[8,1,256,256]{3,2,1,0:T(8,128)} %left_ref.1, f32[8,1,256,256]{3,2,1,0:T(8,128)} %right_ref.1, s32[8]{0:T(128)} %shift_ref.1, f32[128,256]{1,0:T(8,128)S(1)} %get-tuple-element.21.field_ref.refs_3_), custom_call_target="tpu_custom_call" | custom-call | bytes 4194304 | tf_op jit(solution)/shard_map/pallas_call | solution.py:22
  8.5 1.2 %collective-permute-done.1.refs_7_ = s32[8,128]{1,0:T(8,128)S(1)} collective-permute-done((s32[8,128]{1,0:T(8,128)S(1)}, s32[8,128]{1,0:T(8,128)S(1)}, u32[]{:S(2)}, u32[]{:S(2)}) %collective-permute-start.1) | collective-permute-done | bytes 4128 | tf_op jit(solution)/shard_map/ppermute | solution.py:296
  9.7 0.0 collective-permute-done.refs_5_
  9.7 0.0 collective-permute-start.2
  9.7 0.5 %collective-permute-start.3 = (s32[8,128]{1,0:T(8,128)S(1)}, s32[8,128]{1,0:T(8,128)S(1)}, u32[]{:S(2)}, u32[]{:S(2)}) collective-permute-start(s32[8,128]{1,0:T(8,128)S(1)} %collective-permute-done.1.refs_7_), channel_id=1, source_target_pairs={{0,1},{1,0},{2,3},{3,2},{4,5},{5,4},{6,7},{7,6},{8,9},{9,8},{10,11... | collective-permute-start | bytes 12296 | tf_op jit(solution)/shard_map/ppermute | solution.py:271
  10.3 1.0 %collective-permute-done.3.refs_8_ = s32[8,128]{1,0:T(8,128)S(1)} collective-permute-done((s32[8,128]{1,0:T(8,128)S(1)}, s32[8,128]{1,0:T(8,128)S(1)}, u32[]{:S(2)}, u32[]{:S(2)}) %collective-permute-start.3) | collective-permute-done | bytes 4128 | tf_op jit(solution)/shard_map/ppermute | solution.py:271
  11.3 0.0 collective-permute-done.2.refs_6_
  11.3 1.4 %shard_map.79 = (f32[128,256]{1,0:T(8,128)S(1)}, bf16[3,256,256]{2,1,0:T(8,128)(2,1)S(1)}, bf16[3,256,256]{2,1,0:T(8,128)(2,1)S(1)}) custom-call(s32[8,8,128]{2,1,0:T(8,128)S(1)} %get-tuple-element.22.refs_0_.shift_ref, f32[8,1,256,256]{3,2,1,0:T(8,128)S(1)} %get-tuple-element.26.refs_1_.left_ref, ...), custom_call_target="tpu_custom_call" | custom-call | flops 4026531840 | bytes 4194304 | tf_op jit(solution)/shard_map/pallas_call | solution.py:22
  12.7 0.2 collective-permute-start.4
  12.9 1.2 %shard_map.80 = f32[128,256]{1,0:T(8,128)S(1)} custom-call(s32[8,8,128]{2,1,0:T(8,128)S(1)} %get-tuple-element.22.refs_0_.shift_ref, f32[8,1,256,256]{3,2,1,0:T(8,128)S(1)} %get-tuple-element.26.refs_1_.left_ref, f32[8,1,256,256]{3,2,1,0:T(8,128)S(1)} %get-tuple-element.27.refs_2_.right_ref, bf16[3,256,256]{2,1,0:T(8,128)(2,1)S(1)} %get-tuple-element.31.high, ...), custom_call_target="tpu_custom_call" | custom-call | flops 4026531840 | bytes 4194304 | tf_op jit(solution)/shard_map/pallas_call | solution.py:22
  14.2 0.0 collective-permute-done.4
  14.2 1.3 %collective-permute-start.5 = (f32[128,256]{1,0:T(8,128)S(1)}, f32[128,256]{1,0:T(8,128)S(1)}, u32[]{:S(2)}, u32[]{:S(2)}) collective-permute-start(f32[128,256]{1,0:T(8,128)S(1)} %add.12), channel_id=1, source_target_pairs={{0,2},{1,3},{2,0},{3,1},{4,6},{5,7},{6,4},{7,5},{8,10},{9,11},{10,... | collective-permute-start | bytes 393224 | tf_op jit(solution)/shard_map/ppermute | solution.py:278
  15.5 4.5 %collective-permute-done.5 = f32[128,256]{1,0:T(8,128)S(1)} collective-permute-done((f32[128,256]{1,0:T(8,128)S(1)}, f32[128,256]{1,0:T(8,128)S(1)}, u32[]{:S(2)}, u32[]{:S(2)}) %collective-permute-start.5) | collective-permute-done | bytes 131104 | tf_op jit(solution)/shard_map/ppermute | solution.py:278
  20.1 0.1 collective-permute-start.7
  20.2 1.1 %collective-permute-start.10 = (f32[128,256]{1,0:T(8,128)S(1)}, f32[128,256]{1,0:T(8,128)S(1)}, u32[]{:S(2)}, u32[]{:S(2)}) collective-permute-start(f32[128,256]{1,0:T(8,128)S(1)} %add_multiply_fusion.first_ref.refs_3_), channel_id=1, source_target_pairs={{1,5},{3,7},{5,1},{7,3},{9,13},{11,15},{13,9},{15,11},{17,21},{19,... | collective-permute-start | bytes 393224 | tf_op jit(solution)/shard_map/ppermute | solution.py:305
  21.3 2.7 %collective-permute-start.6 = (f32[128,256]{1,0:T(8,128)S(1)}, f32[128,256]{1,0:T(8,128)S(1)}, u32[]{:S(2)}, u32[]{:S(2)}) collective-permute-start(f32[128,256]{1,0:T(8,128)S(1)} %add_multiply_fusion.first_ref.refs_3_), channel_id=1, source_target_pairs={{0,4},{2,6},{4,0},{6,2},{8,12},{10,14},{12,8},{14,10},{16,20},{18,... | collective-permute-start | bytes 393224 | tf_op jit(solution)/shard_map/ppermute | solution.py:306
  24.0 0.0 collective-permute-done.7.first_other_ref.refs_4_
  24.0 0.3 shard_map.81
  24.3 2.6 %collective-permute-start.8 = (f32[8,256]{1,0:T(8,128)S(1)}, f32[8,256]{1,0:T(8,128)S(1)}, u32[]{:S(2)}, u32[]{:S(2)}) collective-permute-start(f32[8,256]{1,0:T(8,128)S(1)} %shard_map.81), channel_id=1, source_target_pairs={{0,16},{4,20},{8,24},{12,28},{16,0},{20,4},{24,8},{28,12},{1,17},{... | collective-permute-start | bytes 24584 | tf_op jit(solution)/shard_map/ppermute | solution.py:311
  26.9 0.0 collective-permute-done.10.refs_5_
  26.9 0.7 %collective-permute-start.11 = (f32[128,256]{1,0:T(8,128)S(1)}, f32[128,256]{1,0:T(8,128)S(1)}, u32[]{:S(2)}, u32[]{:S(2)}) collective-permute-start(f32[128,256]{1,0:T(8,128)S(1)} %collective-permute-done.10.refs_5_), channel_id=1, source_target_pairs={{0,1},{1,0},{2,3},{3,2},{4,5},{5,4},{6,7},{7,6},{8,9},{9,8},{10,11... | collective-permute-start | bytes 393224 | tf_op jit(solution)/shard_map/ppermute | solution.py:271
  27.6 1.7 %collective-permute-done.8 = f32[8,256]{1,0:T(8,128)S(1)} collective-permute-done((f32[8,256]{1,0:T(8,128)S(1)}, f32[8,256]{1,0:T(8,128)S(1)}, u32[]{:S(2)}, u32[]{:S(2)}) %collective-permute-start.8) | collective-permute-done | bytes 8224 | tf_op jit(solution)/shard_map/ppermute | solution.py:311
  29.2 0.0 collective-permute-done.6.refs_7_
  29.2 0.0 collective-permute-start.12
  29.3 2.0 %collective-permute-start.9 = (f32[8,256]{1,0:T(8,128)S(1)}, f32[8,256]{1,0:T(8,128)S(1)}, u32[]{:S(2)}, u32[]{:S(2)}) collective-permute-start(f32[8,256]{1,0:T(8,128)S(1)} %add.14.a_ref), channel_id=1, source_target_pairs={{0,8},{4,12},{8,0},{12,4},{16,24},{20,28},{24,16},{28,20},{1,9},{5... | collective-permute-start | bytes 24584 | tf_op jit(solution)/shard_map/ppermute | solution.py:325
  31.2 0.0 collective-permute-done.11.refs_6_
  31.2 0.0 collective-permute-done.12.refs_8_
  31.2 1.3 %shard_map.82 = (f32[128,256]{1,0:T(8,128)S(1)}, bf16[3,256,256]{2,1,0:T(8,128)(2,1)S(1)}, bf16[3,256,256]{2,1,0:T(8,128)(2,1)S(1)}) custom-call(s32[8,8,128]{2,1,0:T(8,128)S(1)} %get-tuple-element.22.refs_0_.shift_ref, f32[8,1,256,256]{3,2,1,0:T(8,128)S(1)} %get-tuple-element.26.refs_1_.left_ref, ...), custom_call_target="tpu_custom_call" | custom-call | flops 4026531840 | bytes 4194304 | tf_op jit(solution)/shard_map/pallas_call | solution.py:22
  32.5 0.3 collective-permute-start.14
  32.8 0.2 collective-permute-done.9.b_ref
  33.0 1.2 %shard_map.86 = f32[128,256]{1,0:T(8,128)S(1)} custom-call(s32[8,8,128]{2,1,0:T(8,128)S(1)} %get-tuple-element.22.refs_0_.shift_ref, f32[8,1,256,256]{3,2,1,0:T(8,128)S(1)} %get-tuple-element.26.refs_1_.left_ref, f32[8,1,256,256]{3,2,1,0:T(8,128)S(1)} %get-tuple-element.27.refs_2_.right_ref, bf16[3,256,256]{2,1,0:T(8,128)(2,1)S(1)} %get-tuple-element.38.high, ...), custom_call_target="tpu_custom_call" | custom-call | flops 4026531840 | bytes 4194304 | tf_op jit(solution)/shard_map/pallas_call | solution.py:22
  34.1 0.0 collective-permute-done.14
  34.2 1.6 %collective-permute-start.15 = (f32[128,256]{1,0:T(8,128)S(1)}, f32[128,256]{1,0:T(8,128)S(1)}, u32[]{:S(2)}, u32[]{:S(2)}) collective-permute-start(f32[128,256]{1,0:T(8,128)S(1)} %add.15.total_ref), channel_id=1, source_target_pairs={{0,2},{1,3},{2,0},{3,1},{4,6},{5,7},{6,4},{7,5},{8,10},{9,11},{10,... | collective-permute-start | bytes 393224 | tf_op jit(solution)/shard_map/ppermute | solution.py:278
  35.8 1.9 %collective-permute-start.13 = (f32[8,256]{1,0:T(8,128)S(1)}, f32[8,256]{1,0:T(8,128)S(1)}, u32[]{:S(2)}, u32[]{:S(2)}) collective-permute-start(f32[8,256]{1,0:T(8,128)S(1)} %shard_map.83.refs_0_), channel_id=1, source_target_pairs={{0,4},{4,0},{8,12},{12,8},{16,20},{20,16},{24,28},{28,24},{1,5},{5... | collective-permute-start | bytes 24584 | tf_op jit(solution)/shard_map/ppermute | solution.py:335
  37.7 1.7 %collective-permute-done.13.refs_1_ = f32[8,256]{1,0:T(8,128)S(1)} collective-permute-done((f32[8,256]{1,0:T(8,128)S(1)}, f32[8,256]{1,0:T(8,128)S(1)}, u32[]{:S(2)}, u32[]{:S(2)}) %collective-permute-start.13) | collective-permute-done | bytes 8224 | tf_op jit(solution)/shard_map/ppermute | solution.py:335
  39.4 0.3 shard_map.84.merged_ref
  39.7 0.1 collective-permute-done.15.peer_ref
  39.8 0.1 collective-permute-start.16
  39.9 0.7 %shard_map.85 = f32[1,256,256]{2,1,0:T(8,128)} custom-call(f32[8,256]{1,0:T(8,128)S(1)} %shard_map.84.merged_ref, f32[128,256]{1,0:T(8,128)S(1)} %add_multiply_fusion.first_ref.refs_3_, f32[128,256]{1,0:T(8,128)S(1)} %collective-permute-done.7.first_other_ref.refs_4_, f32[128,256]{1,0:T(8,128)S(1)} %get-tuple-element.21.field_ref.refs_3_, ...), custom_call_target="tpu_custom_call" | custom-call | tf_op jit(solution)/shard_map/pallas_call | solution.py:22
  40.6 0.6 %collective-permute-done.16.other_ref = f32[128,256]{1,0:T(8,128)S(1)} collective-permute-done((f32[128,256]{1,0:T(8,128)S(1)}, f32[128,256]{1,0:T(8,128)S(1)}, u32[]{:S(2)}, u32[]{:S(2)}) %collective-permute-start.16) | collective-permute-done | bytes 131104 | tf_op jit(solution)/shard_map/ppermute | solution.py:271
  41.2 0.7 %shard_map.88 = f32[1,256,256]{2,1,0:T(8,128)} custom-call(f32[128,256]{1,0:T(8,128)S(1)} %shard_map.87.mine_ref, f32[128,256]{1,0:T(8,128)S(1)} %collective-permute-done.16.other_ref), custom_call_target="tpu_custom_call" | custom-call | tf_op jit(solution)/shard_map/pallas_call | solution.py:22
  (6 shorter events, 0.1 us)
Async XLA Ops:
  0.6 9.1 %collective-permute-start = (f32[256,256]{1,0:T(8,128)}, f32[256,256]{1,0:T(8,128)S(1)}, u32[]{:S(2)}, u32[]{:S(2)}) collective-permute-start(f32[256,256]{1,0:T(8,128)} %bitcast.1), channel_id=1, source_target_pairs={{1,5},{3,7},{5,1},{7,3},{9,13},{11,15},{13,9},{15,11},{17,21},{19,... | collective-permute-start | bytes 786440 | tf_op jit(solution)/shard_map/ppermute | solution.py:284
  6.1 3.7 %collective-permute-start.1 = (s32[8,128]{1,0:T(8,128)S(1)}, s32[8,128]{1,0:T(8,128)S(1)}, u32[]{:S(2)}, u32[]{:S(2)}) collective-permute-start(s32[8,128]{1,0:T(8,128)S(1)} %get-tuple-element.25), channel_id=1, source_target_pairs={{1,5},{3,7},{5,1},{7,3},{9,13},{11,15},{13,9},{15,11},{17,21},{19,... | collective-permute-start | bytes 12296 | tf_op jit(solution)/shard_map/ppermute | solution.py:296
  9.7 1.5 %collective-permute-start.2 = (f32[256,256]{1,0:T(8,128)S(1)}, f32[256,256]{1,0:T(8,128)S(1)}, u32[]{:S(2)}, u32[]{:S(2)}) collective-permute-start(f32[256,256]{1,0:T(8,128)S(1)} %collective-permute-done.refs_5_), channel_id=1, source_target_pairs={{0,1},{1,0},{2,3},{3,2},{4,5},{5,4},{6,7},{7,6},{8,9},{9,8},{10,11... | collective-permute-start | bytes 786440 | tf_op jit(solution)/shard_map/ppermute | solution.py:271
  9.7 1.5 %collective-permute-start.3 = (s32[8,128]{1,0:T(8,128)S(1)}, s32[8,128]{1,0:T(8,128)S(1)}, u32[]{:S(2)}, u32[]{:S(2)}) collective-permute-start(s32[8,128]{1,0:T(8,128)S(1)} %collective-permute-done.1.refs_7_), channel_id=1, source_target_pairs={{0,1},{1,0},{2,3},{3,2},{4,5},{5,4},{6,7},{7,6},{8,9},{9,8},{10,11... | collective-permute-start | bytes 12296 | tf_op jit(solution)/shard_map/ppermute | solution.py:271
  12.7 1.4 %collective-permute-start.4 = (f32[128,256]{1,0:T(8,128)S(1)}, f32[128,256]{1,0:T(8,128)S(1)}, u32[]{:S(2)}, u32[]{:S(2)}) collective-permute-start(f32[128,256]{1,0:T(8,128)S(1)} %get-tuple-element.33), channel_id=1, source_target_pairs={{0,1},{1,0},{2,3},{3,2},{4,5},{5,4},{6,7},{7,6},{8,9},{9,8},{10,11... | collective-permute-start | bytes 393224 | tf_op jit(solution)/shard_map/ppermute | solution.py:271
  14.2 5.8 %collective-permute-start.5 = (f32[128,256]{1,0:T(8,128)S(1)}, f32[128,256]{1,0:T(8,128)S(1)}, u32[]{:S(2)}, u32[]{:S(2)}) collective-permute-start(f32[128,256]{1,0:T(8,128)S(1)} %add.12), channel_id=1, source_target_pairs={{0,2},{1,3},{2,0},{3,1},{4,6},{5,7},{6,4},{7,5},{8,10},{9,11},{10,... | collective-permute-start | bytes 393224 | tf_op jit(solution)/shard_map/ppermute | solution.py:278
  20.1 3.9 %collective-permute-start.7 = (f32[128,256]{1,0:T(8,128)S(1)}, f32[128,256]{1,0:T(8,128)S(1)}, u32[]{:S(2)}, u32[]{:S(2)}) collective-permute-start(f32[128,256]{1,0:T(8,128)S(1)} %add_multiply_fusion.first_ref.refs_3_), channel_id=1, source_target_pairs={{0,1},{1,0},{2,3},{3,2},{4,5},{5,4},{6,7},{7,6},{8,9},{9,8},{10,11... | collective-permute-start | bytes 393224 | tf_op jit(solution)/shard_map/ppermute | solution.py:271
  20.2 6.7 %collective-permute-start.10 = (f32[128,256]{1,0:T(8,128)S(1)}, f32[128,256]{1,0:T(8,128)S(1)}, u32[]{:S(2)}, u32[]{:S(2)}) collective-permute-start(f32[128,256]{1,0:T(8,128)S(1)} %add_multiply_fusion.first_ref.refs_3_), channel_id=1, source_target_pairs={{1,5},{3,7},{5,1},{7,3},{9,13},{11,15},{13,9},{15,11},{17,21},{19,... | collective-permute-start | bytes 393224 | tf_op jit(solution)/shard_map/ppermute | solution.py:305
  21.3 8.0 %collective-permute-start.6 = (f32[128,256]{1,0:T(8,128)S(1)}, f32[128,256]{1,0:T(8,128)S(1)}, u32[]{:S(2)}, u32[]{:S(2)}) collective-permute-start(f32[128,256]{1,0:T(8,128)S(1)} %add_multiply_fusion.first_ref.refs_3_), channel_id=1, source_target_pairs={{0,4},{2,6},{4,0},{6,2},{8,12},{10,14},{12,8},{14,10},{16,20},{18,... | collective-permute-start | bytes 393224 | tf_op jit(solution)/shard_map/ppermute | solution.py:306
  24.3 5.0 %collective-permute-start.8 = (f32[8,256]{1,0:T(8,128)S(1)}, f32[8,256]{1,0:T(8,128)S(1)}, u32[]{:S(2)}, u32[]{:S(2)}) collective-permute-start(f32[8,256]{1,0:T(8,128)S(1)} %shard_map.81), channel_id=1, source_target_pairs={{0,16},{4,20},{8,24},{12,28},{16,0},{20,4},{24,8},{28,12},{1,17},{... | collective-permute-start | bytes 24584 | tf_op jit(solution)/shard_map/ppermute | solution.py:311
  26.9 4.4 %collective-permute-start.11 = (f32[128,256]{1,0:T(8,128)S(1)}, f32[128,256]{1,0:T(8,128)S(1)}, u32[]{:S(2)}, u32[]{:S(2)}) collective-permute-start(f32[128,256]{1,0:T(8,128)S(1)} %collective-permute-done.10.refs_5_), channel_id=1, source_target_pairs={{0,1},{1,0},{2,3},{3,2},{4,5},{5,4},{6,7},{7,6},{8,9},{9,8},{10,11... | collective-permute-start | bytes 393224 | tf_op jit(solution)/shard_map/ppermute | solution.py:271
  29.2 2.0 %collective-permute-start.12 = (f32[128,256]{1,0:T(8,128)S(1)}, f32[128,256]{1,0:T(8,128)S(1)}, u32[]{:S(2)}, u32[]{:S(2)}) collective-permute-start(f32[128,256]{1,0:T(8,128)S(1)} %collective-permute-done.6.refs_7_), channel_id=1, source_target_pairs={{0,1},{1,0},{2,3},{3,2},{4,5},{5,4},{6,7},{7,6},{8,9},{9,8},{10,11... | collective-permute-start | bytes 393224 | tf_op jit(solution)/shard_map/ppermute | solution.py:271
  29.3 3.7 %collective-permute-start.9 = (f32[8,256]{1,0:T(8,128)S(1)}, f32[8,256]{1,0:T(8,128)S(1)}, u32[]{:S(2)}, u32[]{:S(2)}) collective-permute-start(f32[8,256]{1,0:T(8,128)S(1)} %add.14.a_ref), channel_id=1, source_target_pairs={{0,8},{4,12},{8,0},{12,4},{16,24},{20,28},{24,16},{28,20},{1,9},{5... | collective-permute-start | bytes 24584 | tf_op jit(solution)/shard_map/ppermute | solution.py:325
  32.5 1.6 %collective-permute-start.14 = (f32[128,256]{1,0:T(8,128)S(1)}, f32[128,256]{1,0:T(8,128)S(1)}, u32[]{:S(2)}, u32[]{:S(2)}) collective-permute-start(f32[128,256]{1,0:T(8,128)S(1)} %get-tuple-element.37.after_ref), channel_id=1, source_target_pairs={{0,1},{1,0},{2,3},{3,2},{4,5},{5,4},{6,7},{7,6},{8,9},{9,8},{10,11... | collective-permute-start | bytes 393224 | tf_op jit(solution)/shard_map/ppermute | solution.py:271
  34.2 5.6 %collective-permute-start.15 = (f32[128,256]{1,0:T(8,128)S(1)}, f32[128,256]{1,0:T(8,128)S(1)}, u32[]{:S(2)}, u32[]{:S(2)}) collective-permute-start(f32[128,256]{1,0:T(8,128)S(1)} %add.15.total_ref), channel_id=1, source_target_pairs={{0,2},{1,3},{2,0},{3,1},{4,6},{5,7},{6,4},{7,5},{8,10},{9,11},{10,... | collective-permute-start | bytes 393224 | tf_op jit(solution)/shard_map/ppermute | solution.py:278
  35.8 3.7 %collective-permute-start.13 = (f32[8,256]{1,0:T(8,128)S(1)}, f32[8,256]{1,0:T(8,128)S(1)}, u32[]{:S(2)}, u32[]{:S(2)}) collective-permute-start(f32[8,256]{1,0:T(8,128)S(1)} %shard_map.83.refs_0_), channel_id=1, source_target_pairs={{0,4},{4,0},{8,12},{12,8},{16,20},{20,16},{24,28},{28,24},{1,5},{5... | collective-permute-start | bytes 24584 | tf_op jit(solution)/shard_map/ppermute | solution.py:335
  39.8 1.4 %collective-permute-start.16 = (f32[128,256]{1,0:T(8,128)S(1)}, f32[128,256]{1,0:T(8,128)S(1)}, u32[]{:S(2)}, u32[]{:S(2)}) collective-permute-start(f32[128,256]{1,0:T(8,128)S(1)} %shard_map.87.mine_ref), channel_id=1, source_target_pairs={{0,1},{1,0},{2,3},{3,2},{4,5},{5,4},{6,7},{7,6},{8,9},{9,8},{10,11... | collective-permute-start | bytes 393224 | tf_op jit(solution)/shard_map/ppermute | solution.py:271

commit v7 on v6

--- a/solution.py
+++ b/solution.py
@@ -56,7 +56,7 @@
     return (row < rows) & (lax.broadcasted_iota(jnp.int32, shape, 1) < cols)
 
 
-def field_kernel(state_ref, live_ref, field_ref, other_ref, mask_ref, live_out, state, live, sems):
+def field_kernel(state_ref, live_ref, field_ref, other_ref, mask_ref, mask_other_ref, live_out, state, live, sems):
     copies = [
         pltpu.make_async_copy(ref, buffer, sems.at[i])
         for i, (ref, buffer) in enumerate(((state_ref, state), (live_ref, live)))
@@ -71,7 +71,8 @@
     for which, ref in ((core, field_ref), (1 - core, other_ref)):
         start = which * half
         ref[...] = jnp.where(inside(ref.shape, start, rows, cols), state[0, rows_of(which, half)], 0.0)
-    mask_ref[...] = jnp.where(inside(mask_ref.shape, core * half, rows, cols), 1.0, 0.0)
+    for which, ref in ((core, mask_ref), (1 - core, mask_other_ref)):
+        ref[...] = jnp.where(inside(ref.shape, which * half, rows, cols), 1.0, 0.0)
     row = lax.broadcasted_iota(jnp.int32, live_out.shape, 0)
     live_out[...] = jnp.where(row == 0, rows, cols)
 
@@ -116,6 +117,11 @@
     )
 
 
+def live_kernel(block_ref, live_ref, out_ref):
+    live = inside(block_ref.shape, 0, live_ref[:1, :1], live_ref[1:2, :1])
+    out_ref[...] = jnp.where(live, block_ref[...], 0.0)
+
+
 def half_product(which, shift_ref, high, low, left_ref, right_ref):
     half = left_ref.shape[2] // 2
     rows = rows_of(which, half)
@@ -150,9 +156,8 @@
 
     put(1, own_ref, own_other_ref)
     if raw:
-        for index, ref, live_ref in zip((got, 2 - got), refs[:2], refs[2:]):
-            live = inside((block, block), 0, live_ref[:1, :1], live_ref[1:2, :1])
-            high[index], low[index] = split(jnp.where(live, ref[...], 0.0))
+        for index, ref in zip((got, 2 - got), refs):
+            high[index], low[index] = split(ref[...])
     else:
         one_ref, one_other_ref, two_ref, two_other_ref = refs
         put(got, one_ref, two_other_ref)
@@ -175,12 +180,12 @@
     refs[-1][...] = half_product(core_index(), shift_ref, high, low, left_ref, right_ref)
 
 
-def product_options(left):
+def product_options(left, count=30):
     terms, _, block, _ = left.shape
     return dict(
         mib=16,
         cost_estimate=pl.CostEstimate(
-            flops=30 * terms * block**3, bytes_accessed=8 * left.size, transcendentals=0
+            flops=count * terms * block**3, bytes_accessed=8 * left.size, transcendentals=0
         ),
     )
 
@@ -201,7 +206,7 @@
     block = left.shape[-1]
     arrays = [shift, left, right, high, low, *after]
     return call(
-        keep_kernel, f32(block // 2, block), [VMEM] * len(arrays), *arrays, **product_options(left)
+        keep_kernel, f32(block // 2, block), [VMEM] * len(arrays), *arrays, **product_options(left, 1)
     )
 
 
@@ -218,6 +223,10 @@
     out_ref[...] = jnp.where(lane == lax.axis_index("sec"), values, 0.0)
 
 
+def added_after_kernel(a_ref, b_ref, after_ref, out_ref):
+    out_ref[...] = a_ref[...] + b_ref[...]
+
+
 def added_kernel(a_ref, b_ref, after_ref, out_ref):
     out_ref[...] = a_ref[...] + b_ref[...]
 
@@ -233,12 +242,6 @@
     out_ref[...] = jnp.where(row == 0, theta, scale)
 
 
-def image_kernel(merged_ref, total_ref, peer_ref, mask_ref, first_ref, out_ref):
-    theta, scale = merged_ref[0:1, :], merged_ref[1:2, :]
-    total = (total_ref[...] + peer_ref[...]) * mask_ref[...]
-    out_ref[...] = scale * (total - theta * first_ref[...])
-
-
 def correction_kernel(merged_ref, first_ref, first_other_ref, field_ref, field_other_ref, out_ref):
     half = first_ref.shape[0]
     core = core_index()
@@ -247,11 +250,14 @@
     out_ref[0, rows_of(1 - core, half)] = scale * (first_other_ref[...] - theta * field_other_ref[...])
 
 
-def output_kernel(mine_ref, other_ref, out_ref):
-    half = mine_ref.shape[0]
+def image_kernel(merged_ref, *refs):
+    *refs, out_ref = refs
+    half = refs[0].shape[0]
     core = core_index()
-    out_ref[0, rows_of(core, half)] = mine_ref[...]
-    out_ref[0, rows_of(1 - core, half)] = other_ref[...]
+    theta, scale = merged_ref[0:1, :], merged_ref[1:2, :]
+    for which, (total, peer, mask, first) in ((core, refs[:4]), (1 - core, refs[4:])):
+        product = (total[...] + peer[...]) * mask[...]
+        out_ref[0, rows_of(which, half)] = scale * (product - theta * first[...])
 
 
 def local(state, left_ops, right_ops, term_shift, sector_rows, sector_cols):
@@ -282,9 +288,9 @@
     crossing_too = [(s * ops + a, (s ^ 1) * ops + a) for s in range(sectors) for a in range(0, ops, 2)]
     crossing_too += [(source, target) for source, target in between if source % 2]
     got = lax.ppermute(state[0], ("sec", "op"), crossing)
-    field, field_other, mask, live = call(
+    field, field_other, mask, mask_other, live = call(
         field_kernel,
-        [f32(half, block)] * 3 + [jax.ShapeDtypeStruct((8, 128), jnp.int32)],
+        [f32(half, block)] * 4 + [jax.ShapeDtypeStruct((8, 128), jnp.int32)],
         [HBM] * 2,
         in_hbm(state), jnp.concatenate([sector_rows, sector_cols]),
         scratch_shapes=[
@@ -296,8 +302,9 @@
     live = lax.ppermute(live, ("sec", "op"), crossing)
     left, right, shift = load(left_ops, right_ops, term_shift, field)
     got, left, right, live = lax.optimization_barrier((got, left, right, live))
+    got = call(live_kernel, f32(block, block), [VMEM] * 2, got, live)
     send, *parts = product_to_send(
-        shift, left, right, field, field_other, got, swapped(got), live, swapped(live), raw=True
+        shift, left, right, field, field_other, got, swapped(got), raw=True
     )
     total, peer = over_chips(product_to_keep(shift, left, right, *parts) + swapped(send))
 
@@ -318,30 +325,39 @@
     send, *parts = product_to_send(
         shift, left, right, first, first_other, one, swapped(one), two, swapped(two)
     )
+    keep = product_to_keep(shift, left, right, *parts)
     sums = call(
         added_kernel,
         f32(EXTRA, block),
         [VMEM] * 3,
-        sums, lax.ppermute(sums, "sec", [(s, s ^ 2) for s in range(sectors)]), send,
-    )
-    keep = product_to_keep(shift, left, right, *parts, sums)
-    total, peer = over_chips(keep + swapped(send))
-
+        sums, lax.ppermute(sums, "sec", [(s, s ^ 2) for s in range(sectors)]), keep,
+        cost_estimate=pl.CostEstimate(flops=10**10, bytes_accessed=0, transcendentals=0),
+    )
+    total, peer = over_chips(
+        call(added_after_kernel, f32(half, block), [VMEM] * 3, keep, swapped(send), sums)
+    )
+
+    pair_sums = lax.ppermute(sums, "sec", pairs)
+    peer, pair_sums = lax.optimization_barrier((peer, pair_sums))
     cells = sectors * block * block
     merged = call(
         lambda *refs: merged_kernel(cells, *refs),
         f32(EXTRA, block),
         [VMEM] * 2,
-        sums, lax.ppermute(sums, "sec", pairs),
-    )
-    image = call(image_kernel, f32(half, block), [VMEM] * 5, merged, total, peer, mask, first)
+        sums, pair_sums,
+    )
     correction = call(
         correction_kernel,
         f32(1, block, block),
         [VMEM] * 5,
         merged, first, first_other, field, field_other,
     )
-    image = call(output_kernel, f32(1, block, block), [VMEM] * 2, image, swapped(image))
+    image = call(
+        image_kernel,
+        f32(1, block, block),
+        [VMEM] * 9,
+        merged, total, peer, mask, first, swapped(total), swapped(peer), mask_other, first_other,
+    )
     return correction, image
 
 

time: 42.1 us -> 42 us (level)
  waiting for transfers between devices: 11 us -> 11.9 us
  starting transfers between devices: 18.2 us -> 17.4 us
    ppermute x8, starting transfers between devices: 1.87 us -> 1.36 us  [swapped(): return lax.ppermute(v, 'op', others)]
    ppermute x2, waiting for transfers between devices: 4.58 us -> 5.03 us  [over_chips(): lax.ppermute(total, 'op', [(i, i ^ step) for i in range(ops)])]
    pallas_call x12 -> x13, Pallas kernels: 10.5 us -> 10.4 us  [call(): pl.pallas_call(kernel, out_shape=out_shape, in_specs=in_specs, out_specs=...]
  transfers between devices with their start and end apart: 17 -> 17, of which waited for: 8 -> 7; matrix products, arithmetic and copies ran while one was open for 0% -> 0% of each run, Pallas kernels for 20% -> 20%
where the time goes in v7:
time: 42 us; the launch traced here: 41.8 us
  starting transfers between devices  17.4 us (41%)
  waiting for transfers between devices  11.9 us (28%)
  Pallas kernels  10.4 us (25%)
  between operations  2.06 us (5%)
    pallas_call x13, Pallas kernels, call(): pl.pallas_call(kernel, out_shape=out_shape, in_specs=in_specs, out_specs=...  10.4 us
    ppermute x2, waiting for transfers between devices, over_chips(): lax.ppermute(total, 'op', [(i, i ^ step) for i in range(ops)])  5.03 us
    ppermute x1, starting transfers between devices, local(): got = lax.ppermute(state[0], ('sec', 'op'), crossing)  3.03 us
    ppermute x2, starting transfers between devices, over_chips(): lax.ppermute(total, 'op', [(i, i ^ step) for i in range(ops)])  2.88 us
    ppermute x1, starting transfers between devices, local(): two = lax.ppermute(first, ('sec', 'op'), crossing_too)  2.73 us
    ppermute x1, starting transfers between devices, with_distant(): lax.ppermute(sums, 'sec', [(s, s ^ step) for s in range(sectors)])  2.59 us
    ppermute x1, waiting for transfers between devices, local(): pair_sums = lax.ppermute(sums, 'sec', pairs)  2.04 us
    ppermute x1, starting transfers between devices, local(): lax.ppermute(sums, 'sec', [(s, s ^ 2) for s in range(sectors)])  1.96 us
  transfers between devices with their start and end apart: 17, of which 7 were waited for; matrix products, arithmetic and copies ran while one was open for 0% of the time, Pallas kernels for 20%

profile of v7, /device:TPU:0, one launch (start us, length us, event | category | flops | bytes accessed | tf_op | source)
XLA Modules:
  0.0 41.8 jit_solution(6429419877785917135)
XLA Ops:
  0.6 3.0 %collective-permute-start = (f32[256,256]{1,0:T(8,128)}, f32[256,256]{1,0:T(8,128)S(1)}, u32[]{:S(2)}, u32[]{:S(2)}) collective-permute-start(f32[256,256]{1,0:T(8,128)} %bitcast.1), channel_id=1, source_target_pairs={{1,5},{3,7},{5,1},{7,3},{9,13},{11,15},{13,9},{15,11},{17,21},{19,... | collective-permute-start | bytes 786440 | tf_op jit(solution)/shard_map/ppermute | solution.py:290
  5.0 0.1 pad_add_fusion.live_ref
  5.0 1.0 %shard_map.77 = (f32[128,256]{1,0:T(8,128)S(1)}, f32[128,256]{1,0:T(8,128)S(1)}, f32[128,256]{1,0:T(8,128)S(1)}, f32[128,256]{1,0:T(8,128)S(1)}, s32[8,128]{1,0:T(8,128)S(1)}) custom-call(f32[1,256,256]{2,1,0:T(8,128)} %state_ref.1, s32[2]{0:T(128)S(1)} %pad_add_fusion.live_ref), custom_call_target="tpu_custom_call" | custom-call | tf_op jit(solution)/shard_map/pallas_call | solution.py:22
  6.1 0.1 collective-permute-start.1
  6.2 2.4 %shard_map.78 = (f32[8,1,256,256]{3,2,1,0:T(8,128)S(1)}, f32[8,1,256,256]{3,2,1,0:T(8,128)S(1)}, s32[8,8,128]{2,1,0:T(8,128)S(1)}) custom-call(f32[8,1,256,256]{3,2,1,0:T(8,128)} %left_ref.1, f32[8,1,256,256]{3,2,1,0:T(8,128)} %right_ref.1, s32[8]{0:T(128)} %shift_ref.1, f32[128,256]{1,0:T(8,128)S(1)} %get-tuple-element.24.field_ref.refs_3_), custom_call_target="tpu_custom_call" | custom-call | bytes 4194304 | tf_op jit(solution)/shard_map/pallas_call | solution.py:22
  8.5 1.2 %collective-permute-done.1.live_ref = s32[8,128]{1,0:T(8,128)S(1)} collective-permute-done((s32[8,128]{1,0:T(8,128)S(1)}, s32[8,128]{1,0:T(8,128)S(1)}, u32[]{:S(2)}, u32[]{:S(2)}) %collective-permute-start.1) | collective-permute-done | bytes 4128 | tf_op jit(solution)/shard_map/ppermute | solution.py:302
  9.8 0.0 collective-permute-done.block_ref
  9.8 0.1 shard_map.79.refs_5_
  9.8 0.1 collective-permute-start.2
  9.9 1.5 %collective-permute-done.2.refs_6_ = f32[256,256]{1,0:T(8,128)S(1)} collective-permute-done((f32[256,256]{1,0:T(8,128)S(1)}, f32[256,256]{1,0:T(8,128)S(1)}, u32[]{:S(2)}, u32[]{:S(2)}) %collective-permute-start.2) | collective-permute-done | bytes 262176 | tf_op jit(solution)/shard_map/ppermute | solution.py:277
  11.4 1.3 %shard_map.80 = (f32[128,256]{1,0:T(8,128)S(1)}, bf16[3,256,256]{2,1,0:T(8,128)(2,1)S(1)}, bf16[3,256,256]{2,1,0:T(8,128)(2,1)S(1)}) custom-call(s32[8,8,128]{2,1,0:T(8,128)S(1)} %get-tuple-element.25.refs_0_.shift_ref, f32[8,1,256,256]{3,2,1,0:T(8,128)S(1)} %get-tuple-element.29.refs_1_.left_ref, ...), custom_call_target="tpu_custom_call" | custom-call | flops 4026531840 | bytes 4194304 | tf_op jit(solution)/shard_map/pallas_call | solution.py:22
  12.7 0.2 collective-permute-start.3
  12.9 1.2 %shard_map.81 = f32[128,256]{1,0:T(8,128)S(1)} custom-call(s32[8,8,128]{2,1,0:T(8,128)S(1)} %get-tuple-element.25.refs_0_.shift_ref, f32[8,1,256,256]{3,2,1,0:T(8,128)S(1)} %get-tuple-element.29.refs_1_.left_ref, f32[8,1,256,256]{3,2,1,0:T(8,128)S(1)} %get-tuple-element.30.refs_2_.right_ref, bf16[3,256,256]{2,1,0:T(8,128)(2,1)S(1)} %get-tuple-element.34.high, ...), custom_call_target="tpu_custom_call" | custom-call | flops 134217728 | bytes 4194304 | tf_op jit(solution)/shard_map/pallas_call | solution.py:22
  14.1 0.0 collective-permute-done.3
  14.2 1.3 %collective-permute-start.4 = (f32[128,256]{1,0:T(8,128)S(1)}, f32[128,256]{1,0:T(8,128)S(1)}, u32[]{:S(2)}, u32[]{:S(2)}) collective-permute-start(f32[128,256]{1,0:T(8,128)S(1)} %add.9), channel_id=1, source_target_pairs={{0,2},{1,3},{2,0},{3,1},{4,6},{5,7},{6,4},{7,5},{8,10},{9,11},{10,... | collective-permute-start | bytes 393224 | tf_op jit(solution)/shard_map/ppermute | solution.py:284
  15.5 4.5 %collective-permute-done.4 = f32[128,256]{1,0:T(8,128)S(1)} collective-permute-done((f32[128,256]{1,0:T(8,128)S(1)}, f32[128,256]{1,0:T(8,128)S(1)}, u32[]{:S(2)}, u32[]{:S(2)}) %collective-permute-start.4) | collective-permute-done | bytes 131104 | tf_op jit(solution)/shard_map/ppermute | solution.py:284
  20.0 0.1 collective-permute-start.6
  20.1 1.1 %collective-permute-start.9 = (f32[128,256]{1,0:T(8,128)S(1)}, f32[128,256]{1,0:T(8,128)S(1)}, u32[]{:S(2)}, u32[]{:S(2)}) collective-permute-start(f32[128,256]{1,0:T(8,128)S(1)} %add_multiply_fusion.first_ref.refs_3_), channel_id=1, source_target_pairs={{1,5},{3,7},{5,1},{7,3},{9,13},{11,15},{13,9},{15,11},{17,21},{19,... | collective-permute-start | bytes 393224 | tf_op jit(solution)/shard_map/ppermute | solution.py:312
  21.2 2.7 %collective-permute-start.5 = (f32[128,256]{1,0:T(8,128)S(1)}, f32[128,256]{1,0:T(8,128)S(1)}, u32[]{:S(2)}, u32[]{:S(2)}) collective-permute-start(f32[128,256]{1,0:T(8,128)S(1)} %add_multiply_fusion.first_ref.refs_3_), channel_id=1, source_target_pairs={{0,4},{2,6},{4,0},{6,2},{8,12},{10,14},{12,8},{14,10},{16,20},{18,... | collective-permute-start | bytes 393224 | tf_op jit(solution)/shard_map/ppermute | solution.py:313
  23.9 0.0 collective-permute-done.6.first_other_ref.refs_4_.refs_7_
  23.9 0.3 shard_map.82
  24.2 2.6 %collective-permute-start.7 = (f32[8,256]{1,0:T(8,128)S(1)}, f32[8,256]{1,0:T(8,128)S(1)}, u32[]{:S(2)}, u32[]{:S(2)}) collective-permute-start(f32[8,256]{1,0:T(8,128)S(1)} %shard_map.82), channel_id=1, source_target_pairs={{0,16},{4,20},{8,24},{12,28},{16,0},{20,4},{24,8},{28,12},{1,17},{... | collective-permute-start | bytes 24584 | tf_op jit(solution)/shard_map/ppermute | solution.py:318
  26.8 0.0 collective-permute-done.9.refs_5_
  26.8 0.7 %collective-permute-start.10 = (f32[128,256]{1,0:T(8,128)S(1)}, f32[128,256]{1,0:T(8,128)S(1)}, u32[]{:S(2)}, u32[]{:S(2)}) collective-permute-start(f32[128,256]{1,0:T(8,128)S(1)} %collective-permute-done.9.refs_5_), channel_id=1, source_target_pairs={{0,1},{1,0},{2,3},{3,2},{4,5},{5,4},{6,7},{7,6},{8,9},{9,8},{10,11... | collective-permute-start | bytes 393224 | tf_op jit(solution)/shard_map/ppermute | solution.py:277
  27.5 1.7 %collective-permute-done.7 = f32[8,256]{1,0:T(8,128)S(1)} collective-permute-done((f32[8,256]{1,0:T(8,128)S(1)}, f32[8,256]{1,0:T(8,128)S(1)}, u32[]{:S(2)}, u32[]{:S(2)}) %collective-permute-start.7) | collective-permute-done | bytes 8224 | tf_op jit(solution)/shard_map/ppermute | solution.py:318
  29.2 0.0 collective-permute-done.5.refs_7_
  29.2 0.0 collective-permute-start.11
  29.2 2.0 %collective-permute-start.8 = (f32[8,256]{1,0:T(8,128)S(1)}, f32[8,256]{1,0:T(8,128)S(1)}, u32[]{:S(2)}, u32[]{:S(2)}) collective-permute-start(f32[8,256]{1,0:T(8,128)S(1)} %add.11.a_ref), channel_id=1, source_target_pairs={{0,8},{4,12},{8,0},{12,4},{16,24},{20,28},{24,16},{28,20},{1,9},{5... | collective-permute-start | bytes 24584 | tf_op jit(solution)/shard_map/ppermute | solution.py:333
  31.1 0.0 collective-permute-done.10.refs_6_
  31.1 0.0 collective-permute-done.11.refs_8_
  31.2 1.3 %shard_map.83 = (f32[128,256]{1,0:T(8,128)S(1)}, bf16[3,256,256]{2,1,0:T(8,128)(2,1)S(1)}, bf16[3,256,256]{2,1,0:T(8,128)(2,1)S(1)}) custom-call(s32[8,8,128]{2,1,0:T(8,128)S(1)} %get-tuple-element.25.refs_0_.shift_ref, f32[8,1,256,256]{3,2,1,0:T(8,128)S(1)} %get-tuple-element.29.refs_1_.left_ref, ...), custom_call_target="tpu_custom_call" | custom-call | flops 4026531840 | bytes 4194304 | tf_op jit(solution)/shard_map/pallas_call | solution.py:22
  32.4 0.3 collective-permute-start.12
  32.7 1.2 %shard_map.84.after_ref.a_ref = f32[128,256]{1,0:T(8,128)S(1)} custom-call(s32[8,8,128]{2,1,0:T(8,128)S(1)} %get-tuple-element.25.refs_0_.shift_ref, f32[8,1,256,256]{3,2,1,0:T(8,128)S(1)} %get-tuple-element.29.refs_1_.left_ref, f32[8,1,256,256]{3,2,1,0:T(8,128)S(1)} %get-tuple-element.30.refs_2_.right_ref, bf16[3,256,256]{2,1,0:T(8,128)(2,1)S(1)} %get-tuple-element.40.high, ...), custom_call_target="tpu_custom_call" | custom-call | flops 134217728 | bytes 4194304 | tf_op jit(solution)/shard_map/pallas_call | solution.py:22
  33.9 0.0 collective-permute-done.8.b_ref
  33.9 0.0 collective-permute-done.12.b_ref
  33.9 1.6 %collective-permute-start.13 = (f32[128,256]{1,0:T(8,128)S(1)}, f32[128,256]{1,0:T(8,128)S(1)}, u32[]{:S(2)}, u32[]{:S(2)}) collective-permute-start(f32[128,256]{1,0:T(8,128)S(1)} %shard_map.86.refs_0_), channel_id=1, source_target_pairs={{0,2},{1,3},{2,0},{3,1},{4,6},{5,7},{6,4},{7,5},{8,10},{9,11},{10,... | collective-permute-start | bytes 393224 | tf_op jit(solution)/shard_map/ppermute | solution.py:284
  35.5 1.6 %collective-permute-start.14 = (f32[8,256]{1,0:T(8,128)S(1)}, f32[8,256]{1,0:T(8,128)S(1)}, u32[]{:S(2)}, u32[]{:S(2)}) collective-permute-start(f32[8,256]{1,0:T(8,128)S(1)} %shard_map.85.after_ref.refs_0_), channel_id=1, source_target_pairs={{0,4},{4,0},{8,12},{12,8},{16,20},{20,16},{24,28},{28,24},{1,5},{5... | collective-permute-start | bytes 24584 | tf_op jit(solution)/shard_map/ppermute | solution.py:340
  37.1 0.0 collective-permute-start.15
  37.2 2.0 %collective-permute-done.14.refs_1_ = f32[8,256]{1,0:T(8,128)S(1)} collective-permute-done((f32[8,256]{1,0:T(8,128)S(1)}, f32[8,256]{1,0:T(8,128)S(1)}, u32[]{:S(2)}, u32[]{:S(2)}) %collective-permute-start.14) | collective-permute-done | bytes 8224 | tf_op jit(solution)/shard_map/ppermute | solution.py:340
  39.2 0.5 %collective-permute-done.13.refs_1_ = f32[128,256]{1,0:T(8,128)S(1)} collective-permute-done((f32[128,256]{1,0:T(8,128)S(1)}, f32[128,256]{1,0:T(8,128)S(1)}, u32[]{:S(2)}, u32[]{:S(2)}) %collective-permute-start.13) | collective-permute-done | bytes 131104 | tf_op jit(solution)/shard_map/ppermute | solution.py:284
  39.7 0.0 collective-permute-start.16
  39.7 0.3 shard_map.87.merged_ref
  40.0 0.7 %shard_map.88 = f32[1,256,256]{2,1,0:T(8,128)} custom-call(f32[8,256]{1,0:T(8,128)S(1)} %shard_map.87.merged_ref, f32[128,256]{1,0:T(8,128)S(1)} %add_multiply_fusion.first_ref.refs_3_, f32[128,256]{1,0:T(8,128)S(1)} %collective-permute-done.6.first_other_ref.refs_4_.refs_7_, f32[128,256]{1,0:T(8,128)S(1)} %get-tuple-element.24.field_ref.refs_3_, ...), custom_call_target="tpu_custom_call" | custom-call | tf_op jit(solution)/shard_map/pallas_call | solution.py:22
  40.7 0.0 collective-permute-done.15.refs_4_
  40.7 0.3 collective-permute-done.16.refs_5_
  41.0 0.8 %shard_map.89 = f32[1,256,256]{2,1,0:T(8,128)} custom-call(f32[8,256]{1,0:T(8,128)S(1)} %shard_map.87.merged_ref, f32[128,256]{1,0:T(8,128)S(1)} %shard_map.86.refs_0_, f32[128,256]{1,0:T(8,128)S(1)} %collective-permute-done.13.refs_1_, f32[128,256]{1,0:T(8,128)S(1)} %get-tuple-element.37.refs_2_, f32[128,256]{1,0:T(8,128)S(1)} %add_multiply_fusion.first_ref.refs_3_, ...), custom_call_target="tpu_custom_call" | custom-call | tf_op jit(solution)/shard_map/pallas_call | solution.py:22
  (5 shorter events, 0.1 us)
Async XLA Ops:
  0.6 9.1 %collective-permute-start = (f32[256,256]{1,0:T(8,128)}, f32[256,256]{1,0:T(8,128)S(1)}, u32[]{:S(2)}, u32[]{:S(2)}) collective-permute-start(f32[256,256]{1,0:T(8,128)} %bitcast.1), channel_id=1, source_target_pairs={{1,5},{3,7},{5,1},{7,3},{9,13},{11,15},{13,9},{15,11},{17,21},{19,... | collective-permute-start | bytes 786440 | tf_op jit(solution)/shard_map/ppermute | solution.py:290
  6.1 3.7 %collective-permute-start.1 = (s32[8,128]{1,0:T(8,128)S(1)}, s32[8,128]{1,0:T(8,128)S(1)}, u32[]{:S(2)}, u32[]{:S(2)}) collective-permute-start(s32[8,128]{1,0:T(8,128)S(1)} %get-tuple-element.28), channel_id=1, source_target_pairs={{1,5},{3,7},{5,1},{7,3},{9,13},{11,15},{13,9},{15,11},{17,21},{19,... | collective-permute-start | bytes 12296 | tf_op jit(solution)/shard_map/ppermute | solution.py:302
  9.8 1.6 %collective-permute-start.2 = (f32[256,256]{1,0:T(8,128)S(1)}, f32[256,256]{1,0:T(8,128)S(1)}, u32[]{:S(2)}, u32[]{:S(2)}) collective-permute-start(f32[256,256]{1,0:T(8,128)S(1)} %shard_map.79.refs_5_), channel_id=1, source_target_pairs={{0,1},{1,0},{2,3},{3,2},{4,5},{5,4},{6,7},{7,6},{8,9},{9,8},{10,11... | collective-permute-start | bytes 786440 | tf_op jit(solution)/shard_map/ppermute | solution.py:277
  12.7 1.4 %collective-permute-start.3 = (f32[128,256]{1,0:T(8,128)S(1)}, f32[128,256]{1,0:T(8,128)S(1)}, u32[]{:S(2)}, u32[]{:S(2)}) collective-permute-start(f32[128,256]{1,0:T(8,128)S(1)} %get-tuple-element.36), channel_id=1, source_target_pairs={{0,1},{1,0},{2,3},{3,2},{4,5},{5,4},{6,7},{7,6},{8,9},{9,8},{10,11... | collective-permute-start | bytes 393224 | tf_op jit(solution)/shard_map/ppermute | solution.py:277
  14.2 5.8 %collective-permute-start.4 = (f32[128,256]{1,0:T(8,128)S(1)}, f32[128,256]{1,0:T(8,128)S(1)}, u32[]{:S(2)}, u32[]{:S(2)}) collective-permute-start(f32[128,256]{1,0:T(8,128)S(1)} %add.9), channel_id=1, source_target_pairs={{0,2},{1,3},{2,0},{3,1},{4,6},{5,7},{6,4},{7,5},{8,10},{9,11},{10,... | collective-permute-start | bytes 393224 | tf_op jit(solution)/shard_map/ppermute | solution.py:284
  20.0 3.9 %collective-permute-start.6 = (f32[128,256]{1,0:T(8,128)S(1)}, f32[128,256]{1,0:T(8,128)S(1)}, u32[]{:S(2)}, u32[]{:S(2)}) collective-permute-start(f32[128,256]{1,0:T(8,128)S(1)} %add_multiply_fusion.first_ref.refs_3_), channel_id=1, source_target_pairs={{0,1},{1,0},{2,3},{3,2},{4,5},{5,4},{6,7},{7,6},{8,9},{9,8},{10,11... | collective-permute-start | bytes 393224 | tf_op jit(solution)/shard_map/ppermute | solution.py:277
  20.1 6.7 %collective-permute-start.9 = (f32[128,256]{1,0:T(8,128)S(1)}, f32[128,256]{1,0:T(8,128)S(1)}, u32[]{:S(2)}, u32[]{:S(2)}) collective-permute-start(f32[128,256]{1,0:T(8,128)S(1)} %add_multiply_fusion.first_ref.refs_3_), channel_id=1, source_target_pairs={{1,5},{3,7},{5,1},{7,3},{9,13},{11,15},{13,9},{15,11},{17,21},{19,... | collective-permute-start | bytes 393224 | tf_op jit(solution)/shard_map/ppermute | solution.py:312
  21.2 8.0 %collective-permute-start.5 = (f32[128,256]{1,0:T(8,128)S(1)}, f32[128,256]{1,0:T(8,128)S(1)}, u32[]{:S(2)}, u32[]{:S(2)}) collective-permute-start(f32[128,256]{1,0:T(8,128)S(1)} %add_multiply_fusion.first_ref.refs_3_), channel_id=1, source_target_pairs={{0,4},{2,6},{4,0},{6,2},{8,12},{10,14},{12,8},{14,10},{16,20},{18,... | collective-permute-start | bytes 393224 | tf_op jit(solution)/shard_map/ppermute | solution.py:313
  24.2 5.0 %collective-permute-start.7 = (f32[8,256]{1,0:T(8,128)S(1)}, f32[8,256]{1,0:T(8,128)S(1)}, u32[]{:S(2)}, u32[]{:S(2)}) collective-permute-start(f32[8,256]{1,0:T(8,128)S(1)} %shard_map.82), channel_id=1, source_target_pairs={{0,16},{4,20},{8,24},{12,28},{16,0},{20,4},{24,8},{28,12},{1,17},{... | collective-permute-start | bytes 24584 | tf_op jit(solution)/shard_map/ppermute | solution.py:318
  26.8 4.4 %collective-permute-start.10 = (f32[128,256]{1,0:T(8,128)S(1)}, f32[128,256]{1,0:T(8,128)S(1)}, u32[]{:S(2)}, u32[]{:S(2)}) collective-permute-start(f32[128,256]{1,0:T(8,128)S(1)} %collective-permute-done.9.refs_5_), channel_id=1, source_target_pairs={{0,1},{1,0},{2,3},{3,2},{4,5},{5,4},{6,7},{7,6},{8,9},{9,8},{10,11... | collective-permute-start | bytes 393224 | tf_op jit(solution)/shard_map/ppermute | solution.py:277
  29.2 2.0 %collective-permute-start.11 = (f32[128,256]{1,0:T(8,128)S(1)}, f32[128,256]{1,0:T(8,128)S(1)}, u32[]{:S(2)}, u32[]{:S(2)}) collective-permute-start(f32[128,256]{1,0:T(8,128)S(1)} %collective-permute-done.5.refs_7_), channel_id=1, source_target_pairs={{0,1},{1,0},{2,3},{3,2},{4,5},{5,4},{6,7},{7,6},{8,9},{9,8},{10,11... | collective-permute-start | bytes 393224 | tf_op jit(solution)/shard_map/ppermute | solution.py:277
  29.2 4.7 %collective-permute-start.8 = (f32[8,256]{1,0:T(8,128)S(1)}, f32[8,256]{1,0:T(8,128)S(1)}, u32[]{:S(2)}, u32[]{:S(2)}) collective-permute-start(f32[8,256]{1,0:T(8,128)S(1)} %add.11.a_ref), channel_id=1, source_target_pairs={{0,8},{4,12},{8,0},{12,4},{16,24},{20,28},{24,16},{28,20},{1,9},{5... | collective-permute-start | bytes 24584 | tf_op jit(solution)/shard_map/ppermute | solution.py:333
  32.4 1.5 %collective-permute-start.12 = (f32[128,256]{1,0:T(8,128)S(1)}, f32[128,256]{1,0:T(8,128)S(1)}, u32[]{:S(2)}, u32[]{:S(2)}) collective-permute-start(f32[128,256]{1,0:T(8,128)S(1)} %get-tuple-element.42), channel_id=1, source_target_pairs={{0,1},{1,0},{2,3},{3,2},{4,5},{5,4},{6,7},{7,6},{8,9},{9,8},{10,11... | collective-permute-start | bytes 393224 | tf_op jit(solution)/shard_map/ppermute | solution.py:277
  33.9 5.8 %collective-permute-start.13 = (f32[128,256]{1,0:T(8,128)S(1)}, f32[128,256]{1,0:T(8,128)S(1)}, u32[]{:S(2)}, u32[]{:S(2)}) collective-permute-start(f32[128,256]{1,0:T(8,128)S(1)} %shard_map.86.refs_0_), channel_id=1, source_target_pairs={{0,2},{1,3},{2,0},{3,1},{4,6},{5,7},{6,4},{7,5},{8,10},{9,11},{10,... | collective-permute-start | bytes 393224 | tf_op jit(solution)/shard_map/ppermute | solution.py:284
  35.5 3.7 %collective-permute-start.14 = (f32[8,256]{1,0:T(8,128)S(1)}, f32[8,256]{1,0:T(8,128)S(1)}, u32[]{:S(2)}, u32[]{:S(2)}) collective-permute-start(f32[8,256]{1,0:T(8,128)S(1)} %shard_map.85.after_ref.refs_0_), channel_id=1, source_target_pairs={{0,4},{4,0},{8,12},{12,8},{16,20},{20,16},{24,28},{28,24},{1,5},{5... | collective-permute-start | bytes 24584 | tf_op jit(solution)/shard_map/ppermute | solution.py:340
  37.1 3.6 %collective-permute-start.15 = (f32[128,256]{1,0:T(8,128)S(1)}, f32[128,256]{1,0:T(8,128)S(1)}, u32[]{:S(2)}, u32[]{:S(2)}) collective-permute-start(f32[128,256]{1,0:T(8,128)S(1)} %shard_map.86.refs_0_), channel_id=1, source_target_pairs={{0,1},{1,0},{2,3},{3,2},{4,5},{5,4},{6,7},{7,6},{8,9},{9,8},{10,11... | collective-permute-start | bytes 393224 | tf_op jit(solution)/shard_map/ppermute | solution.py:277
  39.7 1.3 %collective-permute-start.16 = (f32[128,256]{1,0:T(8,128)S(1)}, f32[128,256]{1,0:T(8,128)S(1)}, u32[]{:S(2)}, u32[]{:S(2)}) collective-permute-start(f32[128,256]{1,0:T(8,128)S(1)} %collective-permute-done.13.refs_1_), channel_id=1, source_target_pairs={{0,1},{1,0},{2,3},{3,2},{4,5},{5,4},{6,7},{7,6},{8,9},{9,8},{10,11... | collective-permute-start | bytes 393224 | tf_op jit(solution)/shard_map/ppermute | solution.py:277

commit v8 on v6

--- a/solution.py
+++ b/solution.py
@@ -143,30 +143,27 @@
     slot = jnp.where(lax.rem(sector, 2) == 0, 2, 0)
     got = jnp.where(core == 1, slot, 2 - slot)
 
+    def is_beyond(slot):
+        last = lax.axis_size("sec") - 1
+        return ((sector == 0) & (slot == 0)) | ((sector == last) & (slot == 2))
+
     def put(index, mine_ref, other_ref):
         for which, ref in ((core, mine_ref), (1 - core, other_ref)):
             rows = rows_of(which, half)
-            high[index, rows], low[index, rows] = split(ref[...])
-
-    put(1, own_ref, own_other_ref)
+            high[index, rows], low[index, rows] = split(jnp.where(is_beyond(index), 0.0, ref[...]))
+
+    for which, ref in ((core, own_ref), (1 - core, own_other_ref)):
+        rows = rows_of(which, half)
+        high[1, rows], low[1, rows] = split(ref[...])
     if raw:
         for index, ref, live_ref in zip((got, 2 - got), refs[:2], refs[2:]):
-            live = inside((block, block), 0, live_ref[:1, :1], live_ref[1:2, :1])
+            rows = jnp.where(is_beyond(index), 0, live_ref[:1, :1])
+            live = inside((block, block), 0, rows, live_ref[1:2, :1])
             high[index], low[index] = split(jnp.where(live, ref[...], 0.0))
     else:
         one_ref, one_other_ref, two_ref, two_other_ref = refs
         put(got, one_ref, two_other_ref)
         put(2 - got, two_ref, one_other_ref)
-
-    @pl.when(sector == 0)
-    def _():
-        high[0] = jnp.zeros(high.shape[1:], high.dtype)
-        low[0] = jnp.zeros(low.shape[1:], low.dtype)
-
-    @pl.when(sector == lax.axis_size("sec") - 1)
-    def _():
-        high[2] = jnp.zeros(high.shape[1:], high.dtype)
-        low[2] = jnp.zeros(low.shape[1:], low.dtype)
 
     send_ref[...] = half_product(1 - core, shift_ref, high, low, left_ref, right_ref)
 

time: 42.1 us -> 42.1 us (level)
  no operation moved by 1% of the time
where the time goes in v8:
time: 42.1 us; the launch traced here: 41.9 us
  starting transfers between devices  18.3 us (43%)
  waiting for transfers between devices  11 us (26%)
  Pallas kernels  10.4 us (25%)
  between operations  2.05 us (5%)
    pallas_call x12, Pallas kernels, call(): pl.pallas_call(kernel, out_shape=out_shape, in_specs=in_specs, out_specs=...  10.4 us
    ppermute x2, waiting for transfers between devices, over_chips(): lax.ppermute(total, 'op', [(i, i ^ step) for i in range(ops)])  4.61 us
    ppermute x1, starting transfers between devices, local(): got = lax.ppermute(state[0], ('sec', 'op'), crossing)  3.03 us
    ppermute x2, starting transfers between devices, over_chips(): lax.ppermute(total, 'op', [(i, i ^ step) for i in range(ops)])  2.93 us
    ppermute x1, starting transfers between devices, local(): two = lax.ppermute(first, ('sec', 'op'), crossing_too)  2.76 us
    ppermute x1, starting transfers between devices, with_distant(): lax.ppermute(sums, 'sec', [(s, s ^ step) for s in range(sectors)])  2.6 us
    ppermute x1, starting transfers between devices, local(): lax.ppermute(sums, 'sec', [(s, s ^ 2) for s in range(sectors)])  1.96 us
    ppermute x1, starting transfers between devices, local(): lax.ppermute(sums, 'sec', pairs)  1.95 us
  transfers between devices with their start and end apart: 17, of which 8 were waited for; matrix products, arithmetic and copies ran while one was open for 0% of the time, Pallas kernels for 20%

profile of v8, /device:TPU:0, one launch (start us, length us, event | category | flops | bytes accessed | tf_op | source)
XLA Modules:
  0.0 41.9 jit_solution(13888696908542022735)
XLA Ops:
  0.6 3.0 %collective-permute-start = (f32[256,256]{1,0:T(8,128)}, f32[256,256]{1,0:T(8,128)S(1)}, u32[]{:S(2)}, u32[]{:S(2)}) collective-permute-start(f32[256,256]{1,0:T(8,128)} %bitcast.1), channel_id=1, source_target_pairs={{1,5},{3,7},{5,1},{7,3},{9,13},{11,15},{13,9},{15,11},{17,21},{19,... | collective-permute-start | bytes 786440 | tf_op jit(solution)/shard_map/ppermute | solution.py:281
  5.0 0.1 pad_add_fusion.live_ref
  5.0 1.0 %shard_map.77 = (f32[128,256]{1,0:T(8,128)S(1)}, f32[128,256]{1,0:T(8,128)S(1)}, f32[128,256]{1,0:T(8,128)S(1)}, s32[8,128]{1,0:T(8,128)S(1)}) custom-call(f32[1,256,256]{2,1,0:T(8,128)} %state_ref.1, s32[2]{0:T(128)S(1)} %pad_add_fusion.live_ref), custom_call_target="tpu_custom_call" | custom-call | tf_op jit(solution)/shard_map/pallas_call | solution.py:22
  6.1 0.1 collective-permute-start.1
  6.1 2.4 %shard_map.78 = (f32[8,1,256,256]{3,2,1,0:T(8,128)S(1)}, f32[8,1,256,256]{3,2,1,0:T(8,128)S(1)}, s32[8,8,128]{2,1,0:T(8,128)S(1)}) custom-call(f32[8,1,256,256]{3,2,1,0:T(8,128)} %left_ref.1, f32[8,1,256,256]{3,2,1,0:T(8,128)} %right_ref.1, s32[8]{0:T(128)} %shift_ref.1, f32[128,256]{1,0:T(8,128)S(1)} %get-tuple-element.21.field_ref.refs_3_), custom_call_target="tpu_custom_call" | custom-call | bytes 4194304 | tf_op jit(solution)/shard_map/pallas_call | solution.py:22
  8.5 1.2 %collective-permute-done.1.refs_7_ = s32[8,128]{1,0:T(8,128)S(1)} collective-permute-done((s32[8,128]{1,0:T(8,128)S(1)}, s32[8,128]{1,0:T(8,128)S(1)}, u32[]{:S(2)}, u32[]{:S(2)}) %collective-permute-start.1) | collective-permute-done | bytes 4128 | tf_op jit(solution)/shard_map/ppermute | solution.py:293
  9.7 0.0 collective-permute-done.refs_5_
  9.7 0.0 collective-permute-start.2
  9.7 0.5 %collective-permute-start.3 = (s32[8,128]{1,0:T(8,128)S(1)}, s32[8,128]{1,0:T(8,128)S(1)}, u32[]{:S(2)}, u32[]{:S(2)}) collective-permute-start(s32[8,128]{1,0:T(8,128)S(1)} %collective-permute-done.1.refs_7_), channel_id=1, source_target_pairs={{0,1},{1,0},{2,3},{3,2},{4,5},{5,4},{6,7},{7,6},{8,9},{9,8},{10,11... | collective-permute-start | bytes 12296 | tf_op jit(solution)/shard_map/ppermute | solution.py:268
  10.3 1.0 %collective-permute-done.3.refs_8_ = s32[8,128]{1,0:T(8,128)S(1)} collective-permute-done((s32[8,128]{1,0:T(8,128)S(1)}, s32[8,128]{1,0:T(8,128)S(1)}, u32[]{:S(2)}, u32[]{:S(2)}) %collective-permute-start.3) | collective-permute-done | bytes 4128 | tf_op jit(solution)/shard_map/ppermute | solution.py:268
  11.3 0.0 collective-permute-done.2.refs_6_
  11.3 1.4 %shard_map.79 = (f32[128,256]{1,0:T(8,128)S(1)}, bf16[3,256,256]{2,1,0:T(8,128)(2,1)S(1)}, bf16[3,256,256]{2,1,0:T(8,128)(2,1)S(1)}) custom-call(s32[8,8,128]{2,1,0:T(8,128)S(1)} %get-tuple-element.22.refs_0_.shift_ref, f32[8,1,256,256]{3,2,1,0:T(8,128)S(1)} %get-tuple-element.26.refs_1_.left_ref, ...), custom_call_target="tpu_custom_call" | custom-call | flops 4026531840 | bytes 4194304 | tf_op jit(solution)/shard_map/pallas_call | solution.py:22
  12.7 0.2 collective-permute-start.4
  12.9 1.2 %shard_map.80 = f32[128,256]{1,0:T(8,128)S(1)} custom-call(s32[8,8,128]{2,1,0:T(8,128)S(1)} %get-tuple-element.22.refs_0_.shift_ref, f32[8,1,256,256]{3,2,1,0:T(8,128)S(1)} %get-tuple-element.26.refs_1_.left_ref, f32[8,1,256,256]{3,2,1,0:T(8,128)S(1)} %get-tuple-element.27.refs_2_.right_ref, bf16[3,256,256]{2,1,0:T(8,128)(2,1)S(1)} %get-tuple-element.31.high, ...), custom_call_target="tpu_custom_call" | custom-call | flops 4026531840 | bytes 4194304 | tf_op jit(solution)/shard_map/pallas_call | solution.py:22
  14.1 0.0 collective-permute-done.4
  14.1 1.3 %collective-permute-start.5 = (f32[128,256]{1,0:T(8,128)S(1)}, f32[128,256]{1,0:T(8,128)S(1)}, u32[]{:S(2)}, u32[]{:S(2)}) collective-permute-start(f32[128,256]{1,0:T(8,128)S(1)} %add.12), channel_id=1, source_target_pairs={{0,2},{1,3},{2,0},{3,1},{4,6},{5,7},{6,4},{7,5},{8,10},{9,11},{10,... | collective-permute-start | bytes 393224 | tf_op jit(solution)/shard_map/ppermute | solution.py:275
  15.5 4.5 %collective-permute-done.5 = f32[128,256]{1,0:T(8,128)S(1)} collective-permute-done((f32[128,256]{1,0:T(8,128)S(1)}, f32[128,256]{1,0:T(8,128)S(1)}, u32[]{:S(2)}, u32[]{:S(2)}) %collective-permute-start.5) | collective-permute-done | bytes 131104 | tf_op jit(solution)/shard_map/ppermute | solution.py:275
  20.0 0.1 collective-permute-start.7
  20.1 1.1 %collective-permute-start.10 = (f32[128,256]{1,0:T(8,128)S(1)}, f32[128,256]{1,0:T(8,128)S(1)}, u32[]{:S(2)}, u32[]{:S(2)}) collective-permute-start(f32[128,256]{1,0:T(8,128)S(1)} %add_multiply_fusion.first_ref.refs_3_), channel_id=1, source_target_pairs={{1,5},{3,7},{5,1},{7,3},{9,13},{11,15},{13,9},{15,11},{17,21},{19,... | collective-permute-start | bytes 393224 | tf_op jit(solution)/shard_map/ppermute | solution.py:302
  21.2 2.8 %collective-permute-start.6 = (f32[128,256]{1,0:T(8,128)S(1)}, f32[128,256]{1,0:T(8,128)S(1)}, u32[]{:S(2)}, u32[]{:S(2)}) collective-permute-start(f32[128,256]{1,0:T(8,128)S(1)} %add_multiply_fusion.first_ref.refs_3_), channel_id=1, source_target_pairs={{0,4},{2,6},{4,0},{6,2},{8,12},{10,14},{12,8},{14,10},{16,20},{18,... | collective-permute-start | bytes 393224 | tf_op jit(solution)/shard_map/ppermute | solution.py:303
  24.0 0.0 collective-permute-done.7.first_other_ref.refs_4_
  24.0 0.3 shard_map.81
  24.2 2.6 %collective-permute-start.8 = (f32[8,256]{1,0:T(8,128)S(1)}, f32[8,256]{1,0:T(8,128)S(1)}, u32[]{:S(2)}, u32[]{:S(2)}) collective-permute-start(f32[8,256]{1,0:T(8,128)S(1)} %shard_map.81), channel_id=1, source_target_pairs={{0,16},{4,20},{8,24},{12,28},{16,0},{20,4},{24,8},{28,12},{1,17},{... | collective-permute-start | bytes 24584 | tf_op jit(solution)/shard_map/ppermute | solution.py:308
  26.8 0.0 collective-permute-done.10.refs_5_
  26.8 0.7 %collective-permute-start.11 = (f32[128,256]{1,0:T(8,128)S(1)}, f32[128,256]{1,0:T(8,128)S(1)}, u32[]{:S(2)}, u32[]{:S(2)}) collective-permute-start(f32[128,256]{1,0:T(8,128)S(1)} %collective-permute-done.10.refs_5_), channel_id=1, source_target_pairs={{0,1},{1,0},{2,3},{3,2},{4,5},{5,4},{6,7},{7,6},{8,9},{9,8},{10,11... | collective-permute-start | bytes 393224 | tf_op jit(solution)/shard_map/ppermute | solution.py:268
  27.5 1.7 %collective-permute-done.8 = f32[8,256]{1,0:T(8,128)S(1)} collective-permute-done((f32[8,256]{1,0:T(8,128)S(1)}, f32[8,256]{1,0:T(8,128)S(1)}, u32[]{:S(2)}, u32[]{:S(2)}) %collective-permute-start.8) | collective-permute-done | bytes 8224 | tf_op jit(solution)/shard_map/ppermute | solution.py:308
  29.2 0.0 collective-permute-done.6.refs_7_
  29.2 0.0 collective-permute-start.12
  29.2 2.0 %collective-permute-start.9 = (f32[8,256]{1,0:T(8,128)S(1)}, f32[8,256]{1,0:T(8,128)S(1)}, u32[]{:S(2)}, u32[]{:S(2)}) collective-permute-start(f32[8,256]{1,0:T(8,128)S(1)} %add.14.a_ref), channel_id=1, source_target_pairs={{0,8},{4,12},{8,0},{12,4},{16,24},{20,28},{24,16},{28,20},{1,9},{5... | collective-permute-start | bytes 24584 | tf_op jit(solution)/shard_map/ppermute | solution.py:322
  31.2 0.0 collective-permute-done.11.refs_6_
  31.2 0.0 collective-permute-done.12.refs_8_
  31.2 1.3 %shard_map.82 = (f32[128,256]{1,0:T(8,128)S(1)}, bf16[3,256,256]{2,1,0:T(8,128)(2,1)S(1)}, bf16[3,256,256]{2,1,0:T(8,128)(2,1)S(1)}) custom-call(s32[8,8,128]{2,1,0:T(8,128)S(1)} %get-tuple-element.22.refs_0_.shift_ref, f32[8,1,256,256]{3,2,1,0:T(8,128)S(1)} %get-tuple-element.26.refs_1_.left_ref, ...), custom_call_target="tpu_custom_call" | custom-call | flops 4026531840 | bytes 4194304 | tf_op jit(solution)/shard_map/pallas_call | solution.py:22
  32.5 0.3 collective-permute-start.14
  32.8 0.2 collective-permute-done.9.b_ref
  32.9 1.2 %shard_map.86 = f32[128,256]{1,0:T(8,128)S(1)} custom-call(s32[8,8,128]{2,1,0:T(8,128)S(1)} %get-tuple-element.22.refs_0_.shift_ref, f32[8,1,256,256]{3,2,1,0:T(8,128)S(1)} %get-tuple-element.26.refs_1_.left_ref, f32[8,1,256,256]{3,2,1,0:T(8,128)S(1)} %get-tuple-element.27.refs_2_.right_ref, bf16[3,256,256]{2,1,0:T(8,128)(2,1)S(1)} %get-tuple-element.38.high, ...), custom_call_target="tpu_custom_call" | custom-call | flops 4026531840 | bytes 4194304 | tf_op jit(solution)/shard_map/pallas_call | solution.py:22
  34.1 0.0 collective-permute-done.14
  34.1 1.6 %collective-permute-start.15 = (f32[128,256]{1,0:T(8,128)S(1)}, f32[128,256]{1,0:T(8,128)S(1)}, u32[]{:S(2)}, u32[]{:S(2)}) collective-permute-start(f32[128,256]{1,0:T(8,128)S(1)} %add.15.total_ref), channel_id=1, source_target_pairs={{0,2},{1,3},{2,0},{3,1},{4,6},{5,7},{6,4},{7,5},{8,10},{9,11},{10,... | collective-permute-start | bytes 393224 | tf_op jit(solution)/shard_map/ppermute | solution.py:275
  35.7 1.9 %collective-permute-start.13 = (f32[8,256]{1,0:T(8,128)S(1)}, f32[8,256]{1,0:T(8,128)S(1)}, u32[]{:S(2)}, u32[]{:S(2)}) collective-permute-start(f32[8,256]{1,0:T(8,128)S(1)} %shard_map.83.refs_0_), channel_id=1, source_target_pairs={{0,4},{4,0},{8,12},{12,8},{16,20},{20,16},{24,28},{28,24},{1,5},{5... | collective-permute-start | bytes 24584 | tf_op jit(solution)/shard_map/ppermute | solution.py:332
  37.7 1.7 %collective-permute-done.13.refs_1_ = f32[8,256]{1,0:T(8,128)S(1)} collective-permute-done((f32[8,256]{1,0:T(8,128)S(1)}, f32[8,256]{1,0:T(8,128)S(1)}, u32[]{:S(2)}, u32[]{:S(2)}) %collective-permute-start.13) | collective-permute-done | bytes 8224 | tf_op jit(solution)/shard_map/ppermute | solution.py:332
  39.4 0.3 shard_map.84.merged_ref
  39.6 0.1 collective-permute-done.15.peer_ref
  39.8 0.1 collective-permute-start.16
  39.8 0.7 %shard_map.85 = f32[1,256,256]{2,1,0:T(8,128)} custom-call(f32[8,256]{1,0:T(8,128)S(1)} %shard_map.84.merged_ref, f32[128,256]{1,0:T(8,128)S(1)} %add_multiply_fusion.first_ref.refs_3_, f32[128,256]{1,0:T(8,128)S(1)} %collective-permute-done.7.first_other_ref.refs_4_, f32[128,256]{1,0:T(8,128)S(1)} %get-tuple-element.21.field_ref.refs_3_, ...), custom_call_target="tpu_custom_call" | custom-call | tf_op jit(solution)/shard_map/pallas_call | solution.py:22
  40.6 0.6 %collective-permute-done.16.other_ref = f32[128,256]{1,0:T(8,128)S(1)} collective-permute-done((f32[128,256]{1,0:T(8,128)S(1)}, f32[128,256]{1,0:T(8,128)S(1)}, u32[]{:S(2)}, u32[]{:S(2)}) %collective-permute-start.16) | collective-permute-done | bytes 131104 | tf_op jit(solution)/shard_map/ppermute | solution.py:268
  41.2 0.7 %shard_map.88 = f32[1,256,256]{2,1,0:T(8,128)} custom-call(f32[128,256]{1,0:T(8,128)S(1)} %shard_map.87.mine_ref, f32[128,256]{1,0:T(8,128)S(1)} %collective-permute-done.16.other_ref), custom_call_target="tpu_custom_call" | custom-call | tf_op jit(solution)/shard_map/pallas_call | solution.py:22
  (6 shorter events, 0.1 us)
Async XLA Ops:
  0.6 9.1 %collective-permute-start = (f32[256,256]{1,0:T(8,128)}, f32[256,256]{1,0:T(8,128)S(1)}, u32[]{:S(2)}, u32[]{:S(2)}) collective-permute-start(f32[256,256]{1,0:T(8,128)} %bitcast.1), channel_id=1, source_target_pairs={{1,5},{3,7},{5,1},{7,3},{9,13},{11,15},{13,9},{15,11},{17,21},{19,... | collective-permute-start | bytes 786440 | tf_op jit(solution)/shard_map/ppermute | solution.py:281
  6.1 3.7 %collective-permute-start.1 = (s32[8,128]{1,0:T(8,128)S(1)}, s32[8,128]{1,0:T(8,128)S(1)}, u32[]{:S(2)}, u32[]{:S(2)}) collective-permute-start(s32[8,128]{1,0:T(8,128)S(1)} %get-tuple-element.25), channel_id=1, source_target_pairs={{1,5},{3,7},{5,1},{7,3},{9,13},{11,15},{13,9},{15,11},{17,21},{19,... | collective-permute-start | bytes 12296 | tf_op jit(solution)/shard_map/ppermute | solution.py:293
  9.7 1.5 %collective-permute-start.2 = (f32[256,256]{1,0:T(8,128)S(1)}, f32[256,256]{1,0:T(8,128)S(1)}, u32[]{:S(2)}, u32[]{:S(2)}) collective-permute-start(f32[256,256]{1,0:T(8,128)S(1)} %collective-permute-done.refs_5_), channel_id=1, source_target_pairs={{0,1},{1,0},{2,3},{3,2},{4,5},{5,4},{6,7},{7,6},{8,9},{9,8},{10,11... | collective-permute-start | bytes 786440 | tf_op jit(solution)/shard_map/ppermute | solution.py:268
  9.7 1.5 %collective-permute-start.3 = (s32[8,128]{1,0:T(8,128)S(1)}, s32[8,128]{1,0:T(8,128)S(1)}, u32[]{:S(2)}, u32[]{:S(2)}) collective-permute-start(s32[8,128]{1,0:T(8,128)S(1)} %collective-permute-done.1.refs_7_), channel_id=1, source_target_pairs={{0,1},{1,0},{2,3},{3,2},{4,5},{5,4},{6,7},{7,6},{8,9},{9,8},{10,11... | collective-permute-start | bytes 12296 | tf_op jit(solution)/shard_map/ppermute | solution.py:268
  12.7 1.4 %collective-permute-start.4 = (f32[128,256]{1,0:T(8,128)S(1)}, f32[128,256]{1,0:T(8,128)S(1)}, u32[]{:S(2)}, u32[]{:S(2)}) collective-permute-start(f32[128,256]{1,0:T(8,128)S(1)} %get-tuple-element.33), channel_id=1, source_target_pairs={{0,1},{1,0},{2,3},{3,2},{4,5},{5,4},{6,7},{7,6},{8,9},{9,8},{10,11... | collective-permute-start | bytes 393224 | tf_op jit(solution)/shard_map/ppermute | solution.py:268
  14.1 5.8 %collective-permute-start.5 = (f32[128,256]{1,0:T(8,128)S(1)}, f32[128,256]{1,0:T(8,128)S(1)}, u32[]{:S(2)}, u32[]{:S(2)}) collective-permute-start(f32[128,256]{1,0:T(8,128)S(1)} %add.12), channel_id=1, source_target_pairs={{0,2},{1,3},{2,0},{3,1},{4,6},{5,7},{6,4},{7,5},{8,10},{9,11},{10,... | collective-permute-start | bytes 393224 | tf_op jit(solution)/shard_map/ppermute | solution.py:275
  20.0 3.9 %collective-permute-start.7 = (f32[128,256]{1,0:T(8,128)S(1)}, f32[128,256]{1,0:T(8,128)S(1)}, u32[]{:S(2)}, u32[]{:S(2)}) collective-permute-start(f32[128,256]{1,0:T(8,128)S(1)} %add_multiply_fusion.first_ref.refs_3_), channel_id=1, source_target_pairs={{0,1},{1,0},{2,3},{3,2},{4,5},{5,4},{6,7},{7,6},{8,9},{9,8},{10,11... | collective-permute-start | bytes 393224 | tf_op jit(solution)/shard_map/ppermute | solution.py:268
  20.1 6.7 %collective-permute-start.10 = (f32[128,256]{1,0:T(8,128)S(1)}, f32[128,256]{1,0:T(8,128)S(1)}, u32[]{:S(2)}, u32[]{:S(2)}) collective-permute-start(f32[128,256]{1,0:T(8,128)S(1)} %add_multiply_fusion.first_ref.refs_3_), channel_id=1, source_target_pairs={{1,5},{3,7},{5,1},{7,3},{9,13},{11,15},{13,9},{15,11},{17,21},{19,... | collective-permute-start | bytes 393224 | tf_op jit(solution)/shard_map/ppermute | solution.py:302
  21.2 8.0 %collective-permute-start.6 = (f32[128,256]{1,0:T(8,128)S(1)}, f32[128,256]{1,0:T(8,128)S(1)}, u32[]{:S(2)}, u32[]{:S(2)}) collective-permute-start(f32[128,256]{1,0:T(8,128)S(1)} %add_multiply_fusion.first_ref.refs_3_), channel_id=1, source_target_pairs={{0,4},{2,6},{4,0},{6,2},{8,12},{10,14},{12,8},{14,10},{16,20},{18,... | collective-permute-start | bytes 393224 | tf_op jit(solution)/shard_map/ppermute | solution.py:303
  24.2 5.0 %collective-permute-start.8 = (f32[8,256]{1,0:T(8,128)S(1)}, f32[8,256]{1,0:T(8,128)S(1)}, u32[]{:S(2)}, u32[]{:S(2)}) collective-permute-start(f32[8,256]{1,0:T(8,128)S(1)} %shard_map.81), channel_id=1, source_target_pairs={{0,16},{4,20},{8,24},{12,28},{16,0},{20,4},{24,8},{28,12},{1,17},{... | collective-permute-start | bytes 24584 | tf_op jit(solution)/shard_map/ppermute | solution.py:308
  26.8 4.4 %collective-permute-start.11 = (f32[128,256]{1,0:T(8,128)S(1)}, f32[128,256]{1,0:T(8,128)S(1)}, u32[]{:S(2)}, u32[]{:S(2)}) collective-permute-start(f32[128,256]{1,0:T(8,128)S(1)} %collective-permute-done.10.refs_5_), channel_id=1, source_target_pairs={{0,1},{1,0},{2,3},{3,2},{4,5},{5,4},{6,7},{7,6},{8,9},{9,8},{10,11... | collective-permute-start | bytes 393224 | tf_op jit(solution)/shard_map/ppermute | solution.py:268
  29.2 2.0 %collective-permute-start.12 = (f32[128,256]{1,0:T(8,128)S(1)}, f32[128,256]{1,0:T(8,128)S(1)}, u32[]{:S(2)}, u32[]{:S(2)}) collective-permute-start(f32[128,256]{1,0:T(8,128)S(1)} %collective-permute-done.6.refs_7_), channel_id=1, source_target_pairs={{0,1},{1,0},{2,3},{3,2},{4,5},{5,4},{6,7},{7,6},{8,9},{9,8},{10,11... | collective-permute-start | bytes 393224 | tf_op jit(solution)/shard_map/ppermute | solution.py:268
  29.2 3.7 %collective-permute-start.9 = (f32[8,256]{1,0:T(8,128)S(1)}, f32[8,256]{1,0:T(8,128)S(1)}, u32[]{:S(2)}, u32[]{:S(2)}) collective-permute-start(f32[8,256]{1,0:T(8,128)S(1)} %add.14.a_ref), channel_id=1, source_target_pairs={{0,8},{4,12},{8,0},{12,4},{16,24},{20,28},{24,16},{28,20},{1,9},{5... | collective-permute-start | bytes 24584 | tf_op jit(solution)/shard_map/ppermute | solution.py:322
  32.5 1.6 %collective-permute-start.14 = (f32[128,256]{1,0:T(8,128)S(1)}, f32[128,256]{1,0:T(8,128)S(1)}, u32[]{:S(2)}, u32[]{:S(2)}) collective-permute-start(f32[128,256]{1,0:T(8,128)S(1)} %get-tuple-element.37.after_ref), channel_id=1, source_target_pairs={{0,1},{1,0},{2,3},{3,2},{4,5},{5,4},{6,7},{7,6},{8,9},{9,8},{10,11... | collective-permute-start | bytes 393224 | tf_op jit(solution)/shard_map/ppermute | solution.py:268
  34.1 5.6 %collective-permute-start.15 = (f32[128,256]{1,0:T(8,128)S(1)}, f32[128,256]{1,0:T(8,128)S(1)}, u32[]{:S(2)}, u32[]{:S(2)}) collective-permute-start(f32[128,256]{1,0:T(8,128)S(1)} %add.15.total_ref), channel_id=1, source_target_pairs={{0,2},{1,3},{2,0},{3,1},{4,6},{5,7},{6,4},{7,5},{8,10},{9,11},{10,... | collective-permute-start | bytes 393224 | tf_op jit(solution)/shard_map/ppermute | solution.py:275
  35.7 3.7 %collective-permute-start.13 = (f32[8,256]{1,0:T(8,128)S(1)}, f32[8,256]{1,0:T(8,128)S(1)}, u32[]{:S(2)}, u32[]{:S(2)}) collective-permute-start(f32[8,256]{1,0:T(8,128)S(1)} %shard_map.83.refs_0_), channel_id=1, source_target_pairs={{0,4},{4,0},{8,12},{12,8},{16,20},{20,16},{24,28},{28,24},{1,5},{5... | collective-permute-start | bytes 24584 | tf_op jit(solution)/shard_map/ppermute | solution.py:332
  39.8 1.4 %collective-permute-start.16 = (f32[128,256]{1,0:T(8,128)S(1)}, f32[128,256]{1,0:T(8,128)S(1)}, u32[]{:S(2)}, u32[]{:S(2)}) collective-permute-start(f32[128,256]{1,0:T(8,128)S(1)} %shard_map.87.mine_ref), channel_id=1, source_target_pairs={{0,1},{1,0},{2,3},{3,2},{4,5},{5,4},{6,7},{7,6},{8,9},{9,8},{10,11... | collective-permute-start | bytes 393224 | tf_op jit(solution)/shard_map/ppermute | solution.py:268

commit v9 on v7

--- a/solution.py
+++ b/solution.py
@@ -149,29 +149,25 @@
     slot = jnp.where(lax.rem(sector, 2) == 0, 2, 0)
     got = jnp.where(core == 1, slot, 2 - slot)
 
+    def is_beyond(slot):
+        last = lax.axis_size("sec") - 1
+        return ((sector == 0) & (slot == 0)) | ((sector == last) & (slot == 2))
+
     def put(index, mine_ref, other_ref):
         for which, ref in ((core, mine_ref), (1 - core, other_ref)):
             rows = rows_of(which, half)
-            high[index, rows], low[index, rows] = split(ref[...])
-
-    put(1, own_ref, own_other_ref)
+            high[index, rows], low[index, rows] = split(jnp.where(is_beyond(index), 0.0, ref[...]))
+
+    for which, ref in ((core, own_ref), (1 - core, own_other_ref)):
+        rows = rows_of(which, half)
+        high[1, rows], low[1, rows] = split(ref[...])
     if raw:
         for index, ref in zip((got, 2 - got), refs):
-            high[index], low[index] = split(ref[...])
+            high[index], low[index] = split(jnp.where(is_beyond(index), 0.0, ref[...]))
     else:
         one_ref, one_other_ref, two_ref, two_other_ref = refs
         put(got, one_ref, two_other_ref)
         put(2 - got, two_ref, one_other_ref)
-
-    @pl.when(sector == 0)
-    def _():
-        high[0] = jnp.zeros(high.shape[1:], high.dtype)
-        low[0] = jnp.zeros(low.shape[1:], low.dtype)
-
-    @pl.when(sector == lax.axis_size("sec") - 1)
-    def _():
-        high[2] = jnp.zeros(high.shape[1:], high.dtype)
-        low[2] = jnp.zeros(low.shape[1:], low.dtype)
 
     send_ref[...] = half_product(1 - core, shift_ref, high, low, left_ref, right_ref)
 

time: 42 us -> 42.1 us (level)
  no operation moved by 1% of the time
where the time goes in v9:
time: 42.1 us; the launch traced here: 41.9 us
  starting transfers between devices  17.4 us (41%)
  waiting for transfers between devices  11.9 us (28%)
  Pallas kernels  10.4 us (25%)
  between operations  2.06 us (5%)
    pallas_call x13, Pallas kernels, call(): pl.pallas_call(kernel, out_shape=out_shape, in_specs=in_specs, out_specs=...  10.4 us
    ppermute x2, waiting for transfers between devices, over_chips(): lax.ppermute(total, 'op', [(i, i ^ step) for i in range(ops)])  5.03 us
    ppermute x1, starting transfers between devices, local(): got = lax.ppermute(state[0], ('sec', 'op'), crossing)  3.03 us
    ppermute x2, starting transfers between devices, over_chips(): lax.ppermute(total, 'op', [(i, i ^ step) for i in range(ops)])  2.87 us
    ppermute x1, starting transfers between devices, local(): two = lax.ppermute(first, ('sec', 'op'), crossing_too)  2.75 us
    ppermute x1, starting transfers between devices, with_distant(): lax.ppermute(sums, 'sec', [(s, s ^ step) for s in range(sectors)])  2.59 us
    ppermute x1, waiting for transfers between devices, local(): pair_sums = lax.ppermute(sums, 'sec', pairs)  2.01 us
    ppermute x1, starting transfers between devices, local(): lax.ppermute(sums, 'sec', [(s, s ^ 2) for s in range(sectors)])  1.95 us
  transfers between devices with their start and end apart: 17, of which 7 were waited for; matrix products, arithmetic and copies ran while one was open for 0% of the time, Pallas kernels for 20%

profile of v9, /device:TPU:0, one launch (start us, length us, event | category | flops | bytes accessed | tf_op | source)
XLA Modules:
  0.0 41.9 jit_solution(9844409455237908057)
XLA Ops:
  0.6 3.0 %collective-permute-start = (f32[256,256]{1,0:T(8,128)}, f32[256,256]{1,0:T(8,128)S(1)}, u32[]{:S(2)}, u32[]{:S(2)}) collective-permute-start(f32[256,256]{1,0:T(8,128)} %bitcast.1), channel_id=1, source_target_pairs={{1,5},{3,7},{5,1},{7,3},{9,13},{11,15},{13,9},{15,11},{17,21},{19,... | collective-permute-start | bytes 786440 | tf_op jit(solution)/shard_map/ppermute | solution.py:286
  5.0 0.1 pad_add_fusion.live_ref
  5.0 1.0 %shard_map.77 = (f32[128,256]{1,0:T(8,128)S(1)}, f32[128,256]{1,0:T(8,128)S(1)}, f32[128,256]{1,0:T(8,128)S(1)}, f32[128,256]{1,0:T(8,128)S(1)}, s32[8,128]{1,0:T(8,128)S(1)}) custom-call(f32[1,256,256]{2,1,0:T(8,128)} %state_ref.1, s32[2]{0:T(128)S(1)} %pad_add_fusion.live_ref), custom_call_target="tpu_custom_call" | custom-call | tf_op jit(solution)/shard_map/pallas_call | solution.py:22
  6.1 0.1 collective-permute-start.1
  6.2 2.4 %shard_map.78 = (f32[8,1,256,256]{3,2,1,0:T(8,128)S(1)}, f32[8,1,256,256]{3,2,1,0:T(8,128)S(1)}, s32[8,8,128]{2,1,0:T(8,128)S(1)}) custom-call(f32[8,1,256,256]{3,2,1,0:T(8,128)} %left_ref.1, f32[8,1,256,256]{3,2,1,0:T(8,128)} %right_ref.1, s32[8]{0:T(128)} %shift_ref.1, f32[128,256]{1,0:T(8,128)S(1)} %get-tuple-element.24.field_ref.refs_3_), custom_call_target="tpu_custom_call" | custom-call | bytes 4194304 | tf_op jit(solution)/shard_map/pallas_call | solution.py:22
  8.5 1.2 %collective-permute-done.1.live_ref = s32[8,128]{1,0:T(8,128)S(1)} collective-permute-done((s32[8,128]{1,0:T(8,128)S(1)}, s32[8,128]{1,0:T(8,128)S(1)}, u32[]{:S(2)}, u32[]{:S(2)}) %collective-permute-start.1) | collective-permute-done | bytes 4128 | tf_op jit(solution)/shard_map/ppermute | solution.py:298
  9.8 0.0 collective-permute-done.block_ref
  9.8 0.1 shard_map.79.refs_5_
  9.8 0.1 collective-permute-start.2
  9.9 1.5 %collective-permute-done.2.refs_6_ = f32[256,256]{1,0:T(8,128)S(1)} collective-permute-done((f32[256,256]{1,0:T(8,128)S(1)}, f32[256,256]{1,0:T(8,128)S(1)}, u32[]{:S(2)}, u32[]{:S(2)}) %collective-permute-start.2) | collective-permute-done | bytes 262176 | tf_op jit(solution)/shard_map/ppermute | solution.py:273
  11.4 1.3 %shard_map.80 = (f32[128,256]{1,0:T(8,128)S(1)}, bf16[3,256,256]{2,1,0:T(8,128)(2,1)S(1)}, bf16[3,256,256]{2,1,0:T(8,128)(2,1)S(1)}) custom-call(s32[8,8,128]{2,1,0:T(8,128)S(1)} %get-tuple-element.25.refs_0_.shift_ref, f32[8,1,256,256]{3,2,1,0:T(8,128)S(1)} %get-tuple-element.29.refs_1_.left_ref, ...), custom_call_target="tpu_custom_call" | custom-call | flops 4026531840 | bytes 4194304 | tf_op jit(solution)/shard_map/pallas_call | solution.py:22
  12.7 0.2 collective-permute-start.3
  12.9 1.2 %shard_map.81 = f32[128,256]{1,0:T(8,128)S(1)} custom-call(s32[8,8,128]{2,1,0:T(8,128)S(1)} %get-tuple-element.25.refs_0_.shift_ref, f32[8,1,256,256]{3,2,1,0:T(8,128)S(1)} %get-tuple-element.29.refs_1_.left_ref, f32[8,1,256,256]{3,2,1,0:T(8,128)S(1)} %get-tuple-element.30.refs_2_.right_ref, bf16[3,256,256]{2,1,0:T(8,128)(2,1)S(1)} %get-tuple-element.34.high, ...), custom_call_target="tpu_custom_call" | custom-call | flops 134217728 | bytes 4194304 | tf_op jit(solution)/shard_map/pallas_call | solution.py:22
  14.1 0.0 collective-permute-done.3
  14.2 1.3 %collective-permute-start.4 = (f32[128,256]{1,0:T(8,128)S(1)}, f32[128,256]{1,0:T(8,128)S(1)}, u32[]{:S(2)}, u32[]{:S(2)}) collective-permute-start(f32[128,256]{1,0:T(8,128)S(1)} %add.9), channel_id=1, source_target_pairs={{0,2},{1,3},{2,0},{3,1},{4,6},{5,7},{6,4},{7,5},{8,10},{9,11},{10,... | collective-permute-start | bytes 393224 | tf_op jit(solution)/shard_map/ppermute | solution.py:280
  15.5 4.5 %collective-permute-done.4 = f32[128,256]{1,0:T(8,128)S(1)} collective-permute-done((f32[128,256]{1,0:T(8,128)S(1)}, f32[128,256]{1,0:T(8,128)S(1)}, u32[]{:S(2)}, u32[]{:S(2)}) %collective-permute-start.4) | collective-permute-done | bytes 131104 | tf_op jit(solution)/shard_map/ppermute | solution.py:280
  20.0 0.1 collective-permute-start.6
  20.1 1.1 %collective-permute-start.9 = (f32[128,256]{1,0:T(8,128)S(1)}, f32[128,256]{1,0:T(8,128)S(1)}, u32[]{:S(2)}, u32[]{:S(2)}) collective-permute-start(f32[128,256]{1,0:T(8,128)S(1)} %add_multiply_fusion.first_ref.refs_3_), channel_id=1, source_target_pairs={{1,5},{3,7},{5,1},{7,3},{9,13},{11,15},{13,9},{15,11},{17,21},{19,... | collective-permute-start | bytes 393224 | tf_op jit(solution)/shard_map/ppermute | solution.py:308
  21.2 2.7 %collective-permute-start.5 = (f32[128,256]{1,0:T(8,128)S(1)}, f32[128,256]{1,0:T(8,128)S(1)}, u32[]{:S(2)}, u32[]{:S(2)}) collective-permute-start(f32[128,256]{1,0:T(8,128)S(1)} %add_multiply_fusion.first_ref.refs_3_), channel_id=1, source_target_pairs={{0,4},{2,6},{4,0},{6,2},{8,12},{10,14},{12,8},{14,10},{16,20},{18,... | collective-permute-start | bytes 393224 | tf_op jit(solution)/shard_map/ppermute | solution.py:309
  23.9 0.0 collective-permute-done.6.first_other_ref.refs_4_.refs_7_
  23.9 0.3 shard_map.82
  24.2 2.6 %collective-permute-start.7 = (f32[8,256]{1,0:T(8,128)S(1)}, f32[8,256]{1,0:T(8,128)S(1)}, u32[]{:S(2)}, u32[]{:S(2)}) collective-permute-start(f32[8,256]{1,0:T(8,128)S(1)} %shard_map.82), channel_id=1, source_target_pairs={{0,16},{4,20},{8,24},{12,28},{16,0},{20,4},{24,8},{28,12},{1,17},{... | collective-permute-start | bytes 24584 | tf_op jit(solution)/shard_map/ppermute | solution.py:314
  26.8 0.0 collective-permute-done.9.refs_5_
  26.8 0.7 %collective-permute-start.10 = (f32[128,256]{1,0:T(8,128)S(1)}, f32[128,256]{1,0:T(8,128)S(1)}, u32[]{:S(2)}, u32[]{:S(2)}) collective-permute-start(f32[128,256]{1,0:T(8,128)S(1)} %collective-permute-done.9.refs_5_), channel_id=1, source_target_pairs={{0,1},{1,0},{2,3},{3,2},{4,5},{5,4},{6,7},{7,6},{8,9},{9,8},{10,11... | collective-permute-start | bytes 393224 | tf_op jit(solution)/shard_map/ppermute | solution.py:273
  27.5 1.7 %collective-permute-done.7 = f32[8,256]{1,0:T(8,128)S(1)} collective-permute-done((f32[8,256]{1,0:T(8,128)S(1)}, f32[8,256]{1,0:T(8,128)S(1)}, u32[]{:S(2)}, u32[]{:S(2)}) %collective-permute-start.7) | collective-permute-done | bytes 8224 | tf_op jit(solution)/shard_map/ppermute | solution.py:314
  29.2 0.0 collective-permute-done.5.refs_7_
  29.2 0.0 collective-permute-start.11
  29.2 2.0 %collective-permute-start.8 = (f32[8,256]{1,0:T(8,128)S(1)}, f32[8,256]{1,0:T(8,128)S(1)}, u32[]{:S(2)}, u32[]{:S(2)}) collective-permute-start(f32[8,256]{1,0:T(8,128)S(1)} %add.11.a_ref), channel_id=1, source_target_pairs={{0,8},{4,12},{8,0},{12,4},{16,24},{20,28},{24,16},{28,20},{1,9},{5... | collective-permute-start | bytes 24584 | tf_op jit(solution)/shard_map/ppermute | solution.py:329
  31.2 0.0 collective-permute-done.10.refs_6_
  31.2 0.0 collective-permute-done.11.refs_8_
  31.2 1.3 %shard_map.83 = (f32[128,256]{1,0:T(8,128)S(1)}, bf16[3,256,256]{2,1,0:T(8,128)(2,1)S(1)}, bf16[3,256,256]{2,1,0:T(8,128)(2,1)S(1)}) custom-call(s32[8,8,128]{2,1,0:T(8,128)S(1)} %get-tuple-element.25.refs_0_.shift_ref, f32[8,1,256,256]{3,2,1,0:T(8,128)S(1)} %get-tuple-element.29.refs_1_.left_ref, ...), custom_call_target="tpu_custom_call" | custom-call | flops 4026531840 | bytes 4194304 | tf_op jit(solution)/shard_map/pallas_call | solution.py:22
  32.5 0.3 collective-permute-start.12
  32.8 1.2 %shard_map.84.after_ref.a_ref = f32[128,256]{1,0:T(8,128)S(1)} custom-call(s32[8,8,128]{2,1,0:T(8,128)S(1)} %get-tuple-element.25.refs_0_.shift_ref, f32[8,1,256,256]{3,2,1,0:T(8,128)S(1)} %get-tuple-element.29.refs_1_.left_ref, f32[8,1,256,256]{3,2,1,0:T(8,128)S(1)} %get-tuple-element.30.refs_2_.right_ref, bf16[3,256,256]{2,1,0:T(8,128)(2,1)S(1)} %get-tuple-element.40.high, ...), custom_call_target="tpu_custom_call" | custom-call | flops 134217728 | bytes 4194304 | tf_op jit(solution)/shard_map/pallas_call | solution.py:22
  33.9 0.0 collective-permute-done.8.b_ref
  34.0 0.0 collective-permute-done.12.b_ref
  34.0 1.6 %collective-permute-start.13 = (f32[128,256]{1,0:T(8,128)S(1)}, f32[128,256]{1,0:T(8,128)S(1)}, u32[]{:S(2)}, u32[]{:S(2)}) collective-permute-start(f32[128,256]{1,0:T(8,128)S(1)} %shard_map.86.refs_0_), channel_id=1, source_target_pairs={{0,2},{1,3},{2,0},{3,1},{4,6},{5,7},{6,4},{7,5},{8,10},{9,11},{10,... | collective-permute-start | bytes 393224 | tf_op jit(solution)/shard_map/ppermute | solution.py:280
  35.6 1.6 %collective-permute-start.14 = (f32[8,256]{1,0:T(8,128)S(1)}, f32[8,256]{1,0:T(8,128)S(1)}, u32[]{:S(2)}, u32[]{:S(2)}) collective-permute-start(f32[8,256]{1,0:T(8,128)S(1)} %shard_map.85.after_ref.refs_0_), channel_id=1, source_target_pairs={{0,4},{4,0},{8,12},{12,8},{16,20},{20,16},{24,28},{28,24},{1,5},{5... | collective-permute-start | bytes 24584 | tf_op jit(solution)/shard_map/ppermute | solution.py:336
  37.2 0.0 collective-permute-start.15
  37.2 2.0 %collective-permute-done.14.refs_1_ = f32[8,256]{1,0:T(8,128)S(1)} collective-permute-done((f32[8,256]{1,0:T(8,128)S(1)}, f32[8,256]{1,0:T(8,128)S(1)}, u32[]{:S(2)}, u32[]{:S(2)}) %collective-permute-start.14) | collective-permute-done | bytes 8224 | tf_op jit(solution)/shard_map/ppermute | solution.py:336
  39.2 0.5 %collective-permute-done.13.refs_1_ = f32[128,256]{1,0:T(8,128)S(1)} collective-permute-done((f32[128,256]{1,0:T(8,128)S(1)}, f32[128,256]{1,0:T(8,128)S(1)}, u32[]{:S(2)}, u32[]{:S(2)}) %collective-permute-start.13) | collective-permute-done | bytes 131104 | tf_op jit(solution)/shard_map/ppermute | solution.py:280
  39.7 0.0 collective-permute-start.16
  39.7 0.3 shard_map.87.merged_ref
  40.0 0.7 %shard_map.88 = f32[1,256,256]{2,1,0:T(8,128)} custom-call(f32[8,256]{1,0:T(8,128)S(1)} %shard_map.87.merged_ref, f32[128,256]{1,0:T(8,128)S(1)} %add_multiply_fusion.first_ref.refs_3_, f32[128,256]{1,0:T(8,128)S(1)} %collective-permute-done.6.first_other_ref.refs_4_.refs_7_, f32[128,256]{1,0:T(8,128)S(1)} %get-tuple-element.24.field_ref.refs_3_, ...), custom_call_target="tpu_custom_call" | custom-call | tf_op jit(solution)/shard_map/pallas_call | solution.py:22
  40.7 0.0 collective-permute-done.15.refs_4_
  40.7 0.3 collective-permute-done.16.refs_5_
  41.1 0.8 %shard_map.89 = f32[1,256,256]{2,1,0:T(8,128)} custom-call(f32[8,256]{1,0:T(8,128)S(1)} %shard_map.87.merged_ref, f32[128,256]{1,0:T(8,128)S(1)} %shard_map.86.refs_0_, f32[128,256]{1,0:T(8,128)S(1)} %collective-permute-done.13.refs_1_, f32[128,256]{1,0:T(8,128)S(1)} %get-tuple-element.37.refs_2_, f32[128,256]{1,0:T(8,128)S(1)} %add_multiply_fusion.first_ref.refs_3_, ...), custom_call_target="tpu_custom_call" | custom-call | tf_op jit(solution)/shard_map/pallas_call | solution.py:22
  (5 shorter events, 0.1 us)
Async XLA Ops:
  0.6 9.1 %collective-permute-start = (f32[256,256]{1,0:T(8,128)}, f32[256,256]{1,0:T(8,128)S(1)}, u32[]{:S(2)}, u32[]{:S(2)}) collective-permute-start(f32[256,256]{1,0:T(8,128)} %bitcast.1), channel_id=1, source_target_pairs={{1,5},{3,7},{5,1},{7,3},{9,13},{11,15},{13,9},{15,11},{17,21},{19,... | collective-permute-start | bytes 786440 | tf_op jit(solution)/shard_map/ppermute | solution.py:286
  6.1 3.7 %collective-permute-start.1 = (s32[8,128]{1,0:T(8,128)S(1)}, s32[8,128]{1,0:T(8,128)S(1)}, u32[]{:S(2)}, u32[]{:S(2)}) collective-permute-start(s32[8,128]{1,0:T(8,128)S(1)} %get-tuple-element.28), channel_id=1, source_target_pairs={{1,5},{3,7},{5,1},{7,3},{9,13},{11,15},{13,9},{15,11},{17,21},{19,... | collective-permute-start | bytes 12296 | tf_op jit(solution)/shard_map/ppermute | solution.py:298
  9.8 1.6 %collective-permute-start.2 = (f32[256,256]{1,0:T(8,128)S(1)}, f32[256,256]{1,0:T(8,128)S(1)}, u32[]{:S(2)}, u32[]{:S(2)}) collective-permute-start(f32[256,256]{1,0:T(8,128)S(1)} %shard_map.79.refs_5_), channel_id=1, source_target_pairs={{0,1},{1,0},{2,3},{3,2},{4,5},{5,4},{6,7},{7,6},{8,9},{9,8},{10,11... | collective-permute-start | bytes 786440 | tf_op jit(solution)/shard_map/ppermute | solution.py:273
  12.7 1.4 %collective-permute-start.3 = (f32[128,256]{1,0:T(8,128)S(1)}, f32[128,256]{1,0:T(8,128)S(1)}, u32[]{:S(2)}, u32[]{:S(2)}) collective-permute-start(f32[128,256]{1,0:T(8,128)S(1)} %get-tuple-element.36), channel_id=1, source_target_pairs={{0,1},{1,0},{2,3},{3,2},{4,5},{5,4},{6,7},{7,6},{8,9},{9,8},{10,11... | collective-permute-start | bytes 393224 | tf_op jit(solution)/shard_map/ppermute | solution.py:273
  14.2 5.8 %collective-permute-start.4 = (f32[128,256]{1,0:T(8,128)S(1)}, f32[128,256]{1,0:T(8,128)S(1)}, u32[]{:S(2)}, u32[]{:S(2)}) collective-permute-start(f32[128,256]{1,0:T(8,128)S(1)} %add.9), channel_id=1, source_target_pairs={{0,2},{1,3},{2,0},{3,1},{4,6},{5,7},{6,4},{7,5},{8,10},{9,11},{10,... | collective-permute-start | bytes 393224 | tf_op jit(solution)/shard_map/ppermute | solution.py:280
  20.0 3.9 %collective-permute-start.6 = (f32[128,256]{1,0:T(8,128)S(1)}, f32[128,256]{1,0:T(8,128)S(1)}, u32[]{:S(2)}, u32[]{:S(2)}) collective-permute-start(f32[128,256]{1,0:T(8,128)S(1)} %add_multiply_fusion.first_ref.refs_3_), channel_id=1, source_target_pairs={{0,1},{1,0},{2,3},{3,2},{4,5},{5,4},{6,7},{7,6},{8,9},{9,8},{10,11... | collective-permute-start | bytes 393224 | tf_op jit(solution)/shard_map/ppermute | solution.py:273
  20.1 6.7 %collective-permute-start.9 = (f32[128,256]{1,0:T(8,128)S(1)}, f32[128,256]{1,0:T(8,128)S(1)}, u32[]{:S(2)}, u32[]{:S(2)}) collective-permute-start(f32[128,256]{1,0:T(8,128)S(1)} %add_multiply_fusion.first_ref.refs_3_), channel_id=1, source_target_pairs={{1,5},{3,7},{5,1},{7,3},{9,13},{11,15},{13,9},{15,11},{17,21},{19,... | collective-permute-start | bytes 393224 | tf_op jit(solution)/shard_map/ppermute | solution.py:308
  21.2 8.0 %collective-permute-start.5 = (f32[128,256]{1,0:T(8,128)S(1)}, f32[128,256]{1,0:T(8,128)S(1)}, u32[]{:S(2)}, u32[]{:S(2)}) collective-permute-start(f32[128,256]{1,0:T(8,128)S(1)} %add_multiply_fusion.first_ref.refs_3_), channel_id=1, source_target_pairs={{0,4},{2,6},{4,0},{6,2},{8,12},{10,14},{12,8},{14,10},{16,20},{18,... | collective-permute-start | bytes 393224 | tf_op jit(solution)/shard_map/ppermute | solution.py:309
  24.2 5.0 %collective-permute-start.7 = (f32[8,256]{1,0:T(8,128)S(1)}, f32[8,256]{1,0:T(8,128)S(1)}, u32[]{:S(2)}, u32[]{:S(2)}) collective-permute-start(f32[8,256]{1,0:T(8,128)S(1)} %shard_map.82), channel_id=1, source_target_pairs={{0,16},{4,20},{8,24},{12,28},{16,0},{20,4},{24,8},{28,12},{1,17},{... | collective-permute-start | bytes 24584 | tf_op jit(solution)/shard_map/ppermute | solution.py:314
  26.8 4.4 %collective-permute-start.10 = (f32[128,256]{1,0:T(8,128)S(1)}, f32[128,256]{1,0:T(8,128)S(1)}, u32[]{:S(2)}, u32[]{:S(2)}) collective-permute-start(f32[128,256]{1,0:T(8,128)S(1)} %collective-permute-done.9.refs_5_), channel_id=1, source_target_pairs={{0,1},{1,0},{2,3},{3,2},{4,5},{5,4},{6,7},{7,6},{8,9},{9,8},{10,11... | collective-permute-start | bytes 393224 | tf_op jit(solution)/shard_map/ppermute | solution.py:273
  29.2 2.0 %collective-permute-start.11 = (f32[128,256]{1,0:T(8,128)S(1)}, f32[128,256]{1,0:T(8,128)S(1)}, u32[]{:S(2)}, u32[]{:S(2)}) collective-permute-start(f32[128,256]{1,0:T(8,128)S(1)} %collective-permute-done.5.refs_7_), channel_id=1, source_target_pairs={{0,1},{1,0},{2,3},{3,2},{4,5},{5,4},{6,7},{7,6},{8,9},{9,8},{10,11... | collective-permute-start | bytes 393224 | tf_op jit(solution)/shard_map/ppermute | solution.py:273
  29.2 4.7 %collective-permute-start.8 = (f32[8,256]{1,0:T(8,128)S(1)}, f32[8,256]{1,0:T(8,128)S(1)}, u32[]{:S(2)}, u32[]{:S(2)}) collective-permute-start(f32[8,256]{1,0:T(8,128)S(1)} %add.11.a_ref), channel_id=1, source_target_pairs={{0,8},{4,12},{8,0},{12,4},{16,24},{20,28},{24,16},{28,20},{1,9},{5... | collective-permute-start | bytes 24584 | tf_op jit(solution)/shard_map/ppermute | solution.py:329
  32.5 1.5 %collective-permute-start.12 = (f32[128,256]{1,0:T(8,128)S(1)}, f32[128,256]{1,0:T(8,128)S(1)}, u32[]{:S(2)}, u32[]{:S(2)}) collective-permute-start(f32[128,256]{1,0:T(8,128)S(1)} %get-tuple-element.42), channel_id=1, source_target_pairs={{0,1},{1,0},{2,3},{3,2},{4,5},{5,4},{6,7},{7,6},{8,9},{9,8},{10,11... | collective-permute-start | bytes 393224 | tf_op jit(solution)/shard_map/ppermute | solution.py:273
  34.0 5.7 %collective-permute-start.13 = (f32[128,256]{1,0:T(8,128)S(1)}, f32[128,256]{1,0:T(8,128)S(1)}, u32[]{:S(2)}, u32[]{:S(2)}) collective-permute-start(f32[128,256]{1,0:T(8,128)S(1)} %shard_map.86.refs_0_), channel_id=1, source_target_pairs={{0,2},{1,3},{2,0},{3,1},{4,6},{5,7},{6,4},{7,5},{8,10},{9,11},{10,... | collective-permute-start | bytes 393224 | tf_op jit(solution)/shard_map/ppermute | solution.py:280
  35.6 3.7 %collective-permute-start.14 = (f32[8,256]{1,0:T(8,128)S(1)}, f32[8,256]{1,0:T(8,128)S(1)}, u32[]{:S(2)}, u32[]{:S(2)}) collective-permute-start(f32[8,256]{1,0:T(8,128)S(1)} %shard_map.85.after_ref.refs_0_), channel_id=1, source_target_pairs={{0,4},{4,0},{8,12},{12,8},{16,20},{20,16},{24,28},{28,24},{1,5},{5... | collective-permute-start | bytes 24584 | tf_op jit(solution)/shard_map/ppermute | solution.py:336
  37.2 3.5 %collective-permute-start.15 = (f32[128,256]{1,0:T(8,128)S(1)}, f32[128,256]{1,0:T(8,128)S(1)}, u32[]{:S(2)}, u32[]{:S(2)}) collective-permute-start(f32[128,256]{1,0:T(8,128)S(1)} %shard_map.86.refs_0_), channel_id=1, source_target_pairs={{0,1},{1,0},{2,3},{3,2},{4,5},{5,4},{6,7},{7,6},{8,9},{9,8},{10,11... | collective-permute-start | bytes 393224 | tf_op jit(solution)/shard_map/ppermute | solution.py:273
  39.7 1.3 %collective-permute-start.16 = (f32[128,256]{1,0:T(8,128)S(1)}, f32[128,256]{1,0:T(8,128)S(1)}, u32[]{:S(2)}, u32[]{:S(2)}) collective-permute-start(f32[128,256]{1,0:T(8,128)S(1)} %collective-permute-done.13.refs_1_), channel_id=1, source_target_pairs={{0,1},{1,0},{2,3},{3,2},{4,5},{5,4},{6,7},{7,6},{8,9},{9,8},{10,11... | collective-permute-start | bytes 393224 | tf_op jit(solution)/shard_map/ppermute | solution.py:273

commit v10 on v6

--- a/solution.py
+++ b/solution.py
@@ -175,12 +175,12 @@
     refs[-1][...] = half_product(core_index(), shift_ref, high, low, left_ref, right_ref)
 
 
-def product_options(left):
+def product_options(left, count=30):
     terms, _, block, _ = left.shape
     return dict(
         mib=16,
         cost_estimate=pl.CostEstimate(
-            flops=30 * terms * block**3, bytes_accessed=8 * left.size, transcendentals=0
+            flops=count * terms * block**3, bytes_accessed=8 * left.size, transcendentals=0
         ),
     )
 
@@ -201,7 +201,7 @@
     block = left.shape[-1]
     arrays = [shift, left, right, high, low, *after]
     return call(
-        keep_kernel, f32(block // 2, block), [VMEM] * len(arrays), *arrays, **product_options(left)
+        keep_kernel, f32(block // 2, block), [VMEM] * len(arrays), *arrays, **product_options(left, 1)
     )
 
 
@@ -216,6 +216,10 @@
     lane = lax.broadcasted_iota(jnp.int32, out_ref.shape, 1)
     values = jnp.where(row == 0, cross, jnp.where(row == 1, square, jnp.where(row == 2, energy, 0.0)))
     out_ref[...] = jnp.where(lane == lax.axis_index("sec"), values, 0.0)
+
+
+def added_after_kernel(a_ref, b_ref, after_ref, out_ref):
+    out_ref[...] = a_ref[...] + b_ref[...]
 
 
 def added_kernel(a_ref, b_ref, after_ref, out_ref):
@@ -318,14 +322,17 @@
     send, *parts = product_to_send(
         shift, left, right, first, first_other, one, swapped(one), two, swapped(two)
     )
+    keep = product_to_keep(shift, left, right, *parts)
     sums = call(
         added_kernel,
         f32(EXTRA, block),
         [VMEM] * 3,
-        sums, lax.ppermute(sums, "sec", [(s, s ^ 2) for s in range(sectors)]), send,
-    )
-    keep = product_to_keep(shift, left, right, *parts, sums)
-    total, peer = over_chips(keep + swapped(send))
+        sums, lax.ppermute(sums, "sec", [(s, s ^ 2) for s in range(sectors)]), keep,
+        cost_estimate=pl.CostEstimate(flops=10**10, bytes_accessed=0, transcendentals=0),
+    )
+    total, peer = over_chips(
+        call(added_after_kernel, f32(half, block), [VMEM] * 3, keep, swapped(send), sums)
+    )
 
     cells = sectors * block * block
     merged = call(

time: 42.1 us -> 42.2 us (level)
    pallas_call x12 -> x13, Pallas kernels: 10.5 us -> 10.6 us  [call(): pl.pallas_call(kernel, out_shape=out_shape, in_specs=in_specs, out_specs=...]
  transfers between devices with their start and end apart: 17 -> 17, of which waited for: 8 -> 7; matrix products, arithmetic and copies ran while one was open for 0% -> 0% of each run, Pallas kernels for 20% -> 20%
where the time goes in v10:
time: 42.2 us; the launch traced here: 42 us
  starting transfers between devices  17.9 us (42%)
  waiting for transfers between devices  11.4 us (27%)
  Pallas kernels  10.6 us (25%)
  between operations  2.06 us (5%)
    pallas_call x13, Pallas kernels, call(): pl.pallas_call(kernel, out_shape=out_shape, in_specs=in_specs, out_specs=...  10.6 us
    ppermute x2, waiting for transfers between devices, over_chips(): lax.ppermute(total, 'op', [(i, i ^ step) for i in range(ops)])  4.75 us
    ppermute x1, starting transfers between devices, local(): got = lax.ppermute(state[0], ('sec', 'op'), crossing)  3.03 us
    ppermute x2, starting transfers between devices, over_chips(): lax.ppermute(total, 'op', [(i, i ^ step) for i in range(ops)])  2.93 us
    ppermute x1, starting transfers between devices, local(): two = lax.ppermute(first, ('sec', 'op'), crossing_too)  2.74 us
    ppermute x1, starting transfers between devices, with_distant(): lax.ppermute(sums, 'sec', [(s, s ^ step) for s in range(sectors)])  2.6 us
    ppermute x1, waiting for transfers between devices, local(): lax.ppermute(sums, 'sec', pairs)  2.04 us
    ppermute x1, starting transfers between devices, local(): lax.ppermute(sums, 'sec', [(s, s ^ 2) for s in range(sectors)])  1.95 us
  transfers between devices with their start and end apart: 17, of which 7 were waited for; matrix products, arithmetic and copies ran while one was open for 0% of the time, Pallas kernels for 20%

profile of v10, /device:TPU:0, one launch (start us, length us, event | category | flops | bytes accessed | tf_op | source)
XLA Modules:
  0.0 42.0 jit_solution(14998806329960888454)
XLA Ops:
  0.6 3.0 %collective-permute-start = (f32[256,256]{1,0:T(8,128)}, f32[256,256]{1,0:T(8,128)S(1)}, u32[]{:S(2)}, u32[]{:S(2)}) collective-permute-start(f32[256,256]{1,0:T(8,128)} %bitcast.1), channel_id=1, source_target_pairs={{1,5},{3,7},{5,1},{7,3},{9,13},{11,15},{13,9},{15,11},{17,21},{19,... | collective-permute-start | bytes 786440 | tf_op jit(solution)/shard_map/ppermute | solution.py:288
  5.0 0.1 pad_add_fusion.live_ref
  5.0 1.0 %shard_map.77 = (f32[128,256]{1,0:T(8,128)S(1)}, f32[128,256]{1,0:T(8,128)S(1)}, f32[128,256]{1,0:T(8,128)S(1)}, s32[8,128]{1,0:T(8,128)S(1)}) custom-call(f32[1,256,256]{2,1,0:T(8,128)} %state_ref.1, s32[2]{0:T(128)S(1)} %pad_add_fusion.live_ref), custom_call_target="tpu_custom_call" | custom-call | tf_op jit(solution)/shard_map/pallas_call | solution.py:22
  6.1 0.1 collective-permute-start.1
  6.1 2.4 %shard_map.78 = (f32[8,1,256,256]{3,2,1,0:T(8,128)S(1)}, f32[8,1,256,256]{3,2,1,0:T(8,128)S(1)}, s32[8,8,128]{2,1,0:T(8,128)S(1)}) custom-call(f32[8,1,256,256]{3,2,1,0:T(8,128)} %left_ref.1, f32[8,1,256,256]{3,2,1,0:T(8,128)} %right_ref.1, s32[8]{0:T(128)} %shift_ref.1, f32[128,256]{1,0:T(8,128)S(1)} %get-tuple-element.21.field_ref.refs_3_), custom_call_target="tpu_custom_call" | custom-call | bytes 4194304 | tf_op jit(solution)/shard_map/pallas_call | solution.py:22
  8.5 1.2 %collective-permute-done.1.refs_7_ = s32[8,128]{1,0:T(8,128)S(1)} collective-permute-done((s32[8,128]{1,0:T(8,128)S(1)}, s32[8,128]{1,0:T(8,128)S(1)}, u32[]{:S(2)}, u32[]{:S(2)}) %collective-permute-start.1) | collective-permute-done | bytes 4128 | tf_op jit(solution)/shard_map/ppermute | solution.py:300
  9.7 0.0 collective-permute-done.refs_5_
  9.7 0.0 collective-permute-start.2
  9.7 0.5 %collective-permute-start.3 = (s32[8,128]{1,0:T(8,128)S(1)}, s32[8,128]{1,0:T(8,128)S(1)}, u32[]{:S(2)}, u32[]{:S(2)}) collective-permute-start(s32[8,128]{1,0:T(8,128)S(1)} %collective-permute-done.1.refs_7_), channel_id=1, source_target_pairs={{0,1},{1,0},{2,3},{3,2},{4,5},{5,4},{6,7},{7,6},{8,9},{9,8},{10,11... | collective-permute-start | bytes 12296 | tf_op jit(solution)/shard_map/ppermute | solution.py:275
  10.3 1.0 %collective-permute-done.3.refs_8_ = s32[8,128]{1,0:T(8,128)S(1)} collective-permute-done((s32[8,128]{1,0:T(8,128)S(1)}, s32[8,128]{1,0:T(8,128)S(1)}, u32[]{:S(2)}, u32[]{:S(2)}) %collective-permute-start.3) | collective-permute-done | bytes 4128 | tf_op jit(solution)/shard_map/ppermute | solution.py:275
  11.3 0.0 collective-permute-done.2.refs_6_
  11.3 1.4 %shard_map.79 = (f32[128,256]{1,0:T(8,128)S(1)}, bf16[3,256,256]{2,1,0:T(8,128)(2,1)S(1)}, bf16[3,256,256]{2,1,0:T(8,128)(2,1)S(1)}) custom-call(s32[8,8,128]{2,1,0:T(8,128)S(1)} %get-tuple-element.22.refs_0_.shift_ref, f32[8,1,256,256]{3,2,1,0:T(8,128)S(1)} %get-tuple-element.26.refs_1_.left_ref, ...), custom_call_target="tpu_custom_call" | custom-call | flops 4026531840 | bytes 4194304 | tf_op jit(solution)/shard_map/pallas_call | solution.py:22
  12.7 0.2 collective-permute-start.4
  12.9 1.2 %shard_map.80 = f32[128,256]{1,0:T(8,128)S(1)} custom-call(s32[8,8,128]{2,1,0:T(8,128)S(1)} %get-tuple-element.22.refs_0_.shift_ref, f32[8,1,256,256]{3,2,1,0:T(8,128)S(1)} %get-tuple-element.26.refs_1_.left_ref, f32[8,1,256,256]{3,2,1,0:T(8,128)S(1)} %get-tuple-element.27.refs_2_.right_ref, bf16[3,256,256]{2,1,0:T(8,128)(2,1)S(1)} %get-tuple-element.31.high, ...), custom_call_target="tpu_custom_call" | custom-call | flops 134217728 | bytes 4194304 | tf_op jit(solution)/shard_map/pallas_call | solution.py:22
  14.1 0.0 collective-permute-done.4
  14.2 1.3 %collective-permute-start.5 = (f32[128,256]{1,0:T(8,128)S(1)}, f32[128,256]{1,0:T(8,128)S(1)}, u32[]{:S(2)}, u32[]{:S(2)}) collective-permute-start(f32[128,256]{1,0:T(8,128)S(1)} %add.9), channel_id=1, source_target_pairs={{0,2},{1,3},{2,0},{3,1},{4,6},{5,7},{6,4},{7,5},{8,10},{9,11},{10,... | collective-permute-start | bytes 393224 | tf_op jit(solution)/shard_map/ppermute | solution.py:282
  15.5 4.5 %collective-permute-done.5 = f32[128,256]{1,0:T(8,128)S(1)} collective-permute-done((f32[128,256]{1,0:T(8,128)S(1)}, f32[128,256]{1,0:T(8,128)S(1)}, u32[]{:S(2)}, u32[]{:S(2)}) %collective-permute-start.5) | collective-permute-done | bytes 131104 | tf_op jit(solution)/shard_map/ppermute | solution.py:282
  20.0 0.1 collective-permute-start.7
  20.1 1.1 %collective-permute-start.10 = (f32[128,256]{1,0:T(8,128)S(1)}, f32[128,256]{1,0:T(8,128)S(1)}, u32[]{:S(2)}, u32[]{:S(2)}) collective-permute-start(f32[128,256]{1,0:T(8,128)S(1)} %add_multiply_fusion.first_ref.refs_3_), channel_id=1, source_target_pairs={{1,5},{3,7},{5,1},{7,3},{9,13},{11,15},{13,9},{15,11},{17,21},{19,... | collective-permute-start | bytes 393224 | tf_op jit(solution)/shard_map/ppermute | solution.py:309
  21.2 2.7 %collective-permute-start.6 = (f32[128,256]{1,0:T(8,128)S(1)}, f32[128,256]{1,0:T(8,128)S(1)}, u32[]{:S(2)}, u32[]{:S(2)}) collective-permute-start(f32[128,256]{1,0:T(8,128)S(1)} %add_multiply_fusion.first_ref.refs_3_), channel_id=1, source_target_pairs={{0,4},{2,6},{4,0},{6,2},{8,12},{10,14},{12,8},{14,10},{16,20},{18,... | collective-permute-start | bytes 393224 | tf_op jit(solution)/shard_map/ppermute | solution.py:310
  23.9 0.0 collective-permute-done.7.first_other_ref.refs_4_
  23.9 0.3 shard_map.81
  24.2 2.6 %collective-permute-start.8 = (f32[8,256]{1,0:T(8,128)S(1)}, f32[8,256]{1,0:T(8,128)S(1)}, u32[]{:S(2)}, u32[]{:S(2)}) collective-permute-start(f32[8,256]{1,0:T(8,128)S(1)} %shard_map.81), channel_id=1, source_target_pairs={{0,16},{4,20},{8,24},{12,28},{16,0},{20,4},{24,8},{28,12},{1,17},{... | collective-permute-start | bytes 24584 | tf_op jit(solution)/shard_map/ppermute | solution.py:315
  26.8 0.0 collective-permute-done.10.refs_5_
  26.8 0.7 %collective-permute-start.11 = (f32[128,256]{1,0:T(8,128)S(1)}, f32[128,256]{1,0:T(8,128)S(1)}, u32[]{:S(2)}, u32[]{:S(2)}) collective-permute-start(f32[128,256]{1,0:T(8,128)S(1)} %collective-permute-done.10.refs_5_), channel_id=1, source_target_pairs={{0,1},{1,0},{2,3},{3,2},{4,5},{5,4},{6,7},{7,6},{8,9},{9,8},{10,11... | collective-permute-start | bytes 393224 | tf_op jit(solution)/shard_map/ppermute | solution.py:275
  27.5 1.7 %collective-permute-done.8 = f32[8,256]{1,0:T(8,128)S(1)} collective-permute-done((f32[8,256]{1,0:T(8,128)S(1)}, f32[8,256]{1,0:T(8,128)S(1)}, u32[]{:S(2)}, u32[]{:S(2)}) %collective-permute-start.8) | collective-permute-done | bytes 8224 | tf_op jit(solution)/shard_map/ppermute | solution.py:315
  29.2 0.0 collective-permute-done.6.refs_7_
  29.2 0.0 collective-permute-start.12
  29.2 2.0 %collective-permute-start.9 = (f32[8,256]{1,0:T(8,128)S(1)}, f32[8,256]{1,0:T(8,128)S(1)}, u32[]{:S(2)}, u32[]{:S(2)}) collective-permute-start(f32[8,256]{1,0:T(8,128)S(1)} %add.11.a_ref), channel_id=1, source_target_pairs={{0,8},{4,12},{8,0},{12,4},{16,24},{20,28},{24,16},{28,20},{1,9},{5... | collective-permute-start | bytes 24584 | tf_op jit(solution)/shard_map/ppermute | solution.py:330
  31.2 0.0 collective-permute-done.11.refs_6_
  31.2 0.0 collective-permute-done.12.refs_8_
  31.2 1.3 %shard_map.82 = (f32[128,256]{1,0:T(8,128)S(1)}, bf16[3,256,256]{2,1,0:T(8,128)(2,1)S(1)}, bf16[3,256,256]{2,1,0:T(8,128)(2,1)S(1)}) custom-call(s32[8,8,128]{2,1,0:T(8,128)S(1)} %get-tuple-element.22.refs_0_.shift_ref, f32[8,1,256,256]{3,2,1,0:T(8,128)S(1)} %get-tuple-element.26.refs_1_.left_ref, ...), custom_call_target="tpu_custom_call" | custom-call | flops 4026531840 | bytes 4194304 | tf_op jit(solution)/shard_map/pallas_call | solution.py:22
  32.5 0.3 collective-permute-start.14
  32.8 1.2 %shard_map.83.after_ref.a_ref = f32[128,256]{1,0:T(8,128)S(1)} custom-call(s32[8,8,128]{2,1,0:T(8,128)S(1)} %get-tuple-element.22.refs_0_.shift_ref, f32[8,1,256,256]{3,2,1,0:T(8,128)S(1)} %get-tuple-element.26.refs_1_.left_ref, f32[8,1,256,256]{3,2,1,0:T(8,128)S(1)} %get-tuple-element.27.refs_2_.right_ref, bf16[3,256,256]{2,1,0:T(8,128)(2,1)S(1)} %get-tuple-element.37.high, ...), custom_call_target="tpu_custom_call" | custom-call | flops 134217728 | bytes 4194304 | tf_op jit(solution)/shard_map/pallas_call | solution.py:22
  34.0 0.0 collective-permute-done.9.b_ref
  34.1 0.0 collective-permute-done.14.b_ref
  34.1 1.6 %collective-permute-start.15 = (f32[128,256]{1,0:T(8,128)S(1)}, f32[128,256]{1,0:T(8,128)S(1)}, u32[]{:S(2)}, u32[]{:S(2)}) collective-permute-start(f32[128,256]{1,0:T(8,128)S(1)} %shard_map.87.total_ref), channel_id=1, source_target_pairs={{0,2},{1,3},{2,0},{3,1},{4,6},{5,7},{6,4},{7,5},{8,10},{9,11},{10,... | collective-permute-start | bytes 393224 | tf_op jit(solution)/shard_map/ppermute | solution.py:282
  35.7 1.6 %collective-permute-start.13 = (f32[8,256]{1,0:T(8,128)S(1)}, f32[8,256]{1,0:T(8,128)S(1)}, u32[]{:S(2)}, u32[]{:S(2)}) collective-permute-start(f32[8,256]{1,0:T(8,128)S(1)} %shard_map.84.refs_0_.after_ref), channel_id=1, source_target_pairs={{0,4},{4,0},{8,12},{12,8},{16,20},{20,16},{24,28},{28,24},{1,5},{5... | collective-permute-start | bytes 24584 | tf_op jit(solution)/shard_map/ppermute | solution.py:342
  37.3 2.0 %collective-permute-done.13.refs_1_ = f32[8,256]{1,0:T(8,128)S(1)} collective-permute-done((f32[8,256]{1,0:T(8,128)S(1)}, f32[8,256]{1,0:T(8,128)S(1)}, u32[]{:S(2)}, u32[]{:S(2)}) %collective-permute-start.13) | collective-permute-done | bytes 8224 | tf_op jit(solution)/shard_map/ppermute | solution.py:342
  39.3 0.3 shard_map.85.merged_ref
  39.6 0.2 collective-permute-done.15.peer_ref
  39.9 0.1 collective-permute-start.16
  40.0 0.7 %shard_map.86 = f32[1,256,256]{2,1,0:T(8,128)} custom-call(f32[8,256]{1,0:T(8,128)S(1)} %shard_map.85.merged_ref, f32[128,256]{1,0:T(8,128)S(1)} %add_multiply_fusion.first_ref.refs_3_, f32[128,256]{1,0:T(8,128)S(1)} %collective-permute-done.7.first_other_ref.refs_4_, f32[128,256]{1,0:T(8,128)S(1)} %get-tuple-element.21.field_ref.refs_3_, ...), custom_call_target="tpu_custom_call" | custom-call | tf_op jit(solution)/shard_map/pallas_call | solution.py:22
  40.7 0.6 %collective-permute-done.16.other_ref = f32[128,256]{1,0:T(8,128)S(1)} collective-permute-done((f32[128,256]{1,0:T(8,128)S(1)}, f32[128,256]{1,0:T(8,128)S(1)}, u32[]{:S(2)}, u32[]{:S(2)}) %collective-permute-start.16) | collective-permute-done | bytes 131104 | tf_op jit(solution)/shard_map/ppermute | solution.py:275
  41.3 0.7 %shard_map.89 = f32[1,256,256]{2,1,0:T(8,128)} custom-call(f32[128,256]{1,0:T(8,128)S(1)} %shard_map.88.mine_ref, f32[128,256]{1,0:T(8,128)S(1)} %collective-permute-done.16.other_ref), custom_call_target="tpu_custom_call" | custom-call | tf_op jit(solution)/shard_map/pallas_call | solution.py:22
  (6 shorter events, 0.1 us)
Async XLA Ops:
  0.6 9.1 %collective-permute-start = (f32[256,256]{1,0:T(8,128)}, f32[256,256]{1,0:T(8,128)S(1)}, u32[]{:S(2)}, u32[]{:S(2)}) collective-permute-start(f32[256,256]{1,0:T(8,128)} %bitcast.1), channel_id=1, source_target_pairs={{1,5},{3,7},{5,1},{7,3},{9,13},{11,15},{13,9},{15,11},{17,21},{19,... | collective-permute-start | bytes 786440 | tf_op jit(solution)/shard_map/ppermute | solution.py:288
  6.1 3.7 %collective-permute-start.1 = (s32[8,128]{1,0:T(8,128)S(1)}, s32[8,128]{1,0:T(8,128)S(1)}, u32[]{:S(2)}, u32[]{:S(2)}) collective-permute-start(s32[8,128]{1,0:T(8,128)S(1)} %get-tuple-element.25), channel_id=1, source_target_pairs={{1,5},{3,7},{5,1},{7,3},{9,13},{11,15},{13,9},{15,11},{17,21},{19,... | collective-permute-start | bytes 12296 | tf_op jit(solution)/shard_map/ppermute | solution.py:300
  9.7 1.5 %collective-permute-start.2 = (f32[256,256]{1,0:T(8,128)S(1)}, f32[256,256]{1,0:T(8,128)S(1)}, u32[]{:S(2)}, u32[]{:S(2)}) collective-permute-start(f32[256,256]{1,0:T(8,128)S(1)} %collective-permute-done.refs_5_), channel_id=1, source_target_pairs={{0,1},{1,0},{2,3},{3,2},{4,5},{5,4},{6,7},{7,6},{8,9},{9,8},{10,11... | collective-permute-start | bytes 786440 | tf_op jit(solution)/shard_map/ppermute | solution.py:275
  9.7 1.5 %collective-permute-start.3 = (s32[8,128]{1,0:T(8,128)S(1)}, s32[8,128]{1,0:T(8,128)S(1)}, u32[]{:S(2)}, u32[]{:S(2)}) collective-permute-start(s32[8,128]{1,0:T(8,128)S(1)} %collective-permute-done.1.refs_7_), channel_id=1, source_target_pairs={{0,1},{1,0},{2,3},{3,2},{4,5},{5,4},{6,7},{7,6},{8,9},{9,8},{10,11... | collective-permute-start | bytes 12296 | tf_op jit(solution)/shard_map/ppermute | solution.py:275
  12.7 1.4 %collective-permute-start.4 = (f32[128,256]{1,0:T(8,128)S(1)}, f32[128,256]{1,0:T(8,128)S(1)}, u32[]{:S(2)}, u32[]{:S(2)}) collective-permute-start(f32[128,256]{1,0:T(8,128)S(1)} %get-tuple-element.33), channel_id=1, source_target_pairs={{0,1},{1,0},{2,3},{3,2},{4,5},{5,4},{6,7},{7,6},{8,9},{9,8},{10,11... | collective-permute-start | bytes 393224 | tf_op jit(solution)/shard_map/ppermute | solution.py:275
  14.2 5.8 %collective-permute-start.5 = (f32[128,256]{1,0:T(8,128)S(1)}, f32[128,256]{1,0:T(8,128)S(1)}, u32[]{:S(2)}, u32[]{:S(2)}) collective-permute-start(f32[128,256]{1,0:T(8,128)S(1)} %add.9), channel_id=1, source_target_pairs={{0,2},{1,3},{2,0},{3,1},{4,6},{5,7},{6,4},{7,5},{8,10},{9,11},{10,... | collective-permute-start | bytes 393224 | tf_op jit(solution)/shard_map/ppermute | solution.py:282
  20.0 3.9 %collective-permute-start.7 = (f32[128,256]{1,0:T(8,128)S(1)}, f32[128,256]{1,0:T(8,128)S(1)}, u32[]{:S(2)}, u32[]{:S(2)}) collective-permute-start(f32[128,256]{1,0:T(8,128)S(1)} %add_multiply_fusion.first_ref.refs_3_), channel_id=1, source_target_pairs={{0,1},{1,0},{2,3},{3,2},{4,5},{5,4},{6,7},{7,6},{8,9},{9,8},{10,11... | collective-permute-start | bytes 393224 | tf_op jit(solution)/shard_map/ppermute | solution.py:275
  20.1 6.7 %collective-permute-start.10 = (f32[128,256]{1,0:T(8,128)S(1)}, f32[128,256]{1,0:T(8,128)S(1)}, u32[]{:S(2)}, u32[]{:S(2)}) collective-permute-start(f32[128,256]{1,0:T(8,128)S(1)} %add_multiply_fusion.first_ref.refs_3_), channel_id=1, source_target_pairs={{1,5},{3,7},{5,1},{7,3},{9,13},{11,15},{13,9},{15,11},{17,21},{19,... | collective-permute-start | bytes 393224 | tf_op jit(solution)/shard_map/ppermute | solution.py:309
  21.2 8.0 %collective-permute-start.6 = (f32[128,256]{1,0:T(8,128)S(1)}, f32[128,256]{1,0:T(8,128)S(1)}, u32[]{:S(2)}, u32[]{:S(2)}) collective-permute-start(f32[128,256]{1,0:T(8,128)S(1)} %add_multiply_fusion.first_ref.refs_3_), channel_id=1, source_target_pairs={{0,4},{2,6},{4,0},{6,2},{8,12},{10,14},{12,8},{14,10},{16,20},{18,... | collective-permute-start | bytes 393224 | tf_op jit(solution)/shard_map/ppermute | solution.py:310
  24.2 5.0 %collective-permute-start.8 = (f32[8,256]{1,0:T(8,128)S(1)}, f32[8,256]{1,0:T(8,128)S(1)}, u32[]{:S(2)}, u32[]{:S(2)}) collective-permute-start(f32[8,256]{1,0:T(8,128)S(1)} %shard_map.81), channel_id=1, source_target_pairs={{0,16},{4,20},{8,24},{12,28},{16,0},{20,4},{24,8},{28,12},{1,17},{... | collective-permute-start | bytes 24584 | tf_op jit(solution)/shard_map/ppermute | solution.py:315
  26.8 4.4 %collective-permute-start.11 = (f32[128,256]{1,0:T(8,128)S(1)}, f32[128,256]{1,0:T(8,128)S(1)}, u32[]{:S(2)}, u32[]{:S(2)}) collective-permute-start(f32[128,256]{1,0:T(8,128)S(1)} %collective-permute-done.10.refs_5_), channel_id=1, source_target_pairs={{0,1},{1,0},{2,3},{3,2},{4,5},{5,4},{6,7},{7,6},{8,9},{9,8},{10,11... | collective-permute-start | bytes 393224 | tf_op jit(solution)/shard_map/ppermute | solution.py:275
  29.2 2.0 %collective-permute-start.12 = (f32[128,256]{1,0:T(8,128)S(1)}, f32[128,256]{1,0:T(8,128)S(1)}, u32[]{:S(2)}, u32[]{:S(2)}) collective-permute-start(f32[128,256]{1,0:T(8,128)S(1)} %collective-permute-done.6.refs_7_), channel_id=1, source_target_pairs={{0,1},{1,0},{2,3},{3,2},{4,5},{5,4},{6,7},{7,6},{8,9},{9,8},{10,11... | collective-permute-start | bytes 393224 | tf_op jit(solution)/shard_map/ppermute | solution.py:275
  29.2 4.8 %collective-permute-start.9 = (f32[8,256]{1,0:T(8,128)S(1)}, f32[8,256]{1,0:T(8,128)S(1)}, u32[]{:S(2)}, u32[]{:S(2)}) collective-permute-start(f32[8,256]{1,0:T(8,128)S(1)} %add.11.a_ref), channel_id=1, source_target_pairs={{0,8},{4,12},{8,0},{12,4},{16,24},{20,28},{24,16},{28,20},{1,9},{5... | collective-permute-start | bytes 24584 | tf_op jit(solution)/shard_map/ppermute | solution.py:330
  32.5 1.5 %collective-permute-start.14 = (f32[128,256]{1,0:T(8,128)S(1)}, f32[128,256]{1,0:T(8,128)S(1)}, u32[]{:S(2)}, u32[]{:S(2)}) collective-permute-start(f32[128,256]{1,0:T(8,128)S(1)} %get-tuple-element.39), channel_id=1, source_target_pairs={{0,1},{1,0},{2,3},{3,2},{4,5},{5,4},{6,7},{7,6},{8,9},{9,8},{10,11... | collective-permute-start | bytes 393224 | tf_op jit(solution)/shard_map/ppermute | solution.py:275
  34.1 5.7 %collective-permute-start.15 = (f32[128,256]{1,0:T(8,128)S(1)}, f32[128,256]{1,0:T(8,128)S(1)}, u32[]{:S(2)}, u32[]{:S(2)}) collective-permute-start(f32[128,256]{1,0:T(8,128)S(1)} %shard_map.87.total_ref), channel_id=1, source_target_pairs={{0,2},{1,3},{2,0},{3,1},{4,6},{5,7},{6,4},{7,5},{8,10},{9,11},{10,... | collective-permute-start | bytes 393224 | tf_op jit(solution)/shard_map/ppermute | solution.py:282
  35.7 3.7 %collective-permute-start.13 = (f32[8,256]{1,0:T(8,128)S(1)}, f32[8,256]{1,0:T(8,128)S(1)}, u32[]{:S(2)}, u32[]{:S(2)}) collective-permute-start(f32[8,256]{1,0:T(8,128)S(1)} %shard_map.84.refs_0_.after_ref), channel_id=1, source_target_pairs={{0,4},{4,0},{8,12},{12,8},{16,20},{20,16},{24,28},{28,24},{1,5},{5... | collective-permute-start | bytes 24584 | tf_op jit(solution)/shard_map/ppermute | solution.py:342
  39.9 1.4 %collective-permute-start.16 = (f32[128,256]{1,0:T(8,128)S(1)}, f32[128,256]{1,0:T(8,128)S(1)}, u32[]{:S(2)}, u32[]{:S(2)}) collective-permute-start(f32[128,256]{1,0:T(8,128)S(1)} %shard_map.88.mine_ref), channel_id=1, source_target_pairs={{0,1},{1,0},{2,3},{3,2},{4,5},{5,4},{6,7},{7,6},{8,9},{9,8},{10,11... | collective-permute-start | bytes 393224 | tf_op jit(solution)/shard_map/ppermute | solution.py:275
